TPU v7x, 32 devices: a whole 2x2x4 slice. The times are simulated.
32 devices in a mesh: aux: 4 (over z), occ: 8 (over y, x, core).
Axes of the slice: x: 2, y: 2, z: 4, core: 2. Of those that a mesh axis runs over, the one named last changes fastest.
Arguments:
- half_ints: bfloat16 [1024, 128, 1024], P('aux', 'occ'), may hold values from -1 to 1
- block_mask: int32 [16, 128], P('aux', 'occ'), may hold values 0 or 1
- vir_coef: bfloat16 [1024, 2048], replicated, may hold values from -0.1875 to 0.1875
- domains: int32 [128, 512], replicated, may hold values from 0 to 2047, as said below
- vir_energy: float32 [2048], replicated, may hold values from 0.5 to 3
- occ_energy: float32 [128], replicated, may hold values from -3 to -0.5
- pair_count: int32 [8, 4], P('occ', 'aux'), may hold values from 2 to 16, as said below
- pair_code: int32 [8, 4, 16], P('occ', 'aux'), may hold values from 0 to 63, as said below
Outputs:
- density: bfloat16 [1024, 128, 512], P('aux', 'occ')
Inputs may be any that keep to these rules, and one draw needn't show every extreme that they name: `domains`: each row names 512 distinct virtual orbitals. `pair_count`: some block holds exactly 16 live pairs. `pair_code`: the entries of one block's list are distinct.
All inputs are finite; a program needn't handle non-finite values. No bound on the sum of `block_mask` on one device may be relied on, other than what follows from the above.
Results may differ from a plain program's by a relative error of at most 0.0075.
Values may be sent and summed in bfloat16 or wider, within the bound.
No kernel may reach another device: no remote copies, remote signals or barrier semaphores. Data moves between devices by JAX's collectives and lax.ppermute only.
A program may use at most 128 MiB of HBM per device.

v0:
```python
import functools

import jax
import jax.numpy as jnp
from jax import lax
from jax.experimental import pallas as pl
from jax.experimental.pallas import tpu as pltpu
from jax.sharding import PartitionSpec as P

BLK = 64
OCC_DEV = 4
PARTNERS = 4
ROWS = 16
MIB = 1024 * 1024


def sort_kernel(mask_ref, aux_ref, occ_ref, x_ref, dom_ref, out_ref, own_ref, place_ref):
    step = pl.program_id(0)
    block, orbitals, basis = x_ref.shape
    width = orbitals * ROWS
    place_ref[0] = aux_ref[0]
    place_ref[1] = occ_ref[0]
    start = pl.multiple_of(occ_ref[0] * orbitals, 8)
    own_ref[:, 0, :] = dom_ref[pl.ds(start, orbitals), :]
    row = lax.broadcasted_iota(jnp.int32, (ROWS, width), 0)
    col = lax.broadcasted_iota(jnp.int32, (ROWS, width), 1)
    spread = jnp.concatenate(
        [
            jnp.where(
                col == row * orbitals + orbital, mask_ref[step * block // BLK, orbital].astype(jnp.float32), 0.0
            )
            for orbital in range(orbitals)
        ],
        axis=0,
    ).astype(jnp.bfloat16)
    for part in range(block // ROWS):
        span = slice(part * ROWS, (part + 1) * ROWS)
        moved = jnp.dot(spread, x_ref[span].reshape(width, basis), preferred_element_type=jnp.float32)
        out_ref[:, span, :] = moved.astype(jnp.bfloat16).reshape(orbitals, ROWS, basis)


def sorted_rows(half_ints, block_mask, domains, aux_pos, occ_pos):
    rows, orbitals, basis = half_ints.shape
    virs = domains.shape[1]
    block = BLK // 2
    smem = pl.BlockSpec(memory_space=pltpu.SMEM)
    return pl.pallas_call(
        sort_kernel,
        grid=(rows // block,),
        in_specs=[
            smem,
            smem,
            smem,
            pl.BlockSpec((block, orbitals, basis), lambda g: (g, 0, 0)),
            pl.BlockSpec(domains.shape, lambda g: (0, 0)),
        ],
        out_specs=[
            pl.BlockSpec((orbitals, block, basis), lambda g: (0, g, 0)),
            pl.BlockSpec((orbitals, 1, virs), lambda g: (0, 0, 0)),
            smem,
        ],
        out_shape=[
            jax.ShapeDtypeStruct((orbitals, rows, basis), jnp.bfloat16),
            jax.ShapeDtypeStruct((orbitals, 1, virs), jnp.int32),
            jax.ShapeDtypeStruct((2,), jnp.int32),
        ],
        compiler_params=pltpu.CompilerParams(vmem_limit_bytes=40 * MIB),
        cost_estimate=pl.CostEstimate(
            flops=2 * rows * orbitals * basis * orbitals * ROWS,
            bytes_accessed=4 * rows * orbitals * basis,
            transcendentals=0,
        ),
        name="sort_rows",
    )(block_mask, aux_pos, occ_pos, half_ints, domains)


def transform_kernel(count, after, pos_ref, x_ref, dom_ref, coef_ref, *refs):
    out_refs = refs[after:]
    step = pl.program_id(0)
    tile = 512
    whole = coef_ref.shape[1]
    dom = dom_ref[...]
    total = None
    for part in range(whole // tile):
        full = jnp.dot(
            x_ref[...], coef_ref[:, part * tile : (part + 1) * tile], preferred_element_type=jnp.float32
        ).astype(jnp.bfloat16)
        row = lax.broadcasted_iota(jnp.int32, (tile, dom.shape[1]), 0) + part * tile
        pick = jnp.where(row == dom, 1.0, 0.0).astype(jnp.bfloat16)
        term = jnp.dot(full, pick, preferred_element_type=jnp.float32)
        total = term if total is None else total + term
    total = total.astype(jnp.bfloat16)
    for index in range(count):
        @pl.when(step == index)
        def _():
            out_refs[index][...] = total


def transformed(rows_of, own_domains, vir_coef, aux_pos, aux_count, chunk, first, count, after):
    orbitals, rows, basis = rows_of.shape
    virs = own_domains.shape[2]
    whole = vir_coef.shape[1]

    def orbital(step, pos_ref):
        return lax.rem(pos_ref[0] + first + step, aux_count) * OCC_DEV + chunk

    return pl.pallas_call(
        functools.partial(transform_kernel, count, len(after)),
        grid_spec=pltpu.PrefetchScalarGridSpec(
            num_scalar_prefetch=1,
            grid=(count,),
            in_specs=[
                pl.BlockSpec((None, rows, basis), lambda g, pos: (orbital(g, pos), 0, 0)),
                pl.BlockSpec((None, 1, virs), lambda g, pos: (orbital(g, pos), 0, 0)),
                pl.BlockSpec((basis, whole), lambda g, pos: (0, 0), pipeline_mode=pl.Buffered(1)),
            ]
            + [pl.BlockSpec(memory_space=pl.ANY)] * len(after),
            out_specs=[pl.BlockSpec((rows, virs), lambda g, pos: (0, 0)) for _ in range(count)],
        ),
        out_shape=[jax.ShapeDtypeStruct((rows, virs), jnp.bfloat16) for _ in range(count)],
        compiler_params=pltpu.CompilerParams(vmem_limit_bytes=20 * MIB),
        cost_estimate=pl.CostEstimate(
            flops=2 * count * rows * whole * (basis + virs),
            bytes_accessed=2 * (count * rows * (basis + virs) + basis * whole),
            transcendentals=0,
        ),
        name="transform",
    )(aux_pos, rows_of, own_domains, vir_coef, *after)


def join_kernel(count, *refs):
    out = refs[-1]
    rows = refs[0].shape[0]
    for index in range(count):
        out[index * rows : (index + 1) * rows, :] = refs[index][...]


def stacked(pieces, after):
    rows, virs = pieces[0].shape
    count = len(pieces)
    return pl.pallas_call(
        functools.partial(join_kernel, count),
        in_specs=[pl.BlockSpec((rows, virs), lambda: (0, 0))] * count
        + [pl.BlockSpec(memory_space=pl.ANY)] * len(after),
        out_specs=pl.BlockSpec((count * rows, virs), lambda: (0, 0)),
        out_shape=jax.ShapeDtypeStruct((count * rows, virs), pieces[0].dtype),
        compiler_params=pltpu.CompilerParams(vmem_limit_bytes=16 * MIB),
        cost_estimate=pl.CostEstimate(flops=0, bytes_accessed=4 * count * rows * virs, transcendentals=0),
        name="join",
    )(*pieces, *after)


def pick_kernel(late, place_ref, own_ref, near_ref, late_ref, *refs):
    out = refs[-1]
    is_late = functools.reduce(jnp.logical_or, [place_ref[1] == n for n in late], place_ref[1] < 0)
    out[0] = own_ref[...]

    @pl.when(jnp.logical_not(is_late))
    def _():
        out[1] = near_ref[...]

    @pl.when(is_late)
    def _():
        out[1] = late_ref[...]


def with_next(own, near, late_near, late, place, after):
    rows, virs = own.shape
    block = rows // 4
    return pl.pallas_call(
        functools.partial(pick_kernel, late),
        grid=(rows // block,),
        in_specs=[pl.BlockSpec(memory_space=pltpu.SMEM)]
        + [pl.BlockSpec((block, virs), lambda g: (g, 0))] * 3
        + [pl.BlockSpec(memory_space=pl.ANY)] * len(after),
        out_specs=pl.BlockSpec((2, block, virs), lambda g: (0, g, 0)),
        out_shape=jax.ShapeDtypeStruct((2, rows, virs), own.dtype),
        compiler_params=pltpu.CompilerParams(vmem_limit_bytes=16 * MIB),
        cost_estimate=pl.CostEstimate(flops=0, bytes_accessed=10 * rows * virs, transcendentals=0),
        name="pick",
    )(place, own, near, late_near, *after)


def slot_orbital(place_ref, aux_count, occ_count, slot):
    block = lax.rem(place_ref[1] + slot // OCC_DEV, occ_count) * aux_count + place_ref[0]
    return block * OCC_DEV + slot % OCC_DEV


def energy_kernel(aux_count, occ_count, place_ref, dom_ref, table_ref, row_ref, col_ref):
    slots, _, virs = row_ref.shape
    lanes = table_ref.shape[1]
    rows = []
    for slot in range(slots):
        orbital = slot_orbital(place_ref, aux_count, occ_count, slot)
        rows.append(dom_ref[pl.ds(orbital, 1), :])
    doms = jnp.concatenate(rows, axis=0)
    for part in range(virs // lanes):
        span = slice(part * lanes, (part + 1) * lanes)
        dom = doms[:, span]
        high, low = dom // lanes, dom % lanes
        total = jnp.zeros((slots, lanes), jnp.float32)
        for line in range(table_ref.shape[0]):
            table = jnp.broadcast_to(table_ref[line : line + 1, :], (slots, lanes))
            found = jnp.take_along_axis(table, low, axis=1, mode="promise_in_bounds")
            total = jnp.where(high == line, found, total)
        row_ref[:, 0, span] = total
        col_ref[span, :] = total.T


def energies(place, domains, vir_energy, aux_count, occ_count):
    slots, virs = PARTNERS * OCC_DEV, domains.shape[1]
    vmem = pl.BlockSpec(memory_space=pltpu.VMEM)
    return pl.pallas_call(
        functools.partial(energy_kernel, aux_count, occ_count),
        in_specs=[pl.BlockSpec(memory_space=pltpu.SMEM), vmem, vmem],
        out_specs=[vmem, vmem],
        out_shape=[
            jax.ShapeDtypeStruct((slots, 1, virs), jnp.float32),
            jax.ShapeDtypeStruct((virs, slots), jnp.float32),
        ],
        compiler_params=pltpu.CompilerParams(vmem_limit_bytes=8 * MIB),
        cost_estimate=pl.CostEstimate(flops=0, bytes_accessed=4 * domains.size, transcendentals=0),
        name="energies",
    )(place, domains, vir_energy.reshape(-1, 128))


def pair_kernel(chunk, count, occ_count, live_ref, code_ref, place_ref, occ_ref, own_ref, col_ref, row_ref, *refs):
    sets = 3
    blocks = refs[: sets * OCC_DEV]
    outs = refs[sets * OCC_DEV : sets * OCC_DEV + count]
    turned, total, held, sems, todo = refs[sets * OCC_DEV + count :]
    span = PARTNERS * OCC_DEV
    slots = code_ref.shape[0]
    odd = place_ref[1] % 2

    def scan(slot, found):
        code = code_ref[slot]
        mine = (slot < live_ref[0, 0]) & (code // span == chunk)

        @pl.when(mine)
        def _():
            todo[found] = code % span

        return found + mine.astype(jnp.int32)

    pairs = lax.fori_loop(0, slots, scan, jnp.int32(0))

    def source(slot):
        offset = slot // OCC_DEV
        one = jnp.where(odd == 1, 3, 2)
        three = jnp.where(odd == 1, 4, 3)
        kind = jnp.where(offset == 0, 0, jnp.where(offset == 1, one, jnp.where(offset == 2, 1, three)))
        return kind * OCC_DEV + slot % OCC_DEV

    def fetch(index):
        place = source(todo[index])
        buffer = lax.rem(index, 2)
        for kind in range(5):
            for orbital in range(OCC_DEV):
                block = blocks[kind // 2 * OCC_DEV + orbital]
                block = block.at[kind % 2] if kind < 4 else block

                @pl.when(place == kind * OCC_DEV + orbital)
                def _():
                    pltpu.make_async_copy(block, held.at[buffer], sems.at[buffer]).start()

    @pl.when(pairs > 0)
    def _():
        fetch(0)
        turned[...] = own_ref[...].T

    total[...] = jnp.zeros_like(total)

    def step(index, carry):
        @pl.when(index + 1 < pairs)
        def _():
            fetch(index + 1)

        buffer = lax.rem(index, 2)
        pltpu.make_async_copy(blocks[0].at[0], held.at[buffer], sems.at[buffer]).wait()
        slot = todo[index]
        energy = lambda which: occ_ref[slot_orbital(place_ref, count, occ_count, which)]
        shift = energy(chunk) + energy(slot)
        other = held[buffer]
        exchange = jnp.dot(turned[...], other, preferred_element_type=jnp.float32)
        denom = (col_ref[:, chunk : chunk + 1] + row_ref[slot]) - shift
        amplitude = (exchange / denom).astype(jnp.bfloat16)
        total[...] += lax.dot_general(
            other, amplitude, (((1,), (1,)), ((), ())), preferred_element_type=jnp.float32
        )
        return carry

    lax.fori_loop(0, pairs, step, jnp.int32(0))
    part = outs[0].shape[0]
    for index, out in enumerate(outs):
        out[...] = total[index * part : (index + 1) * part, :].astype(jnp.bfloat16)


def densities(chunk, count, occ_count, live, codes, place, occ_energy, own, own_vir, vir_rows, blocks):
    aux, virs = own.shape
    rows = aux // count
    whole = lambda shape: pl.BlockSpec(shape, lambda: (0,) * len(shape))
    smem = pl.BlockSpec(memory_space=pltpu.SMEM)
    return pl.pallas_call(
        functools.partial(pair_kernel, chunk, count, occ_count),
        in_specs=[smem, smem, smem, smem, whole(own.shape), whole(own_vir.shape), whole(vir_rows.shape)]
        + [pl.BlockSpec(memory_space=pl.ANY)] * len(blocks),
        out_specs=[whole((rows, virs))] * count,
        out_shape=[jax.ShapeDtypeStruct((rows, virs), jnp.bfloat16)] * count,
        scratch_shapes=[
            pltpu.VMEM((virs, aux), jnp.bfloat16),
            pltpu.VMEM((aux, virs), jnp.float32),
            pltpu.VMEM((2, aux, virs), jnp.bfloat16),
            pltpu.SemaphoreType.DMA((2,)),
            pltpu.SMEM((codes.shape[0],), jnp.int32),
        ],
        compiler_params=pltpu.CompilerParams(vmem_limit_bytes=20 * MIB),
        cost_estimate=pl.CostEstimate(
            flops=4 * 4 * aux * virs * virs, bytes_accessed=6 * aux * virs, transcendentals=0
        ),
        name="pairs",
    )(live, codes, place, occ_energy, own, own_vir, vir_rows, *blocks)


def spread_kernel(count, pos_ref, *refs):
    pieces, out = refs[:-1], refs[-1]
    orbitals = count * OCC_DEV
    width = orbitals * ROWS
    row = lax.broadcasted_iota(jnp.int32, (width, width), 0)
    col = lax.broadcasted_iota(jnp.int32, (width, width), 1)
    group = col // ROWS
    place = lax.rem(pos_ref[0] + group % count, count) * OCC_DEV + group // count
    hit = jnp.where((row % orbitals == place) & (row // orbitals == col % ROWS), 1.0, 0.0).astype(jnp.bfloat16)
    for part in range(out.shape[0] // ROWS):
        span = pl.ds(part * ROWS, ROWS)
        rows = jnp.concatenate([piece[span, :] for piece in pieces], axis=0)
        moved = jnp.dot(hit, rows, preferred_element_type=jnp.float32).astype(jnp.bfloat16)
        out[span] = moved.reshape(ROWS, orbitals, -1)


def assembled(pieces, aux_pos, count):
    rows, virs = pieces[0].shape
    orbitals = count * OCC_DEV
    block = 4 * ROWS
    return pl.pallas_call(
        functools.partial(spread_kernel, count),
        grid_spec=pltpu.PrefetchScalarGridSpec(
            num_scalar_prefetch=1,
            grid=(rows // block,),
            in_specs=[pl.BlockSpec((block, virs), lambda g, pos: (g, 0))] * len(pieces),
            out_specs=pl.BlockSpec((block, orbitals, virs), lambda g, pos: (g, 0, 0)),
        ),
        out_shape=jax.ShapeDtypeStruct((rows, orbitals, virs), jnp.bfloat16),
        compiler_params=pltpu.CompilerParams(vmem_limit_bytes=20 * MIB),
        cost_estimate=pl.CostEstimate(
            flops=2 * rows * orbitals * virs * orbitals * ROWS,
            bytes_accessed=4 * rows * orbitals * virs,
            transcendentals=0,
        ),
        name="assemble",
    )(aux_pos, *pieces)


def body(half_ints, block_mask, vir_coef, domains, vir_energy, occ_energy, pair_count, pair_code):
    aux_count = lax.axis_size("aux")
    occ_count = lax.axis_size("occ")
    aux_pos = lax.axis_index("aux")
    occ_pos = lax.axis_index("occ")

    def along_aux(value, steps):
        return lax.ppermute(value, "aux", [(z, (z + steps) % aux_count) for z in range(aux_count)])

    rows_of, own_domains, place = sorted_rows(
        half_ints, block_mask, domains, aux_pos.astype(jnp.int32).reshape(1), occ_pos.astype(jnp.int32).reshape(1)
    )
    vir_rows, vir_cols = energies(place, domains, vir_energy, aux_count, occ_count)
    twin, direct, far, last, late = routes(occ_count)
    owns, nears, thirds, lates, sets, swaps = [], [], [], [], [], []
    transform = functools.partial(transformed, rows_of, own_domains, vir_coef, place, aux_count)
    sent = [None] * aux_count
    for step in list(range(1, aux_count)) + [0]:
        sent[step] = transform(0, step, 1, [])[0]
    after = [sent[0]]
    pieces = [sent[0]] + [along_aux(sent[step], step) for step in range(1, aux_count)]
    for chunk in range(OCC_DEV + 1):
        coming = []
        if chunk + 1 < OCC_DEV:
            sent = transform(chunk + 1, 0, aux_count, after)
            coming = [sent[0]] + [along_aux(sent[step], step) for step in range(1, aux_count)]
        if chunk < OCC_DEV:
            own = stacked(pieces, nears[-1:] + thirds[-1:] + lates[-2:-1] + coming[:1])
            near = lax.ppermute(own, "occ", direct)
            third = lax.ppermute(own, "occ", far)
            owns.append(own)
            nears.append(near)
            thirds.append(third)
            lates.append(lax.ppermute(third, "occ", last) if last else near)
        if chunk >= 1:
            waits = coming[1:] + nears[-1:] if coming else []
            both = with_next(owns[chunk - 1], nears[chunk - 1], lates[chunk - 1], late, place, waits)
            sets.append(both)
            swaps.append(lax.ppermute(both, "occ", twin))
        pieces, after = coming, [own, vir_rows]
    blocks = sets + swaps + thirds
    codes = pair_code[0, 0]
    results = []
    for chunk in range(OCC_DEV):
        pieces = densities(
            chunk, aux_count, occ_count, pair_count, codes, place, occ_energy, owns[chunk], vir_cols, vir_rows, blocks
        )
        results += [pieces[0]] + [along_aux(pieces[step], -step) for step in range(1, aux_count)]
    return assembled(results, place, aux_count)


def routes(count):
    chips = count // 2
    twin = [(n, n ^ 1) for n in range(count)]
    turned = [c for c in range(0, chips, 2)] if chips == 4 else []
    direct = [(n, (n - 2) % count) for n in range(count) if n % 2 or n // 2 not in turned]
    far = [((n + 3) % count, n) for n in range(1, count, 2)]
    last = [(2 * ((c + 2) % chips) + 1, 2 * ((c - 1) % chips)) for c in turned]
    late = [target for _, target in last]
    return twin, direct, far, last, late


def solution(mesh):
    placed = (
        P("aux", "occ", None),
        P("aux", "occ"),
        P(),
        P(),
        P(),
        P(),
        P("occ", "aux"),
        P("occ", "aux", None),
    )
    return jax.shard_map(
        body, mesh=mesh, in_specs=placed, out_specs=P("aux", "occ", None), check_vma=False
    )
```

profile of v0, /device:TPU:0, one launch (start us, length us, event | category | flops | bytes accessed | tf_op | source)
XLA Modules:
  0.0 278.5 jit_solution(10634494127980668218)
XLA Ops:
  1.6 8.5 %sort_rows.1 = (bf16[16,256,1024]{2,1,0:T(8,128)(2,1)S(1)}, s32[16,1,512]{2,1,0:T(1,128)S(1)}, s32[2]{0:T(128)S(1)}) custom-call(s32[4,16]{1,0:T(4,128)S(1)} %copy-done.5, s32[1]{0:T(128)} %bitcast.aux_ref, s32[1]{0:T(128)} %bitcast.1.occ_ref, bf16[256,16,1024]{2,1,0:T(8,128)(2,1)} %x_ref.1, s32[128,512]{1,0:T(8,128)S(1)} %copy-done.1), custom_call_target="tpu_custom_call" | custom-call | flops 2147483648 | bytes 16777216 | tf_op jit(solution)/shard_map/sort_rows/pallas_call | solution.py:47
  12.7 3.1 %collective-permute-start = (bf16[256,512]{1,0:T(8,128)(2,1)S(1)}, bf16[256,512]{1,0:T(8,128)(2,1)S(1)}, u32[]{:S(2)}, u32[]{:S(2)}) collective-permute-start(bf16[256,512]{1,0:T(8,128)(2,1)S(1)} %transform.8), channel_id=1, source_target_pairs={{0,8},{8,16},{16,24},{24,0},{1,9},{9,17},{17,25},{25,1},{2,10},{10... | collective-permute-start | bytes 786440 | tf_op jit(solution)/shard_map/ppermute | solution.py:371
  27.6 8.9 %transform.11 = (bf16[256,512]{1,0:T(8,128)(2,1)S(1)}, bf16[256,512]{1,0:T(8,128)(2,1)S(1)}, bf16[256,512]{1,0:T(8,128)(2,1)S(1)}, bf16[256,512]{1,0:T(8,128)(2,1)S(1)}) custom-call(s32[2]{0:T(128)S(1)} %get-tuple-element.38.pos_ref.place_ref, bf16[16,256,1024]{2,1,0:T(8,128)(2,1)S(1)} %get-tuple-element.39.x_ref, ...), custom_call_target="tpu_custom_call" | custom-call | flops 6442450944 | bytes 7340032 | tf_op jit(solution)/shard_map/transform/pallas_call | solution.py:107
  38.0 3.7 %collective-permute-start.4 = (bf16[1024,512]{1,0:T(8,128)(2,1)S(1)}, bf16[1024,512]{1,0:T(8,128)(2,1)S(1)}, u32[]{:S(2)}, u32[]{:S(2)}) collective-permute-start(bf16[1024,512]{1,0:T(8,128)(2,1)S(1)} %join.4.refs_0_.own_ref), channel_id=1, source_target_pairs={{4,1},{6,3},{0,5},{2,7},{12,9},{14,11},{8,13},{10,15},{20,17},{22,... | collective-permute-start | bytes 3145736 | tf_op jit(solution)/shard_map/ppermute | solution.py:393
  41.7 6.2 %collective-permute-start.9 = (bf16[256,512]{1,0:T(8,128)(2,1)S(1)}, bf16[256,512]{1,0:T(8,128)(2,1)S(1)}, u32[]{:S(2)}, u32[]{:S(2)}) collective-permute-start(bf16[256,512]{1,0:T(8,128)(2,1)S(1)} %get-tuple-element.47), channel_id=1, source_target_pairs={{0,8},{8,16},{16,24},{24,0},{1,9},{9,17},{17,25},{25,1},{2,10},{10... | collective-permute-start | bytes 786440 | tf_op jit(solution)/shard_map/ppermute | solution.py:371
  51.4 8.9 %transform.12 = (bf16[256,512]{1,0:T(8,128)(2,1)S(1)}, bf16[256,512]{1,0:T(8,128)(2,1)S(1)}, bf16[256,512]{1,0:T(8,128)(2,1)S(1)}, bf16[256,512]{1,0:T(8,128)(2,1)S(1)}) custom-call(s32[2]{0:T(128)S(1)} %get-tuple-element.38.pos_ref.place_ref, bf16[16,256,1024]{2,1,0:T(8,128)(2,1)S(1)} %get-tuple-element.39.x_ref, ...), custom_call_target="tpu_custom_call" | custom-call | flops 6442450944 | bytes 7340032 | tf_op jit(solution)/shard_map/transform/pallas_call | solution.py:107
  60.3 4.7 %collective-permute-done.10.refs_2_ = bf16[256,512]{1,0:T(8,128)(2,1)S(1)} collective-permute-done((bf16[256,512]{1,0:T(8,128)(2,1)S(1)}, bf16[256,512]{1,0:T(8,128)(2,1)S(1)}, u32[]{:S(2)}, u32[]{:S(2)}) %collective-permute-start.10) | collective-permute-done | bytes 262176 | tf_op jit(solution)/shard_map/ppermute | solution.py:371
  69.0 6.2 %collective-permute-start.6 = (bf16[256,512]{1,0:T(8,128)(2,1)S(1)}, bf16[256,512]{1,0:T(8,128)(2,1)S(1)}, u32[]{:S(2)}, u32[]{:S(2)}) collective-permute-start(bf16[256,512]{1,0:T(8,128)(2,1)S(1)} %get-tuple-element.44), channel_id=1, source_target_pairs={{0,8},{8,16},{16,24},{24,0},{1,9},{9,17},{17,25},{25,1},{2,10},{10... | collective-permute-start | bytes 786440 | tf_op jit(solution)/shard_map/ppermute | solution.py:371
  76.9 5.3 %collective-permute-done.6.refs_0_.refs_1_ = bf16[256,512]{1,0:T(8,128)(2,1)S(1)} collective-permute-done((bf16[256,512]{1,0:T(8,128)(2,1)S(1)}, bf16[256,512]{1,0:T(8,128)(2,1)S(1)}, u32[]{:S(2)}, u32[]{:S(2)}) %collective-permute-start.6) | collective-permute-done | bytes 262176 | tf_op jit(solution)/shard_map/ppermute | solution.py:371
  82.2 3.5 %collective-permute-start.8 = (bf16[256,512]{1,0:T(8,128)(2,1)S(1)}, bf16[256,512]{1,0:T(8,128)(2,1)S(1)}, u32[]{:S(2)}, u32[]{:S(2)}) collective-permute-start(bf16[256,512]{1,0:T(8,128)(2,1)S(1)} %get-tuple-element.46), channel_id=1, source_target_pairs={{0,24},{8,0},{16,8},{24,16},{1,25},{9,1},{17,9},{25,17},{2,26},{10... | collective-permute-start | bytes 786440 | tf_op jit(solution)/shard_map/ppermute | solution.py:371
  85.7 8.9 %transform.13 = (bf16[256,512]{1,0:T(8,128)(2,1)S(1)}, bf16[256,512]{1,0:T(8,128)(2,1)S(1)}, bf16[256,512]{1,0:T(8,128)(2,1)S(1)}, bf16[256,512]{1,0:T(8,128)(2,1)S(1)}) custom-call(s32[2]{0:T(128)S(1)} %get-tuple-element.38.pos_ref.place_ref, bf16[16,256,1024]{2,1,0:T(8,128)(2,1)S(1)} %get-tuple-element.39.x_ref, ...), custom_call_target="tpu_custom_call" | custom-call | flops 6442450944 | bytes 7340032 | tf_op jit(solution)/shard_map/transform/pallas_call | solution.py:107
  96.7 7.7 %collective-permute-start.19 = (bf16[1024,512]{1,0:T(8,128)(2,1)S(1)}, bf16[1024,512]{1,0:T(8,128)(2,1)S(1)}, u32[]{:S(2)}, u32[]{:S(2)}) collective-permute-start(bf16[1024,512]{1,0:T(8,128)(2,1)S(1)} %join.6.own_ref), channel_id=1, source_target_pairs={{4,1},{6,3},{0,5},{2,7},{12,9},{14,11},{8,13},{10,15},{20,17},{22,... | collective-permute-start | bytes 3145736 | tf_op jit(solution)/shard_map/ppermute | solution.py:393
  104.4 4.1 %collective-permute-start.15 = (bf16[256,512]{1,0:T(8,128)(2,1)S(1)}, bf16[256,512]{1,0:T(8,128)(2,1)S(1)}, u32[]{:S(2)}, u32[]{:S(2)}) collective-permute-start(bf16[256,512]{1,0:T(8,128)(2,1)S(1)} %get-tuple-element.51), channel_id=1, source_target_pairs={{0,8},{8,16},{16,24},{24,0},{1,9},{9,17},{17,25},{25,1},{2,10},{10... | collective-permute-start | bytes 786440 | tf_op jit(solution)/shard_map/ppermute | solution.py:371
  109.5 5.6 %collective-permute-done.15.refs_0_.refs_1_ = bf16[256,512]{1,0:T(8,128)(2,1)S(1)} collective-permute-done((bf16[256,512]{1,0:T(8,128)(2,1)S(1)}, bf16[256,512]{1,0:T(8,128)(2,1)S(1)}, u32[]{:S(2)}, u32[]{:S(2)}) %collective-permute-start.15) | collective-permute-done | bytes 262176 | tf_op jit(solution)/shard_map/ppermute | solution.py:371
  115.8 11.7 %collective-permute-done.16.refs_1_.refs_2_ = bf16[256,512]{1,0:T(8,128)(2,1)S(1)} collective-permute-done((bf16[256,512]{1,0:T(8,128)(2,1)S(1)}, bf16[256,512]{1,0:T(8,128)(2,1)S(1)}, u32[]{:S(2)}, u32[]{:S(2)}) %collective-permute-start.16) | collective-permute-done | bytes 262176 | tf_op jit(solution)/shard_map/ppermute | solution.py:371
  131.0 10.2 %collective-permute-done.22.refs_11_ = bf16[1024,512]{1,0:T(8,128)(2,1)S(1)} collective-permute-done((bf16[1024,512]{1,0:T(8,128)(2,1)S(1)}, bf16[1024,512]{1,0:T(8,128)(2,1)S(1)}, u32[]{:S(2)}, u32[]{:S(2)}) %collective-permute-start.22) | collective-permute-done | bytes 1048608 | tf_op jit(solution)/shard_map/ppermute | solution.py:393
  142.9 8.3 %collective-permute-start.24 = (bf16[2,1024,512]{2,1,0:T(8,128)(2,1)S(1)}, bf16[2,1024,512]{2,1,0:T(8,128)(2,1)S(1)}, u32[]{:S(2)}, u32[]{:S(2)}) collective-permute-start(bf16[2,1024,512]{2,1,0:T(8,128)(2,1)S(1)} %pick.4.refs_0_), channel_id=1, source_target_pairs={{0,1},{1,0},{2,3},{3,2},{4,5},{5,4},{6,7},{7,6},{8,9},{9,8},{10,11... | collective-permute-start | bytes 6291464 | tf_op jit(solution)/shard_map/ppermute | solution.py:402
  153.6 3.0 %collective-permute-done.21.near_ref = bf16[1024,512]{1,0:T(8,128)(2,1)S(1)} collective-permute-done((bf16[1024,512]{1,0:T(8,128)(2,1)S(1)}, bf16[1024,512]{1,0:T(8,128)(2,1)S(1)}, u32[]{:S(2)}, u32[]{:S(2)}) %collective-permute-start.21) | collective-permute-done | bytes 1048608 | tf_op jit(solution)/shard_map/ppermute | solution.py:392
  157.6 12.6 %collective-permute-start.27 = (bf16[2,1024,512]{2,1,0:T(8,128)(2,1)S(1)}, bf16[2,1024,512]{2,1,0:T(8,128)(2,1)S(1)}, u32[]{:S(2)}, u32[]{:S(2)}) collective-permute-start(bf16[2,1024,512]{2,1,0:T(8,128)(2,1)S(1)} %pick.7.refs_3_), channel_id=1, source_target_pairs={{0,1},{1,0},{2,3},{3,2},{4,5},{5,4},{6,7},{7,6},{8,9},{9,8},{10,11... | collective-permute-start | bytes 6291464 | tf_op jit(solution)/shard_map/ppermute | solution.py:402
  170.8 3.1 %collective-permute-done.27.refs_7_ = bf16[2,1024,512]{2,1,0:T(8,128)(2,1)S(1)} collective-permute-done((bf16[2,1024,512]{2,1,0:T(8,128)(2,1)S(1)}, bf16[2,1024,512]{2,1,0:T(8,128)(2,1)S(1)}, u32[]{:S(2)}, u32[]{:S(2)}) %collective-permute-start.27) | collective-permute-done | bytes 2097184 | tf_op jit(solution)/shard_map/ppermute | solution.py:402
  173.9 7.7 %pairs.4 = (bf16[256,512]{1,0:T(8,128)(2,1)S(1)}, bf16[256,512]{1,0:T(8,128)(2,1)S(1)}, bf16[256,512]{1,0:T(8,128)(2,1)S(1)}, bf16[256,512]{1,0:T(8,128)(2,1)S(1)}) custom-call(s32[1,1]{1,0:T(1,128)S(6)} %copy.9.live_ref, s32[16]{0:T(128)S(1)} %bitcast.4, s32[2]{0:T(128)S(1)} %get-tuple-element.38.pos_ref.place_ref, f32[128]{0:T(128)S(1)} %copy-done.3, ...), custom_call_target="tpu_custom_call" | custom-call | flops 4294967296 | bytes 3145728 | tf_op jit(solution)/shard_map/pairs/pallas_call | solution.py:304
  185.5 6.1 %pairs.5 = (bf16[256,512]{1,0:T(8,128)(2,1)S(1)}, bf16[256,512]{1,0:T(8,128)(2,1)S(1)}, bf16[256,512]{1,0:T(8,128)(2,1)S(1)}, bf16[256,512]{1,0:T(8,128)(2,1)S(1)}) custom-call(s32[1,1]{1,0:T(1,128)S(6)} %copy.9.live_ref, s32[16]{0:T(128)S(1)} %bitcast.5, s32[2]{0:T(128)S(1)} %get-tuple-element.38.pos_ref.place_ref, f32[128]{0:T(128)S(1)} %copy-done.3, ...), custom_call_target="tpu_custom_call" | custom-call | flops 4294967296 | bytes 3145728 | tf_op jit(solution)/shard_map/pairs/pallas_call | solution.py:304
  192.9 6.1 %pairs.6 = (bf16[256,512]{1,0:T(8,128)(2,1)S(1)}, bf16[256,512]{1,0:T(8,128)(2,1)S(1)}, bf16[256,512]{1,0:T(8,128)(2,1)S(1)}, bf16[256,512]{1,0:T(8,128)(2,1)S(1)}) custom-call(s32[1,1]{1,0:T(1,128)S(6)} %copy.9.live_ref, s32[16]{0:T(128)S(1)} %bitcast.6, s32[2]{0:T(128)S(1)} %get-tuple-element.38.pos_ref.place_ref, f32[128]{0:T(128)S(1)} %copy-done.3, ...), custom_call_target="tpu_custom_call" | custom-call | flops 4294967296 | bytes 3145728 | tf_op jit(solution)/shard_map/pairs/pallas_call | solution.py:304
  199.1 8.4 %collective-permute-done.29.refs_2_ = bf16[256,512]{1,0:T(8,128)(2,1)S(1)} collective-permute-done((bf16[256,512]{1,0:T(8,128)(2,1)S(1)}, bf16[256,512]{1,0:T(8,128)(2,1)S(1)}, u32[]{:S(2)}, u32[]{:S(2)}) %collective-permute-start.29) | collective-permute-done | bytes 262176 | tf_op jit(solution)/shard_map/ppermute | solution.py:371
  207.5 5.4 %collective-permute-start.34 = (bf16[256,512]{1,0:T(8,128)(2,1)S(1)}, bf16[256,512]{1,0:T(8,128)(2,1)S(1)}, u32[]{:S(2)}, u32[]{:S(2)}) collective-permute-start(bf16[256,512]{1,0:T(8,128)(2,1)S(1)} %get-tuple-element.64), channel_id=1, source_target_pairs={{0,24},{8,0},{16,8},{24,16},{1,25},{9,1},{17,9},{25,17},{2,26},{10... | collective-permute-start | bytes 786440 | tf_op jit(solution)/shard_map/ppermute | solution.py:371
  212.9 4.5 %pairs.7 = (bf16[256,512]{1,0:T(8,128)(2,1)S(1)}, bf16[256,512]{1,0:T(8,128)(2,1)S(1)}, bf16[256,512]{1,0:T(8,128)(2,1)S(1)}, bf16[256,512]{1,0:T(8,128)(2,1)S(1)}) custom-call(s32[1,1]{1,0:T(1,128)S(6)} %copy.9.live_ref, s32[16]{0:T(128)S(1)} %bitcast.7, s32[2]{0:T(128)S(1)} %get-tuple-element.38.pos_ref.place_ref, f32[128]{0:T(128)S(1)} %copy-done.3, ...), custom_call_target="tpu_custom_call" | custom-call | flops 4294967296 | bytes 3145728 | tf_op jit(solution)/shard_map/pairs/pallas_call | solution.py:304
  220.1 4.9 %collective-permute-start.36 = (bf16[256,512]{1,0:T(8,128)(2,1)S(1)}, bf16[256,512]{1,0:T(8,128)(2,1)S(1)}, u32[]{:S(2)}, u32[]{:S(2)}) collective-permute-start(bf16[256,512]{1,0:T(8,128)(2,1)S(1)} %get-tuple-element.66), channel_id=1, source_target_pairs={{0,8},{8,16},{16,24},{24,0},{1,9},{9,17},{17,25},{25,1},{2,10},{10... | collective-permute-start | bytes 786440 | tf_op jit(solution)/shard_map/ppermute | solution.py:371
  225.0 16.3 %collective-permute-done.32.refs_6_ = bf16[256,512]{1,0:T(8,128)(2,1)S(1)} collective-permute-done((bf16[256,512]{1,0:T(8,128)(2,1)S(1)}, bf16[256,512]{1,0:T(8,128)(2,1)S(1)}, u32[]{:S(2)}, u32[]{:S(2)}) %collective-permute-start.32) | collective-permute-done | bytes 262176 | tf_op jit(solution)/shard_map/ppermute | solution.py:371
  241.3 6.6 %collective-permute-start.39 = (bf16[256,512]{1,0:T(8,128)(2,1)S(1)}, bf16[256,512]{1,0:T(8,128)(2,1)S(1)}, u32[]{:S(2)}, u32[]{:S(2)}) collective-permute-start(bf16[256,512]{1,0:T(8,128)(2,1)S(1)} %get-tuple-element.70), channel_id=1, source_target_pairs={{0,8},{8,16},{16,24},{24,0},{1,9},{9,17},{17,25},{25,1},{2,10},{10... | collective-permute-start | bytes 786440 | tf_op jit(solution)/shard_map/ppermute | solution.py:371
  247.9 15.8 %collective-permute-done.35.refs_10_ = bf16[256,512]{1,0:T(8,128)(2,1)S(1)} collective-permute-done((bf16[256,512]{1,0:T(8,128)(2,1)S(1)}, bf16[256,512]{1,0:T(8,128)(2,1)S(1)}, u32[]{:S(2)}, u32[]{:S(2)}) %collective-permute-start.35) | collective-permute-done | bytes 262176 | tf_op jit(solution)/shard_map/ppermute | solution.py:371
  263.7 10.9 %collective-permute-done.38.refs_14_ = bf16[256,512]{1,0:T(8,128)(2,1)S(1)} collective-permute-done((bf16[256,512]{1,0:T(8,128)(2,1)S(1)}, bf16[256,512]{1,0:T(8,128)(2,1)S(1)}, u32[]{:S(2)}, u32[]{:S(2)}) %collective-permute-start.38) | collective-permute-done | bytes 262176 | tf_op jit(solution)/shard_map/ppermute | solution.py:371
  274.6 3.9 %assemble.1 = bf16[256,16,512]{2,1,0:T(8,128)(2,1)} custom-call(s32[2]{0:T(128)S(1)} %get-tuple-element.38.pos_ref.place_ref, bf16[256,512]{1,0:T(8,128)(2,1)S(1)} %get-tuple-element.55.refs_0_, bf16[256,512]{1,0:T(8,128)(2,1)S(1)} %collective-permute-done.28.refs_1_, bf16[256,512]{1,0:T(8,128)(2,1)S(1)} %collective-permute-done.29.refs_2_, ...), custom_call_target="tpu_custom_call" | custom-call | flops 1073741824 | bytes 8388608 | tf_op jit(solution)/shard_map/assemble/pallas_call | solution.py:345
  (82 shorter events, 46.8 us)
Async XLA Ops:
  12.7 23.8 %collective-permute-start = (bf16[256,512]{1,0:T(8,128)(2,1)S(1)}, bf16[256,512]{1,0:T(8,128)(2,1)S(1)}, u32[]{:S(2)}, u32[]{:S(2)}) collective-permute-start(bf16[256,512]{1,0:T(8,128)(2,1)S(1)} %transform.8), channel_id=1, source_target_pairs={{0,8},{8,16},{16,24},{24,0},{1,9},{9,17},{17,25},{25,1},{2,10},{10... | collective-permute-start | bytes 786440 | tf_op jit(solution)/shard_map/ppermute | solution.py:371
  18.4 18.1 %collective-permute-start.1 = (bf16[256,512]{1,0:T(8,128)(2,1)S(1)}, bf16[256,512]{1,0:T(8,128)(2,1)S(1)}, u32[]{:S(2)}, u32[]{:S(2)}) collective-permute-start(bf16[256,512]{1,0:T(8,128)(2,1)S(1)} %transform.9), channel_id=1, source_target_pairs={{0,16},{8,24},{16,0},{24,8},{1,17},{9,25},{17,1},{25,9},{2,18},{10... | collective-permute-start | bytes 786440 | tf_op jit(solution)/shard_map/ppermute | solution.py:371
  36.7 28.2 %collective-permute-start.3 = (bf16[1024,512]{1,0:T(8,128)(2,1)S(1)}, bf16[1024,512]{1,0:T(8,128)(2,1)S(1)}, u32[]{:S(2)}, u32[]{:S(2)}) collective-permute-start(bf16[1024,512]{1,0:T(8,128)(2,1)S(1)} %join.4.refs_0_.own_ref), channel_id=1, source_target_pairs={{1,7},{2,0},{3,1},{5,3},{6,4},{7,5},{9,15},{10,8},{11,9},{13,11},{... | collective-permute-start | bytes 3145736 | tf_op jit(solution)/shard_map/ppermute | solution.py:392
  38.0 26.9 %collective-permute-start.4 = (bf16[1024,512]{1,0:T(8,128)(2,1)S(1)}, bf16[1024,512]{1,0:T(8,128)(2,1)S(1)}, u32[]{:S(2)}, u32[]{:S(2)}) collective-permute-start(bf16[1024,512]{1,0:T(8,128)(2,1)S(1)} %join.4.refs_0_.own_ref), channel_id=1, source_target_pairs={{4,1},{6,3},{0,5},{2,7},{12,9},{14,11},{8,13},{10,15},{20,17},{22,... | collective-permute-start | bytes 3145736 | tf_op jit(solution)/shard_map/ppermute | solution.py:393
  41.7 18.5 %collective-permute-start.9 = (bf16[256,512]{1,0:T(8,128)(2,1)S(1)}, bf16[256,512]{1,0:T(8,128)(2,1)S(1)}, u32[]{:S(2)}, u32[]{:S(2)}) collective-permute-start(bf16[256,512]{1,0:T(8,128)(2,1)S(1)} %get-tuple-element.47), channel_id=1, source_target_pairs={{0,8},{8,16},{16,24},{24,0},{1,9},{9,17},{17,25},{25,1},{2,10},{10... | collective-permute-start | bytes 786440 | tf_op jit(solution)/shard_map/ppermute | solution.py:371
  47.9 17.0 %collective-permute-start.10 = (bf16[256,512]{1,0:T(8,128)(2,1)S(1)}, bf16[256,512]{1,0:T(8,128)(2,1)S(1)}, u32[]{:S(2)}, u32[]{:S(2)}) collective-permute-start(bf16[256,512]{1,0:T(8,128)(2,1)S(1)} %get-tuple-element.48), channel_id=1, source_target_pairs={{0,16},{8,24},{16,0},{24,8},{1,17},{9,25},{17,1},{25,9},{2,18},{10... | collective-permute-start | bytes 786440 | tf_op jit(solution)/shard_map/ppermute | solution.py:371
  48.4 16.5 %collective-permute-start.11 = (bf16[256,512]{1,0:T(8,128)(2,1)S(1)}, bf16[256,512]{1,0:T(8,128)(2,1)S(1)}, u32[]{:S(2)}, u32[]{:S(2)}) collective-permute-start(bf16[256,512]{1,0:T(8,128)(2,1)S(1)} %get-tuple-element.49), channel_id=1, source_target_pairs={{0,24},{8,0},{16,8},{24,16},{1,25},{9,1},{17,9},{25,17},{2,26},{10... | collective-permute-start | bytes 786440 | tf_op jit(solution)/shard_map/ppermute | solution.py:371
  65.0 29.6 %collective-permute-start.13 = (bf16[1024,512]{1,0:T(8,128)(2,1)S(1)}, bf16[1024,512]{1,0:T(8,128)(2,1)S(1)}, u32[]{:S(2)}, u32[]{:S(2)}) collective-permute-start(bf16[1024,512]{1,0:T(8,128)(2,1)S(1)} %join.5.refs_0_.own_ref), channel_id=1, source_target_pairs={{4,1},{6,3},{0,5},{2,7},{12,9},{14,11},{8,13},{10,15},{20,17},{22,... | collective-permute-start | bytes 3145736 | tf_op jit(solution)/shard_map/ppermute | solution.py:393
  67.0 28.4 %collective-permute-start.5 = (bf16[1024,512]{1,0:T(8,128)(2,1)S(1)}, bf16[1024,512]{1,0:T(8,128)(2,1)S(1)}, u32[]{:S(2)}, u32[]{:S(2)}) collective-permute-start(bf16[1024,512]{1,0:T(8,128)(2,1)S(1)} %collective-permute-done.4.refs_5_.refs_8_), channel_id=1, source_target_pairs={{5,6},{1,2},{13,14},{9,10},{21,22},{17,18},{29,30},{25,26}} | collective-permute-start | bytes 3145736 | tf_op jit(solution)/shard_map/ppermute | solution.py:397
  67.7 27.6 %collective-permute-start.12 = (bf16[1024,512]{1,0:T(8,128)(2,1)S(1)}, bf16[1024,512]{1,0:T(8,128)(2,1)S(1)}, u32[]{:S(2)}, u32[]{:S(2)}) collective-permute-start(bf16[1024,512]{1,0:T(8,128)(2,1)S(1)} %join.5.refs_0_.own_ref), channel_id=1, source_target_pairs={{1,7},{2,0},{3,1},{5,3},{6,4},{7,5},{9,15},{10,8},{11,9},{13,11},{... | collective-permute-start | bytes 3145736 | tf_op jit(solution)/shard_map/ppermute | solution.py:392
  75.2 20.1 %collective-permute-start.7 = (bf16[256,512]{1,0:T(8,128)(2,1)S(1)}, bf16[256,512]{1,0:T(8,128)(2,1)S(1)}, u32[]{:S(2)}, u32[]{:S(2)}) collective-permute-start(bf16[256,512]{1,0:T(8,128)(2,1)S(1)} %get-tuple-element.45), channel_id=1, source_target_pairs={{0,16},{8,24},{16,0},{24,8},{1,17},{9,25},{17,1},{25,9},{2,18},{10... | collective-permute-start | bytes 786440 | tf_op jit(solution)/shard_map/ppermute | solution.py:371
  94.6 32.9 %collective-permute-start.14 = (bf16[1024,512]{1,0:T(8,128)(2,1)S(1)}, bf16[1024,512]{1,0:T(8,128)(2,1)S(1)}, u32[]{:S(2)}, u32[]{:S(2)}) collective-permute-start(bf16[1024,512]{1,0:T(8,128)(2,1)S(1)} %collective-permute-done.13.refs_5_.refs_9_), channel_id=1, source_target_pairs={{5,6},{1,2},{13,14},{9,10},{21,22},{17,18},{29,30},{25,26}} | collective-permute-start | bytes 3145736 | tf_op jit(solution)/shard_map/ppermute | solution.py:397
  95.4 32.1 %collective-permute-start.18 = (bf16[1024,512]{1,0:T(8,128)(2,1)S(1)}, bf16[1024,512]{1,0:T(8,128)(2,1)S(1)}, u32[]{:S(2)}, u32[]{:S(2)}) collective-permute-start(bf16[1024,512]{1,0:T(8,128)(2,1)S(1)} %join.6.own_ref), channel_id=1, source_target_pairs={{1,7},{2,0},{3,1},{5,3},{6,4},{7,5},{9,15},{10,8},{11,9},{13,11},{... | collective-permute-start | bytes 3145736 | tf_op jit(solution)/shard_map/ppermute | solution.py:392
  96.7 30.8 %collective-permute-start.19 = (bf16[1024,512]{1,0:T(8,128)(2,1)S(1)}, bf16[1024,512]{1,0:T(8,128)(2,1)S(1)}, u32[]{:S(2)}, u32[]{:S(2)}) collective-permute-start(bf16[1024,512]{1,0:T(8,128)(2,1)S(1)} %join.6.own_ref), channel_id=1, source_target_pairs={{4,1},{6,3},{0,5},{2,7},{12,9},{14,11},{8,13},{10,15},{20,17},{22,... | collective-permute-start | bytes 3145736 | tf_op jit(solution)/shard_map/ppermute | solution.py:393
  108.5 18.9 %collective-permute-start.16 = (bf16[256,512]{1,0:T(8,128)(2,1)S(1)}, bf16[256,512]{1,0:T(8,128)(2,1)S(1)}, u32[]{:S(2)}, u32[]{:S(2)}) collective-permute-start(bf16[256,512]{1,0:T(8,128)(2,1)S(1)} %get-tuple-element.52), channel_id=1, source_target_pairs={{0,16},{8,24},{16,0},{24,8},{1,17},{9,25},{17,1},{25,9},{2,18},{10... | collective-permute-start | bytes 786440 | tf_op jit(solution)/shard_map/ppermute | solution.py:371
  129.0 23.2 %collective-permute-start.20 = (bf16[1024,512]{1,0:T(8,128)(2,1)S(1)}, bf16[1024,512]{1,0:T(8,128)(2,1)S(1)}, u32[]{:S(2)}, u32[]{:S(2)}) collective-permute-start(bf16[1024,512]{1,0:T(8,128)(2,1)S(1)} %collective-permute-done.19.refs_5_.refs_10_), channel_id=1, source_target_pairs={{5,6},{1,2},{13,14},{9,10},{21,22},{17,18},{29,30},{25,26}} | collective-permute-start | bytes 3145736 | tf_op jit(solution)/shard_map/ppermute | solution.py:397
  129.7 26.9 %collective-permute-start.21 = (bf16[1024,512]{1,0:T(8,128)(2,1)S(1)}, bf16[1024,512]{1,0:T(8,128)(2,1)S(1)}, u32[]{:S(2)}, u32[]{:S(2)}) collective-permute-start(bf16[1024,512]{1,0:T(8,128)(2,1)S(1)} %join.7.own_ref), channel_id=1, source_target_pairs={{1,7},{2,0},{3,1},{5,3},{6,4},{7,5},{9,15},{10,8},{11,9},{13,11},{... | collective-permute-start | bytes 3145736 | tf_op jit(solution)/shard_map/ppermute | solution.py:392
  142.9 27.9 %collective-permute-start.24 = (bf16[2,1024,512]{2,1,0:T(8,128)(2,1)S(1)}, bf16[2,1024,512]{2,1,0:T(8,128)(2,1)S(1)}, u32[]{:S(2)}, u32[]{:S(2)}) collective-permute-start(bf16[2,1024,512]{2,1,0:T(8,128)(2,1)S(1)} %pick.4.refs_0_), channel_id=1, source_target_pairs={{0,1},{1,0},{2,3},{3,2},{4,5},{5,4},{6,7},{7,6},{8,9},{9,8},{10,11... | collective-permute-start | bytes 6291464 | tf_op jit(solution)/shard_map/ppermute | solution.py:402
  152.1 18.8 %collective-permute-start.25 = (bf16[2,1024,512]{2,1,0:T(8,128)(2,1)S(1)}, bf16[2,1024,512]{2,1,0:T(8,128)(2,1)S(1)}, u32[]{:S(2)}, u32[]{:S(2)}) collective-permute-start(bf16[2,1024,512]{2,1,0:T(8,128)(2,1)S(1)} %pick.5.refs_1_), channel_id=1, source_target_pairs={{0,1},{1,0},{2,3},{3,2},{4,5},{5,4},{6,7},{7,6},{8,9},{9,8},{10,11... | collective-permute-start | bytes 6291464 | tf_op jit(solution)/shard_map/ppermute | solution.py:402
  153.1 17.7 %collective-permute-start.26 = (bf16[2,1024,512]{2,1,0:T(8,128)(2,1)S(1)}, bf16[2,1024,512]{2,1,0:T(8,128)(2,1)S(1)}, u32[]{:S(2)}, u32[]{:S(2)}) collective-permute-start(bf16[2,1024,512]{2,1,0:T(8,128)(2,1)S(1)} %pick.6.refs_2_), channel_id=1, source_target_pairs={{0,1},{1,0},{2,3},{3,2},{4,5},{5,4},{6,7},{7,6},{8,9},{9,8},{10,11... | collective-permute-start | bytes 6291464 | tf_op jit(solution)/shard_map/ppermute | solution.py:402
  181.6 17.4 %collective-permute-start.28 = (bf16[256,512]{1,0:T(8,128)(2,1)S(1)}, bf16[256,512]{1,0:T(8,128)(2,1)S(1)}, u32[]{:S(2)}, u32[]{:S(2)}) collective-permute-start(bf16[256,512]{1,0:T(8,128)(2,1)S(1)} %get-tuple-element.56), channel_id=1, source_target_pairs={{0,24},{8,0},{16,8},{24,16},{1,25},{9,1},{17,9},{25,17},{2,26},{10... | collective-permute-start | bytes 786440 | tf_op jit(solution)/shard_map/ppermute | solution.py:371
  181.7 25.8 %collective-permute-start.29 = (bf16[256,512]{1,0:T(8,128)(2,1)S(1)}, bf16[256,512]{1,0:T(8,128)(2,1)S(1)}, u32[]{:S(2)}, u32[]{:S(2)}) collective-permute-start(bf16[256,512]{1,0:T(8,128)(2,1)S(1)} %get-tuple-element.57), channel_id=1, source_target_pairs={{0,16},{8,24},{16,0},{24,8},{1,17},{9,25},{17,1},{25,9},{2,18},{10... | collective-permute-start | bytes 786440 | tf_op jit(solution)/shard_map/ppermute | solution.py:371
  183.6 33.9 %collective-permute-start.30 = (bf16[256,512]{1,0:T(8,128)(2,1)S(1)}, bf16[256,512]{1,0:T(8,128)(2,1)S(1)}, u32[]{:S(2)}, u32[]{:S(2)}) collective-permute-start(bf16[256,512]{1,0:T(8,128)(2,1)S(1)} %get-tuple-element.58), channel_id=1, source_target_pairs={{0,8},{8,16},{16,24},{24,0},{1,9},{9,17},{17,25},{25,1},{2,10},{10... | collective-permute-start | bytes 786440 | tf_op jit(solution)/shard_map/ppermute | solution.py:371
  191.7 28.4 %collective-permute-start.31 = (bf16[256,512]{1,0:T(8,128)(2,1)S(1)}, bf16[256,512]{1,0:T(8,128)(2,1)S(1)}, u32[]{:S(2)}, u32[]{:S(2)}) collective-permute-start(bf16[256,512]{1,0:T(8,128)(2,1)S(1)} %get-tuple-element.60), channel_id=1, source_target_pairs={{0,24},{8,0},{16,8},{24,16},{1,25},{9,1},{17,9},{25,17},{2,26},{10... | collective-permute-start | bytes 786440 | tf_op jit(solution)/shard_map/ppermute | solution.py:371
  191.7 49.5 %collective-permute-start.32 = (bf16[256,512]{1,0:T(8,128)(2,1)S(1)}, bf16[256,512]{1,0:T(8,128)(2,1)S(1)}, u32[]{:S(2)}, u32[]{:S(2)}) collective-permute-start(bf16[256,512]{1,0:T(8,128)(2,1)S(1)} %get-tuple-element.61), channel_id=1, source_target_pairs={{0,16},{8,24},{16,0},{24,8},{1,17},{9,25},{17,1},{25,9},{2,18},{10... | collective-permute-start | bytes 786440 | tf_op jit(solution)/shard_map/ppermute | solution.py:371
  199.1 42.2 %collective-permute-start.33 = (bf16[256,512]{1,0:T(8,128)(2,1)S(1)}, bf16[256,512]{1,0:T(8,128)(2,1)S(1)}, u32[]{:S(2)}, u32[]{:S(2)}) collective-permute-start(bf16[256,512]{1,0:T(8,128)(2,1)S(1)} %get-tuple-element.62), channel_id=1, source_target_pairs={{0,8},{8,16},{16,24},{24,0},{1,9},{9,17},{17,25},{25,1},{2,10},{10... | collective-permute-start | bytes 786440 | tf_op jit(solution)/shard_map/ppermute | solution.py:371
  207.5 33.8 %collective-permute-start.34 = (bf16[256,512]{1,0:T(8,128)(2,1)S(1)}, bf16[256,512]{1,0:T(8,128)(2,1)S(1)}, u32[]{:S(2)}, u32[]{:S(2)}) collective-permute-start(bf16[256,512]{1,0:T(8,128)(2,1)S(1)} %get-tuple-element.64), channel_id=1, source_target_pairs={{0,24},{8,0},{16,8},{24,16},{1,25},{9,1},{17,9},{25,17},{2,26},{10... | collective-permute-start | bytes 786440 | tf_op jit(solution)/shard_map/ppermute | solution.py:371
  217.5 46.2 %collective-permute-start.35 = (bf16[256,512]{1,0:T(8,128)(2,1)S(1)}, bf16[256,512]{1,0:T(8,128)(2,1)S(1)}, u32[]{:S(2)}, u32[]{:S(2)}) collective-permute-start(bf16[256,512]{1,0:T(8,128)(2,1)S(1)} %get-tuple-element.65), channel_id=1, source_target_pairs={{0,16},{8,24},{16,0},{24,8},{1,17},{9,25},{17,1},{25,9},{2,18},{10... | collective-permute-start | bytes 786440 | tf_op jit(solution)/shard_map/ppermute | solution.py:371
  220.1 43.7 %collective-permute-start.36 = (bf16[256,512]{1,0:T(8,128)(2,1)S(1)}, bf16[256,512]{1,0:T(8,128)(2,1)S(1)}, u32[]{:S(2)}, u32[]{:S(2)}) collective-permute-start(bf16[256,512]{1,0:T(8,128)(2,1)S(1)} %get-tuple-element.66), channel_id=1, source_target_pairs={{0,8},{8,16},{16,24},{24,0},{1,9},{9,17},{17,25},{25,1},{2,10},{10... | collective-permute-start | bytes 786440 | tf_op jit(solution)/shard_map/ppermute | solution.py:371
  241.2 22.5 %collective-permute-start.37 = (bf16[256,512]{1,0:T(8,128)(2,1)S(1)}, bf16[256,512]{1,0:T(8,128)(2,1)S(1)}, u32[]{:S(2)}, u32[]{:S(2)}) collective-permute-start(bf16[256,512]{1,0:T(8,128)(2,1)S(1)} %get-tuple-element.68), channel_id=1, source_target_pairs={{0,24},{8,0},{16,8},{24,16},{1,25},{9,1},{17,9},{25,17},{2,26},{10... | collective-permute-start | bytes 786440 | tf_op jit(solution)/shard_map/ppermute | solution.py:371
  241.3 33.4 %collective-permute-start.38 = (bf16[256,512]{1,0:T(8,128)(2,1)S(1)}, bf16[256,512]{1,0:T(8,128)(2,1)S(1)}, u32[]{:S(2)}, u32[]{:S(2)}) collective-permute-start(bf16[256,512]{1,0:T(8,128)(2,1)S(1)} %get-tuple-element.69), channel_id=1, source_target_pairs={{0,16},{8,24},{16,0},{24,8},{1,17},{9,25},{17,1},{25,9},{2,18},{10... | collective-permute-start | bytes 786440 | tf_op jit(solution)/shard_map/ppermute | solution.py:371
  241.3 33.3 %collective-permute-start.39 = (bf16[256,512]{1,0:T(8,128)(2,1)S(1)}, bf16[256,512]{1,0:T(8,128)(2,1)S(1)}, u32[]{:S(2)}, u32[]{:S(2)}) collective-permute-start(bf16[256,512]{1,0:T(8,128)(2,1)S(1)} %get-tuple-element.70), channel_id=1, source_target_pairs={{0,8},{8,16},{16,24},{24,0},{1,9},{9,17},{17,25},{25,1},{2,10},{10... | collective-permute-start | bytes 786440 | tf_op jit(solution)/shard_map/ppermute | solution.py:371
  (14 other events, 173.5 us)
where the time goes:
time: 281 us; the launch traced here: 279 us
  starting transfers between devices  102 us (36%)
  waiting for transfers between devices  95.3 us (34%)
  Pallas kernels  78.7 us (28%)
    ppermute x24, waiting for transfers between devices, along_aux(): lax.ppermute(value, 'aux', [(z, (z + steps) % aux_count) for z in range(a...  79 us
    ppermute x24, starting transfers between devices, along_aux(): lax.ppermute(value, 'aux', [(z, (z + steps) % aux_count) for z in range(a...  57.5 us
    pallas_call x7, Pallas kernels, transformed(): pl.pallas_call(functools.partial(transform_kernel, count, len(after)), gr...  36.9 us
    pallas_call x4, Pallas kernels, densities(): pl.pallas_call(functools.partial(pair_kernel, chunk, count, occ_count), i...  24.5 us
    ppermute x4, starting transfers between devices, body(): swaps.append(lax.ppermute(both, 'occ', twin))  21.5 us
    ppermute x4, starting transfers between devices, body(): third = lax.ppermute(own, 'occ', far)  14.7 us
    ppermute x4, waiting for transfers between devices, body(): third = lax.ppermute(own, 'occ', far)  10.2 us
    pallas_call x1, Pallas kernels, sorted_rows(): pl.pallas_call(sort_kernel, grid=(rows // block,), in_specs=[smem, smem,...  8.49 us
  transfers between devices with their start and end apart: 40, of which 13 were waited for; matrix products, arithmetic and copies ran while one was open for 0% of the time, Pallas kernels for 20%

commit v1 on v0

--- a/solution.py
+++ b/solution.py
@@ -14,14 +14,12 @@
 MIB = 1024 * 1024
 
 
-def sort_kernel(mask_ref, aux_ref, occ_ref, x_ref, dom_ref, out_ref, own_ref, place_ref):
+def sort_kernel(mask_ref, aux_ref, occ_ref, x_ref, out_ref, place_ref):
     step = pl.program_id(0)
     block, orbitals, basis = x_ref.shape
     width = orbitals * ROWS
     place_ref[0] = aux_ref[0]
     place_ref[1] = occ_ref[0]
-    start = pl.multiple_of(occ_ref[0] * orbitals, 8)
-    own_ref[:, 0, :] = dom_ref[pl.ds(start, orbitals), :]
     row = lax.broadcasted_iota(jnp.int32, (ROWS, width), 0)
     col = lax.broadcasted_iota(jnp.int32, (ROWS, width), 1)
     spread = jnp.concatenate(
@@ -39,10 +37,9 @@
         out_ref[:, span, :] = moved.astype(jnp.bfloat16).reshape(orbitals, ROWS, basis)
 
 
-def sorted_rows(half_ints, block_mask, domains, aux_pos, occ_pos):
+def sorted_rows(half_ints, block_mask, aux_pos, occ_pos):
     rows, orbitals, basis = half_ints.shape
-    virs = domains.shape[1]
-    block = BLK // 2
+    block = BLK
     smem = pl.BlockSpec(memory_space=pltpu.SMEM)
     return pl.pallas_call(
         sort_kernel,
@@ -52,16 +49,13 @@
             smem,
             smem,
             pl.BlockSpec((block, orbitals, basis), lambda g: (g, 0, 0)),
-            pl.BlockSpec(domains.shape, lambda g: (0, 0)),
         ],
         out_specs=[
             pl.BlockSpec((orbitals, block, basis), lambda g: (0, g, 0)),
-            pl.BlockSpec((orbitals, 1, virs), lambda g: (0, 0, 0)),
             smem,
         ],
         out_shape=[
             jax.ShapeDtypeStruct((orbitals, rows, basis), jnp.bfloat16),
-            jax.ShapeDtypeStruct((orbitals, 1, virs), jnp.int32),
             jax.ShapeDtypeStruct((2,), jnp.int32),
         ],
         compiler_params=pltpu.CompilerParams(vmem_limit_bytes=40 * MIB),
@@ -71,15 +65,15 @@
             transcendentals=0,
         ),
         name="sort_rows",
-    )(block_mask, aux_pos, occ_pos, half_ints, domains)
-
-
-def transform_kernel(count, after, pos_ref, x_ref, dom_ref, coef_ref, *refs):
+    )(block_mask, aux_pos, occ_pos, half_ints)
+
+
+def transform_kernel(count, orbitals, orbital, after, pos_ref, x_ref, dom_ref, coef_ref, *refs):
     out_refs = refs[after:]
     step = pl.program_id(0)
     tile = 512
     whole = coef_ref.shape[1]
-    dom = dom_ref[...]
+    dom = dom_ref[pl.ds(pos_ref[1] * orbitals + orbital(step, pos_ref), 1), :]
     total = None
     for part in range(whole // tile):
         full = jnp.dot(
@@ -96,22 +90,22 @@
             out_refs[index][...] = total
 
 
-def transformed(rows_of, own_domains, vir_coef, aux_pos, aux_count, chunk, first, count, after):
+def transformed(rows_of, domains, vir_coef, place, aux_count, chunk, chunk_step, first, first_step, count, after):
     orbitals, rows, basis = rows_of.shape
-    virs = own_domains.shape[2]
+    virs = domains.shape[1]
     whole = vir_coef.shape[1]
 
     def orbital(step, pos_ref):
-        return lax.rem(pos_ref[0] + first + step, aux_count) * OCC_DEV + chunk
-
-    return pl.pallas_call(
-        functools.partial(transform_kernel, count, len(after)),
+        return lax.rem(pos_ref[0] + first + step * first_step, aux_count) * OCC_DEV + chunk + step * chunk_step
+
+    return pl.pallas_call(
+        functools.partial(transform_kernel, count, orbitals, orbital, len(after)),
         grid_spec=pltpu.PrefetchScalarGridSpec(
             num_scalar_prefetch=1,
             grid=(count,),
             in_specs=[
                 pl.BlockSpec((None, rows, basis), lambda g, pos: (orbital(g, pos), 0, 0)),
-                pl.BlockSpec((None, 1, virs), lambda g, pos: (orbital(g, pos), 0, 0)),
+                pl.BlockSpec(domains.shape, lambda g, pos: (0, 0)),
                 pl.BlockSpec((basis, whole), lambda g, pos: (0, 0), pipeline_mode=pl.Buffered(1)),
             ]
             + [pl.BlockSpec(memory_space=pl.ANY)] * len(after),
@@ -125,29 +119,54 @@
             transcendentals=0,
         ),
         name="transform",
-    )(aux_pos, rows_of, own_domains, vir_coef, *after)
-
-
-def join_kernel(count, *refs):
-    out = refs[-1]
+    )(place, rows_of, domains, vir_coef, *after)
+
+
+def join_kernel(count, place_ref, *refs):
+    out = refs[count]
     rows = refs[0].shape[0]
     for index in range(count):
         out[index * rows : (index + 1) * rows, :] = refs[index][...]
 
 
-def stacked(pieces, after):
+def join_pass_kernel(count, place_ref, *refs):
+    out, onward = refs[-2:]
+    rows = refs[0].shape[0]
+    for index in range(count):
+        out[index * rows : (index + 1) * rows, :] = refs[index][...]
+
+    @pl.when(place_ref[1] % 2 == 0)
+    def _():
+        onward[...] = out[...]
+
+    @pl.when(place_ref[1] % 2 == 1)
+    def _():
+        onward[...] = refs[count][...]
+
+
+def stacked(pieces, place, held, after):
     rows, virs = pieces[0].shape
     count = len(pieces)
-    return pl.pallas_call(
-        functools.partial(join_kernel, count),
-        in_specs=[pl.BlockSpec((rows, virs), lambda: (0, 0))] * count
+    whole = pl.BlockSpec((count * rows, virs), lambda: (0, 0))
+    shape = jax.ShapeDtypeStruct((count * rows, virs), pieces[0].dtype)
+    kernel = join_pass_kernel if held else join_kernel
+    outs = 1 + len(held)
+
+    def entry(place_ref, *refs):
+        kernel(count, place_ref, *refs[: count + len(held)], *refs[-outs:])
+
+    return pl.pallas_call(
+        entry,
+        in_specs=[pl.BlockSpec(memory_space=pltpu.SMEM)]
+        + [pl.BlockSpec((rows, virs), lambda: (0, 0))] * count
+        + [whole] * len(held)
         + [pl.BlockSpec(memory_space=pl.ANY)] * len(after),
-        out_specs=pl.BlockSpec((count * rows, virs), lambda: (0, 0)),
-        out_shape=jax.ShapeDtypeStruct((count * rows, virs), pieces[0].dtype),
-        compiler_params=pltpu.CompilerParams(vmem_limit_bytes=16 * MIB),
-        cost_estimate=pl.CostEstimate(flops=0, bytes_accessed=4 * count * rows * virs, transcendentals=0),
+        out_specs=[whole] * outs,
+        out_shape=[shape] * outs,
+        compiler_params=pltpu.CompilerParams(vmem_limit_bytes=20 * MIB),
+        cost_estimate=pl.CostEstimate(flops=0, bytes_accessed=4 * count * rows * virs * outs, transcendentals=0),
         name="join",
-    )(*pieces, *after)
+    )(place, *pieces, *held, *after)
 
 
 def pick_kernel(late, place_ref, own_ref, near_ref, late_ref, *refs):
@@ -166,7 +185,7 @@
 
 def with_next(own, near, late_near, late, place, after):
     rows, virs = own.shape
-    block = rows // 4
+    block = rows // 2
     return pl.pallas_call(
         functools.partial(pick_kernel, late),
         grid=(rows // block,),
@@ -224,11 +243,14 @@
     )(place, domains, vir_energy.reshape(-1, 128))
 
 
-def pair_kernel(chunk, count, occ_count, live_ref, code_ref, place_ref, occ_ref, own_ref, col_ref, row_ref, *refs):
+def pair_kernel(chunk, count, occ_count, live_ref, code_ref, place_ref, occ_ref, *refs):
+    own_refs, (col_ref, row_ref), refs = refs[:count], refs[count : count + 2], refs[count + 2 :]
     sets = 3
     blocks = refs[: sets * OCC_DEV]
     outs = refs[sets * OCC_DEV : sets * OCC_DEV + count]
     turned, total, held, sems, todo = refs[sets * OCC_DEV + count :]
+    split = own_refs[0].shape[0]
+    aux = split * count
     span = PARTNERS * OCC_DEV
     slots = code_ref.shape[0]
     odd = place_ref[1] % 2
@@ -256,18 +278,25 @@
         place = source(todo[index])
         buffer = lax.rem(index, 2)
         for kind in range(5):
+            parts = [blocks[kind // 2 * OCC_DEV + orbital] for orbital in range(OCC_DEV)]
+            parts = [part.at[kind % 2] for part in parts] if kind < 4 else parts
             for orbital in range(OCC_DEV):
-                block = blocks[kind // 2 * OCC_DEV + orbital]
-                block = block.at[kind % 2] if kind < 4 else block
-
                 @pl.when(place == kind * OCC_DEV + orbital)
                 def _():
-                    pltpu.make_async_copy(block, held.at[buffer], sems.at[buffer]).start()
+                    if orbital == 0:
+                        first, rest = parts[0].at[pl.ds(0, split)], parts[0].at[pl.ds(split, aux - split)]
+                    else:
+                        start = aux if orbital == 1 else aux - split
+                        first = parts[orbital - 1].at[pl.ds(start, split)]
+                        rest = parts[orbital].at[pl.ds(0, aux - split)]
+                    pltpu.make_async_copy(first, held.at[buffer, pl.ds(0, split)], sems.at[buffer, 0]).start()
+                    pltpu.make_async_copy(rest, held.at[buffer, pl.ds(split, aux - split)], sems.at[buffer, 1]).start()
 
     @pl.when(pairs > 0)
     def _():
         fetch(0)
-        turned[...] = own_ref[...].T
+        for index, own_ref in enumerate(own_refs):
+            turned[:, index * split : (index + 1) * split] = own_ref[...].T
 
     total[...] = jnp.zeros_like(total)
 
@@ -277,7 +306,9 @@
             fetch(index + 1)
 
         buffer = lax.rem(index, 2)
-        pltpu.make_async_copy(blocks[0].at[0], held.at[buffer], sems.at[buffer]).wait()
+        first, rest = held.at[buffer, pl.ds(0, split)], held.at[buffer, pl.ds(split, aux - split)]
+        pltpu.make_async_copy(blocks[0].at[0, pl.ds(0, split)], first, sems.at[buffer, 0]).wait()
+        pltpu.make_async_copy(blocks[0].at[0, pl.ds(split, aux - split)], rest, sems.at[buffer, 1]).wait()
         slot = todo[index]
         energy = lambda which: occ_ref[slot_orbital(place_ref, count, occ_count, which)]
         shift = energy(chunk) + energy(slot)
@@ -297,13 +328,13 @@
 
 
 def densities(chunk, count, occ_count, live, codes, place, occ_energy, own, own_vir, vir_rows, blocks):
-    aux, virs = own.shape
-    rows = aux // count
+    rows, virs = own[0].shape
+    aux = rows * count
     whole = lambda shape: pl.BlockSpec(shape, lambda: (0,) * len(shape))
     smem = pl.BlockSpec(memory_space=pltpu.SMEM)
     return pl.pallas_call(
         functools.partial(pair_kernel, chunk, count, occ_count),
-        in_specs=[smem, smem, smem, smem, whole(own.shape), whole(own_vir.shape), whole(vir_rows.shape)]
+        in_specs=[smem] * 4 + [whole((rows, virs))] * count + [whole(own_vir.shape), whole(vir_rows.shape)]
         + [pl.BlockSpec(memory_space=pl.ANY)] * len(blocks),
         out_specs=[whole((rows, virs))] * count,
         out_shape=[jax.ShapeDtypeStruct((rows, virs), jnp.bfloat16)] * count,
@@ -311,7 +342,7 @@
             pltpu.VMEM((virs, aux), jnp.bfloat16),
             pltpu.VMEM((aux, virs), jnp.float32),
             pltpu.VMEM((2, aux, virs), jnp.bfloat16),
-            pltpu.SemaphoreType.DMA((2,)),
+            pltpu.SemaphoreType.DMA((2, 2)),
             pltpu.SMEM((codes.shape[0],), jnp.int32),
         ],
         compiler_params=pltpu.CompilerParams(vmem_limit_bytes=20 * MIB),
@@ -319,7 +350,7 @@
             flops=4 * 4 * aux * virs * virs, bytes_accessed=6 * aux * virs, transcendentals=0
         ),
         name="pairs",
-    )(live, codes, place, occ_energy, own, own_vir, vir_rows, *blocks)
+    )(live, codes, place, occ_energy, *own, own_vir, vir_rows, *blocks)
 
 
 def spread_kernel(count, pos_ref, *refs):
@@ -370,31 +401,43 @@
     def along_aux(value, steps):
         return lax.ppermute(value, "aux", [(z, (z + steps) % aux_count) for z in range(aux_count)])
 
-    rows_of, own_domains, place = sorted_rows(
-        half_ints, block_mask, domains, aux_pos.astype(jnp.int32).reshape(1), occ_pos.astype(jnp.int32).reshape(1)
+    rows_of, place = sorted_rows(
+        half_ints, block_mask, aux_pos.astype(jnp.int32).reshape(1), occ_pos.astype(jnp.int32).reshape(1)
     )
     vir_rows, vir_cols = energies(place, domains, vir_energy, aux_count, occ_count)
     twin, direct, far, last, late = routes(occ_count)
-    owns, nears, thirds, lates, sets, swaps = [], [], [], [], [], []
-    transform = functools.partial(transformed, rows_of, own_domains, vir_coef, place, aux_count)
+    transform = functools.partial(transformed, rows_of, domains, vir_coef, place, aux_count)
+
+    order = list(range(1, aux_count)) + [0]
     sent = [None] * aux_count
-    for step in list(range(1, aux_count)) + [0]:
-        sent[step] = transform(0, step, 1, [])[0]
+    for step in order:
+        sent[step] = transform(0, 0, step, 0, 1, [])[0]
+    pieces = [sent[0]] + [along_aux(sent[step], step) for step in range(1, aux_count)]
+    parts, owns, nears, thirds, lates, sets, swaps = [], [], [], [], [], [], []
     after = [sent[0]]
-    pieces = [sent[0]] + [along_aux(sent[step], step) for step in range(1, aux_count)]
     for chunk in range(OCC_DEV + 1):
         coming = []
         if chunk + 1 < OCC_DEV:
-            sent = transform(chunk + 1, 0, aux_count, after)
+            sent = transform(chunk + 1, 0, 0, 1, aux_count, after)
             coming = [sent[0]] + [along_aux(sent[step], step) for step in range(1, aux_count)]
         if chunk < OCC_DEV:
-            own = stacked(pieces, nears[-1:] + thirds[-1:] + lates[-2:-1] + coming[:1])
+            parts.append(pieces)
+            message = pieces[0 if chunk == 0 else 1 :] + coming[:1]
+            rides = bool(last) and 1 < chunk < OCC_DEV - 1
+            ready = nears[-1:] + ([] if rides else thirds[-1:] + lates[-1:])
+            own, *onward = stacked(message, place, thirds[-1:] if rides else [], ready)
             near = lax.ppermute(own, "occ", direct)
-            third = lax.ppermute(own, "occ", far)
+            third = lax.ppermute(onward[0], "occ", far + last) if rides else lax.ppermute(own, "occ", far)
             owns.append(own)
             nears.append(near)
             thirds.append(third)
-            lates.append(lax.ppermute(third, "occ", last) if last else near)
+            if rides:
+                lates.append(third)
+            if last and chunk != 1:
+                onward = stacked([third], place, [], coming[1:3])[0] if coming else third
+                lates.append(lax.ppermute(onward, "occ", last))
+            if not last:
+                lates.append(near)
         if chunk >= 1:
             waits = coming[1:] + nears[-1:] if coming else []
             both = with_next(owns[chunk - 1], nears[chunk - 1], lates[chunk - 1], late, place, waits)
@@ -406,7 +449,7 @@
     results = []
     for chunk in range(OCC_DEV):
         pieces = densities(
-            chunk, aux_count, occ_count, pair_count, codes, place, occ_energy, owns[chunk], vir_cols, vir_rows, blocks
+            chunk, aux_count, occ_count, pair_count, codes, place, occ_energy, parts[chunk], vir_cols, vir_rows, blocks
         )
         results += [pieces[0]] + [along_aux(pieces[step], -step) for step in range(1, aux_count)]
     return assembled(results, place, aux_count)

time: 281 us -> 296 us (1.053)
  starting transfers between devices: 102 us -> 129 us
  Pallas kernels: 78.7 us -> 64 us
  waiting for transfers between devices: 95.3 us -> 100 us
    ppermute x24, starting transfers between devices: 57.5 us -> 77.3 us  [along_aux(): lax.ppermute(value, 'aux', [(z, (z + steps) % aux_count) for z in range(a...]
    pallas_call x4, Pallas kernels: 24.5 us -> 8.35 us  [densities(): pl.pallas_call(functools.partial(pair_kernel, chunk, count, occ_count), i...]
    ppermute x24, waiting for transfers between devices: 79 us -> 89.7 us  [along_aux(): lax.ppermute(value, 'aux', [(z, (z + steps) % aux_count) for z in range(a...]
    ppermute x8 -> x7, starting transfers between devices: 17.6 us -> 27.8 us  [the longest x3 22.8 us: body(): lax.ppermute(own, 'occ', far)]
    pallas_call x11 -> x13, Pallas kernels: 37.2 us -> 40.6 us  [the longest x7 36.9 us: transformed(): pl.pallas_call(functools.partial(transform_kernel, count, orbitals, orbit...]
    ppermute x8 -> x7, waiting for transfers between devices: 10.2 us -> 7.12 us  [the longest x3 7.11 us: body(): lax.ppermute(own, 'occ', far)]
    ppermute x4, starting transfers between devices: 21.5 us -> 18.5 us  [body(): swaps.append(lax.ppermute(both, 'occ', twin))]
  transfers between devices with their start and end apart: 40 -> 39, of which waited for: 13 -> 14; matrix products, arithmetic and copies ran while one was open for 0% -> 0% of each run, Pallas kernels for 20% -> 15%
where the time goes in v1:
time: 296 us; the launch traced here: 295 us
  starting transfers between devices  129 us (44%)
  waiting for transfers between devices  100 us (34%)
  Pallas kernels  64 us (22%)
    ppermute x24, waiting for transfers between devices, along_aux(): lax.ppermute(value, 'aux', [(z, (z + steps) % aux_count) for z in range(a...  89.7 us
    ppermute x24, starting transfers between devices, along_aux(): lax.ppermute(value, 'aux', [(z, (z + steps) % aux_count) for z in range(a...  77.3 us
    pallas_call x7, Pallas kernels, transformed(): pl.pallas_call(functools.partial(transform_kernel, count, orbitals, orbit...  36.9 us
    ppermute x3, starting transfers between devices, body(): lax.ppermute(own, 'occ', far)  22.8 us
    ppermute x4, starting transfers between devices, body(): swaps.append(lax.ppermute(both, 'occ', twin))  18.5 us
    pallas_call x4, Pallas kernels, densities(): pl.pallas_call(functools.partial(pair_kernel, chunk, count, occ_count), i...  8.35 us
    ppermute x3, waiting for transfers between devices, body(): lax.ppermute(own, 'occ', far)  7.11 us
    pallas_call x1, Pallas kernels, sorted_rows(): pl.pallas_call(sort_kernel, grid=(rows // block,), in_specs=[smem, smem,...  6.67 us
  transfers between devices with their start and end apart: 39, of which 14 were waited for; matrix products, arithmetic and copies ran while one was open for 0% of the time, Pallas kernels for 15%

profile of v1, /device:TPU:0, one launch (start us, length us, event | category | flops | bytes accessed | tf_op | source)
XLA Modules:
  0.0 294.8 jit_solution(7854261584323636252)
XLA Ops:
  0.7 6.7 %sort_rows.1 = (bf16[16,256,1024]{2,1,0:T(8,128)(2,1)S(1)}, s32[2]{0:T(128)S(1)}) custom-call(s32[4,16]{1,0:T(4,128)S(1)} %copy-done.5, s32[1]{0:T(128)} %bitcast.aux_ref, s32[1]{0:T(128)} %bitcast.1.occ_ref, bf16[256,16,1024]{2,1,0:T(8,128)(2,1)} %x_ref.1), custom_call_target="tpu_custom_call" | custom-call | flops 2147483648 | bytes 16777216 | tf_op jit(solution)/shard_map/sort_rows/pallas_call | solution.py:44
  10.0 3.1 %collective-permute-start = (bf16[256,512]{1,0:T(8,128)(2,1)S(1)}, bf16[256,512]{1,0:T(8,128)(2,1)S(1)}, u32[]{:S(2)}, u32[]{:S(2)}) collective-permute-start(bf16[256,512]{1,0:T(8,128)(2,1)S(1)} %transform.8), channel_id=1, source_target_pairs={{0,8},{8,16},{16,24},{24,0},{1,9},{9,17},{17,25},{25,1},{2,10},{10... | collective-permute-start | bytes 786440 | tf_op jit(solution)/shard_map/ppermute | solution.py:402
  24.9 8.9 %transform.11 = (bf16[256,512]{1,0:T(8,128)(2,1)S(1)}, bf16[256,512]{1,0:T(8,128)(2,1)S(1)}, bf16[256,512]{1,0:T(8,128)(2,1)S(1)}, bf16[256,512]{1,0:T(8,128)(2,1)S(1)}) custom-call(s32[2]{0:T(128)S(1)} %get-tuple-element.39.pos_ref.place_ref, bf16[16,256,1024]{2,1,0:T(8,128)(2,1)S(1)} %get-tuple-element.40.x_ref, s32[128,512]{1,0:T(8,128)S(1)} %copy-done.1, ...), custom_call_target="tpu_custom_call" | custom-call | flops 6442450944 | bytes 7340032 | tf_op jit(solution)/shard_map/transform/pallas_call | solution.py:101
  36.5 6.2 %collective-permute-start.5 = (bf16[256,512]{1,0:T(8,128)(2,1)S(1)}, bf16[256,512]{1,0:T(8,128)(2,1)S(1)}, u32[]{:S(2)}, u32[]{:S(2)}) collective-permute-start(bf16[256,512]{1,0:T(8,128)(2,1)S(1)} %get-tuple-element.44), channel_id=1, source_target_pairs={{0,8},{8,16},{16,24},{24,0},{1,9},{9,17},{17,25},{25,1},{2,10},{10... | collective-permute-start | bytes 786440 | tf_op jit(solution)/shard_map/ppermute | solution.py:402
  44.5 5.5 %collective-permute-done.5.refs_1_.refs_0_ = bf16[256,512]{1,0:T(8,128)(2,1)S(1)} collective-permute-done((bf16[256,512]{1,0:T(8,128)(2,1)S(1)}, bf16[256,512]{1,0:T(8,128)(2,1)S(1)}, u32[]{:S(2)}, u32[]{:S(2)}) %collective-permute-start.5) | collective-permute-done | bytes 262176 | tf_op jit(solution)/shard_map/ppermute | solution.py:402
  50.0 8.6 %collective-permute-done.6.refs_2_.refs_1_ = bf16[256,512]{1,0:T(8,128)(2,1)S(1)} collective-permute-done((bf16[256,512]{1,0:T(8,128)(2,1)S(1)}, bf16[256,512]{1,0:T(8,128)(2,1)S(1)}, u32[]{:S(2)}, u32[]{:S(2)}) %collective-permute-start.6) | collective-permute-done | bytes 262176 | tf_op jit(solution)/shard_map/ppermute | solution.py:402
  63.4 8.9 %transform.12 = (bf16[256,512]{1,0:T(8,128)(2,1)S(1)}, bf16[256,512]{1,0:T(8,128)(2,1)S(1)}, bf16[256,512]{1,0:T(8,128)(2,1)S(1)}, bf16[256,512]{1,0:T(8,128)(2,1)S(1)}) custom-call(s32[2]{0:T(128)S(1)} %get-tuple-element.39.pos_ref.place_ref, bf16[16,256,1024]{2,1,0:T(8,128)(2,1)S(1)} %get-tuple-element.40.x_ref, s32[128,512]{1,0:T(8,128)S(1)} %copy-done.1, ...), custom_call_target="tpu_custom_call" | custom-call | flops 6442450944 | bytes 7340032 | tf_op jit(solution)/shard_map/transform/pallas_call | solution.py:101
  75.3 15.3 %collective-permute-start.13 = (bf16[1024,512]{1,0:T(8,128)(2,1)S(1)}, bf16[1024,512]{1,0:T(8,128)(2,1)S(1)}, u32[]{:S(2)}, u32[]{:S(2)}) collective-permute-start(bf16[1024,512]{1,0:T(8,128)(2,1)S(1)} %join.8.refs_0_.own_ref), channel_id=1, source_target_pairs={{4,1},{6,3},{0,5},{2,7},{12,9},{14,11},{8,13},{10,15},{20,17},{22,... | collective-permute-start | bytes 3145736 | tf_op jit(solution)/shard_map/ppermute | solution.py:430
  90.6 4.4 %collective-permute-start.8 = (bf16[256,512]{1,0:T(8,128)(2,1)S(1)}, bf16[256,512]{1,0:T(8,128)(2,1)S(1)}, u32[]{:S(2)}, u32[]{:S(2)}) collective-permute-start(bf16[256,512]{1,0:T(8,128)(2,1)S(1)} %get-tuple-element.46), channel_id=1, source_target_pairs={{0,8},{8,16},{16,24},{24,0},{1,9},{9,17},{17,25},{25,1},{2,10},{10... | collective-permute-start | bytes 786440 | tf_op jit(solution)/shard_map/ppermute | solution.py:402
  97.5 8.9 %transform.13 = (bf16[256,512]{1,0:T(8,128)(2,1)S(1)}, bf16[256,512]{1,0:T(8,128)(2,1)S(1)}, bf16[256,512]{1,0:T(8,128)(2,1)S(1)}, bf16[256,512]{1,0:T(8,128)(2,1)S(1)}) custom-call(s32[2]{0:T(128)S(1)} %get-tuple-element.39.pos_ref.place_ref, bf16[16,256,1024]{2,1,0:T(8,128)(2,1)S(1)} %get-tuple-element.40.x_ref, s32[128,512]{1,0:T(8,128)S(1)} %copy-done.1, ...), custom_call_target="tpu_custom_call" | custom-call | flops 6442450944 | bytes 7340032 | tf_op jit(solution)/shard_map/transform/pallas_call | solution.py:101
  106.4 5.7 %collective-permute-done.9.refs_1_.refs_2_ = bf16[256,512]{1,0:T(8,128)(2,1)S(1)} collective-permute-done((bf16[256,512]{1,0:T(8,128)(2,1)S(1)}, bf16[256,512]{1,0:T(8,128)(2,1)S(1)}, u32[]{:S(2)}, u32[]{:S(2)}) %collective-permute-start.9) | collective-permute-done | bytes 262176 | tf_op jit(solution)/shard_map/ppermute | solution.py:402
  112.8 2.8 collective-permute-start.14
  115.6 5.7 %collective-permute-start.15 = (bf16[256,512]{1,0:T(8,128)(2,1)S(1)}, bf16[256,512]{1,0:T(8,128)(2,1)S(1)}, u32[]{:S(2)}, u32[]{:S(2)}) collective-permute-start(bf16[256,512]{1,0:T(8,128)(2,1)S(1)} %get-tuple-element.53), channel_id=1, source_target_pairs={{0,8},{8,16},{16,24},{24,0},{1,9},{9,17},{17,25},{25,1},{2,10},{10... | collective-permute-start | bytes 786440 | tf_op jit(solution)/shard_map/ppermute | solution.py:402
  123.9 3.8 %collective-permute-done.15.refs_0_.refs_1_ = bf16[256,512]{1,0:T(8,128)(2,1)S(1)} collective-permute-done((bf16[256,512]{1,0:T(8,128)(2,1)S(1)}, bf16[256,512]{1,0:T(8,128)(2,1)S(1)}, u32[]{:S(2)}, u32[]{:S(2)}) %collective-permute-start.15) | collective-permute-done | bytes 262176 | tf_op jit(solution)/shard_map/ppermute | solution.py:402
  127.7 12.8 %collective-permute-done.16.refs_1_.refs_2_ = bf16[256,512]{1,0:T(8,128)(2,1)S(1)} collective-permute-done((bf16[256,512]{1,0:T(8,128)(2,1)S(1)}, bf16[256,512]{1,0:T(8,128)(2,1)S(1)}, u32[]{:S(2)}, u32[]{:S(2)}) %collective-permute-start.16) | collective-permute-done | bytes 262176 | tf_op jit(solution)/shard_map/ppermute | solution.py:402
  142.9 8.1 %collective-permute-done.17.refs_2_.refs_3_ = bf16[256,512]{1,0:T(8,128)(2,1)S(1)} collective-permute-done((bf16[256,512]{1,0:T(8,128)(2,1)S(1)}, bf16[256,512]{1,0:T(8,128)(2,1)S(1)}, u32[]{:S(2)}, u32[]{:S(2)}) %collective-permute-start.17) | collective-permute-done | bytes 262176 | tf_op jit(solution)/shard_map/ppermute | solution.py:402
  151.6 5.6 %collective-permute-start.21 = (bf16[768,512]{1,0:T(8,128)(2,1)S(1)}, bf16[768,512]{1,0:T(8,128)(2,1)S(1)}, u32[]{:S(2)}, u32[]{:S(2)}) collective-permute-start(bf16[768,512]{1,0:T(8,128)(2,1)S(1)} %join.11.own_ref), channel_id=1, source_target_pairs={{4,1},{6,3},{0,5},{2,7},{12,9},{14,11},{8,13},{10,15},{20,17},{22,... | collective-permute-start | bytes 2359304 | tf_op jit(solution)/shard_map/ppermute | solution.py:430
  159.5 7.1 %collective-permute-done.21.refs_17_ = bf16[768,512]{1,0:T(8,128)(2,1)S(1)} collective-permute-done((bf16[768,512]{1,0:T(8,128)(2,1)S(1)}, bf16[768,512]{1,0:T(8,128)(2,1)S(1)}, u32[]{:S(2)}, u32[]{:S(2)}) %collective-permute-start.21) | collective-permute-done | bytes 786464 | tf_op jit(solution)/shard_map/ppermute | solution.py:430
  168.2 11.4 %collective-permute-start.24 = (bf16[2,1024,512]{2,1,0:T(8,128)(2,1)S(1)}, bf16[2,1024,512]{2,1,0:T(8,128)(2,1)S(1)}, u32[]{:S(2)}, u32[]{:S(2)}) collective-permute-start(bf16[2,1024,512]{2,1,0:T(8,128)(2,1)S(1)} %pick.5.refs_7_), channel_id=1, source_target_pairs={{0,1},{1,0},{2,3},{3,2},{4,5},{5,4},{6,7},{7,6},{8,9},{9,8},{10,11... | collective-permute-start | bytes 6291464 | tf_op jit(solution)/shard_map/ppermute | solution.py:445
  181.4 7.0 %collective-permute-start.26 = (bf16[2,768,512]{2,1,0:T(8,128)(2,1)S(1)}, bf16[2,768,512]{2,1,0:T(8,128)(2,1)S(1)}, u32[]{:S(2)}, u32[]{:S(2)}) collective-permute-start(bf16[2,768,512]{2,1,0:T(8,128)(2,1)S(1)} %pick.7.refs_9_), channel_id=1, source_target_pairs={{0,1},{1,0},{2,3},{3,2},{4,5},{5,4},{6,7},{7,6},{8,9},{9,8},{10,11... | collective-permute-start | bytes 4718600 | tf_op jit(solution)/shard_map/ppermute | solution.py:445
  191.4 3.0 %pairs.4 = (bf16[256,512]{1,0:T(8,128)(2,1)S(1)}, bf16[256,512]{1,0:T(8,128)(2,1)S(1)}, bf16[256,512]{1,0:T(8,128)(2,1)S(1)}, bf16[256,512]{1,0:T(8,128)(2,1)S(1)}) custom-call(s32[1,1]{1,0:T(1,128)S(6)} %copy.9.live_ref, s32[16]{0:T(128)S(1)} %bitcast.4, s32[2]{0:T(128)S(1)} %get-tuple-element.39.pos_ref.place_ref, f32[128]{0:T(128)S(1)} %copy-done.3, ...), custom_call_target="tpu_custom_call" | custom-call | flops 4294967296 | bytes 3145728 | tf_op jit(solution)/shard_map/pairs/pallas_call | solution.py:335
  194.4 4.3 %collective-permute-start.27 = (bf16[256,512]{1,0:T(8,128)(2,1)S(1)}, bf16[256,512]{1,0:T(8,128)(2,1)S(1)}, u32[]{:S(2)}, u32[]{:S(2)}) collective-permute-start(bf16[256,512]{1,0:T(8,128)(2,1)S(1)} %get-tuple-element.58), channel_id=1, source_target_pairs={{0,24},{8,0},{16,8},{24,16},{1,25},{9,1},{17,9},{25,17},{2,26},{10... | collective-permute-start | bytes 786440 | tf_op jit(solution)/shard_map/ppermute | solution.py:402
  198.7 6.0 %collective-permute-start.28 = (bf16[256,512]{1,0:T(8,128)(2,1)S(1)}, bf16[256,512]{1,0:T(8,128)(2,1)S(1)}, u32[]{:S(2)}, u32[]{:S(2)}) collective-permute-start(bf16[256,512]{1,0:T(8,128)(2,1)S(1)} %get-tuple-element.59), channel_id=1, source_target_pairs={{0,16},{8,24},{16,0},{24,8},{1,17},{9,25},{17,1},{25,9},{2,18},{10... | collective-permute-start | bytes 786440 | tf_op jit(solution)/shard_map/ppermute | solution.py:402
  204.7 3.0 %pairs.5 = (bf16[256,512]{1,0:T(8,128)(2,1)S(1)}, bf16[256,512]{1,0:T(8,128)(2,1)S(1)}, bf16[256,512]{1,0:T(8,128)(2,1)S(1)}, bf16[256,512]{1,0:T(8,128)(2,1)S(1)}) custom-call(s32[1,1]{1,0:T(1,128)S(6)} %copy.9.live_ref, s32[16]{0:T(128)S(1)} %bitcast.5, s32[2]{0:T(128)S(1)} %get-tuple-element.39.pos_ref.place_ref, f32[128]{0:T(128)S(1)} %copy-done.3, ...), custom_call_target="tpu_custom_call" | custom-call | flops 4294967296 | bytes 3145728 | tf_op jit(solution)/shard_map/pairs/pallas_call | solution.py:335
  212.7 9.6 %collective-permute-start.32 = (bf16[256,512]{1,0:T(8,128)(2,1)S(1)}, bf16[256,512]{1,0:T(8,128)(2,1)S(1)}, u32[]{:S(2)}, u32[]{:S(2)}) collective-permute-start(bf16[256,512]{1,0:T(8,128)(2,1)S(1)} %get-tuple-element.64), channel_id=1, source_target_pairs={{0,8},{8,16},{16,24},{24,0},{1,9},{9,17},{17,25},{25,1},{2,10},{10... | collective-permute-start | bytes 786440 | tf_op jit(solution)/shard_map/ppermute | solution.py:402
  222.3 21.9 %collective-permute-done.28.refs_2_ = bf16[256,512]{1,0:T(8,128)(2,1)S(1)} collective-permute-done((bf16[256,512]{1,0:T(8,128)(2,1)S(1)}, bf16[256,512]{1,0:T(8,128)(2,1)S(1)}, u32[]{:S(2)}, u32[]{:S(2)}) %collective-permute-start.28) | collective-permute-done | bytes 262176 | tf_op jit(solution)/shard_map/ppermute | solution.py:402
  245.3 3.3 %collective-permute-start.34 = (bf16[256,512]{1,0:T(8,128)(2,1)S(1)}, bf16[256,512]{1,0:T(8,128)(2,1)S(1)}, u32[]{:S(2)}, u32[]{:S(2)}) collective-permute-start(bf16[256,512]{1,0:T(8,128)(2,1)S(1)} %get-tuple-element.67), channel_id=1, source_target_pairs={{0,16},{8,24},{16,0},{24,8},{1,17},{9,25},{17,1},{25,9},{2,18},{10... | collective-permute-start | bytes 786440 | tf_op jit(solution)/shard_map/ppermute | solution.py:402
  250.4 10.7 %collective-permute-done.31.refs_6_ = bf16[256,512]{1,0:T(8,128)(2,1)S(1)} collective-permute-done((bf16[256,512]{1,0:T(8,128)(2,1)S(1)}, bf16[256,512]{1,0:T(8,128)(2,1)S(1)}, u32[]{:S(2)}, u32[]{:S(2)}) %collective-permute-start.31) | collective-permute-done | bytes 262176 | tf_op jit(solution)/shard_map/ppermute | solution.py:402
  262.3 16.2 %collective-permute-start.38 = (bf16[256,512]{1,0:T(8,128)(2,1)S(1)}, bf16[256,512]{1,0:T(8,128)(2,1)S(1)}, u32[]{:S(2)}, u32[]{:S(2)}) collective-permute-start(bf16[256,512]{1,0:T(8,128)(2,1)S(1)} %get-tuple-element.72), channel_id=1, source_target_pairs={{0,8},{8,16},{16,24},{24,0},{1,9},{9,17},{17,25},{25,1},{2,10},{10... | collective-permute-start | bytes 786440 | tf_op jit(solution)/shard_map/ppermute | solution.py:402
  278.5 5.1 %collective-permute-done.34.refs_10_ = bf16[256,512]{1,0:T(8,128)(2,1)S(1)} collective-permute-done((bf16[256,512]{1,0:T(8,128)(2,1)S(1)}, bf16[256,512]{1,0:T(8,128)(2,1)S(1)}, u32[]{:S(2)}, u32[]{:S(2)}) %collective-permute-start.34) | collective-permute-done | bytes 262176 | tf_op jit(solution)/shard_map/ppermute | solution.py:402
  283.5 7.4 %collective-permute-done.37.refs_14_ = bf16[256,512]{1,0:T(8,128)(2,1)S(1)} collective-permute-done((bf16[256,512]{1,0:T(8,128)(2,1)S(1)}, bf16[256,512]{1,0:T(8,128)(2,1)S(1)}, u32[]{:S(2)}, u32[]{:S(2)}) %collective-permute-start.37) | collective-permute-done | bytes 262176 | tf_op jit(solution)/shard_map/ppermute | solution.py:402
  291.0 3.9 %assemble.1 = bf16[256,16,512]{2,1,0:T(8,128)(2,1)} custom-call(s32[2]{0:T(128)S(1)} %get-tuple-element.39.pos_ref.place_ref, bf16[256,512]{1,0:T(8,128)(2,1)S(1)} %get-tuple-element.57.refs_0_, bf16[256,512]{1,0:T(8,128)(2,1)S(1)} %collective-permute-done.27.refs_1_, bf16[256,512]{1,0:T(8,128)(2,1)S(1)} %collective-permute-done.28.refs_2_, ...), custom_call_target="tpu_custom_call" | custom-call | flops 1073741824 | bytes 8388608 | tf_op jit(solution)/shard_map/assemble/pallas_call | solution.py:376
  (82 shorter events, 53.2 us)
Async XLA Ops:
  10.0 23.8 %collective-permute-start = (bf16[256,512]{1,0:T(8,128)(2,1)S(1)}, bf16[256,512]{1,0:T(8,128)(2,1)S(1)}, u32[]{:S(2)}, u32[]{:S(2)}) collective-permute-start(bf16[256,512]{1,0:T(8,128)(2,1)S(1)} %transform.8), channel_id=1, source_target_pairs={{0,8},{8,16},{16,24},{24,0},{1,9},{9,17},{17,25},{25,1},{2,10},{10... | collective-permute-start | bytes 786440 | tf_op jit(solution)/shard_map/ppermute | solution.py:402
  15.6 18.1 %collective-permute-start.1 = (bf16[256,512]{1,0:T(8,128)(2,1)S(1)}, bf16[256,512]{1,0:T(8,128)(2,1)S(1)}, u32[]{:S(2)}, u32[]{:S(2)}) collective-permute-start(bf16[256,512]{1,0:T(8,128)(2,1)S(1)} %transform.9), channel_id=1, source_target_pairs={{0,16},{8,24},{16,0},{24,8},{1,17},{9,25},{17,1},{25,9},{2,18},{10... | collective-permute-start | bytes 786440 | tf_op jit(solution)/shard_map/ppermute | solution.py:402
  34.6 24.0 %collective-permute-start.4 = (bf16[1280,512]{1,0:T(8,128)(2,1)S(1)}, bf16[1280,512]{1,0:T(8,128)(2,1)S(1)}, u32[]{:S(2)}, u32[]{:S(2)}) collective-permute-start(bf16[1280,512]{1,0:T(8,128)(2,1)S(1)} %join.6.refs_0_.own_ref), channel_id=1, source_target_pairs={{4,1},{6,3},{0,5},{2,7},{12,9},{14,11},{8,13},{10,15},{20,17},{22,... | collective-permute-start | bytes 3932168 | tf_op jit(solution)/shard_map/ppermute | solution.py:430
  36.5 13.5 %collective-permute-start.5 = (bf16[256,512]{1,0:T(8,128)(2,1)S(1)}, bf16[256,512]{1,0:T(8,128)(2,1)S(1)}, u32[]{:S(2)}, u32[]{:S(2)}) collective-permute-start(bf16[256,512]{1,0:T(8,128)(2,1)S(1)} %get-tuple-element.44), channel_id=1, source_target_pairs={{0,8},{8,16},{16,24},{24,0},{1,9},{9,17},{17,25},{25,1},{2,10},{10... | collective-permute-start | bytes 786440 | tf_op jit(solution)/shard_map/ppermute | solution.py:402
  42.7 15.9 %collective-permute-start.6 = (bf16[256,512]{1,0:T(8,128)(2,1)S(1)}, bf16[256,512]{1,0:T(8,128)(2,1)S(1)}, u32[]{:S(2)}, u32[]{:S(2)}) collective-permute-start(bf16[256,512]{1,0:T(8,128)(2,1)S(1)} %get-tuple-element.45), channel_id=1, source_target_pairs={{0,16},{8,24},{16,0},{24,8},{1,17},{9,25},{17,1},{25,9},{2,18},{10... | collective-permute-start | bytes 786440 | tf_op jit(solution)/shard_map/ppermute | solution.py:402
  43.2 30.2 %collective-permute-start.3 = (bf16[1280,512]{1,0:T(8,128)(2,1)S(1)}, bf16[1280,512]{1,0:T(8,128)(2,1)S(1)}, u32[]{:S(2)}, u32[]{:S(2)}) collective-permute-start(bf16[1280,512]{1,0:T(8,128)(2,1)S(1)} %join.6.refs_0_.own_ref), channel_id=1, source_target_pairs={{1,7},{2,0},{3,1},{5,3},{6,4},{7,5},{9,15},{10,8},{11,9},{13,11},{... | collective-permute-start | bytes 3932168 | tf_op jit(solution)/shard_map/ppermute | solution.py:429
  59.2 14.2 %collective-permute-start.7 = (bf16[1280,512]{1,0:T(8,128)(2,1)S(1)}, bf16[1280,512]{1,0:T(8,128)(2,1)S(1)}, u32[]{:S(2)}, u32[]{:S(2)}) collective-permute-start(bf16[1280,512]{1,0:T(8,128)(2,1)S(1)} %join.7), channel_id=1, source_target_pairs={{5,6},{1,2},{13,14},{9,10},{21,22},{17,18},{29,30},{25,26}} | collective-permute-start | bytes 3932168 | tf_op jit(solution)/shard_map/ppermute | solution.py:438
  74.0 38.1 %collective-permute-start.12 = (bf16[1024,512]{1,0:T(8,128)(2,1)S(1)}, bf16[1024,512]{1,0:T(8,128)(2,1)S(1)}, u32[]{:S(2)}, u32[]{:S(2)}) collective-permute-start(bf16[1024,512]{1,0:T(8,128)(2,1)S(1)} %join.8.refs_0_.own_ref), channel_id=1, source_target_pairs={{1,7},{2,0},{3,1},{5,3},{6,4},{7,5},{9,15},{10,8},{11,9},{13,11},{... | collective-permute-start | bytes 3145736 | tf_op jit(solution)/shard_map/ppermute | solution.py:429
  75.3 36.8 %collective-permute-start.13 = (bf16[1024,512]{1,0:T(8,128)(2,1)S(1)}, bf16[1024,512]{1,0:T(8,128)(2,1)S(1)}, u32[]{:S(2)}, u32[]{:S(2)}) collective-permute-start(bf16[1024,512]{1,0:T(8,128)(2,1)S(1)} %join.8.refs_0_.own_ref), channel_id=1, source_target_pairs={{4,1},{6,3},{0,5},{2,7},{12,9},{14,11},{8,13},{10,15},{20,17},{22,... | collective-permute-start | bytes 3145736 | tf_op jit(solution)/shard_map/ppermute | solution.py:430
  90.6 15.7 %collective-permute-start.8 = (bf16[256,512]{1,0:T(8,128)(2,1)S(1)}, bf16[256,512]{1,0:T(8,128)(2,1)S(1)}, u32[]{:S(2)}, u32[]{:S(2)}) collective-permute-start(bf16[256,512]{1,0:T(8,128)(2,1)S(1)} %get-tuple-element.46), channel_id=1, source_target_pairs={{0,8},{8,16},{16,24},{24,0},{1,9},{9,17},{17,25},{25,1},{2,10},{10... | collective-permute-start | bytes 786440 | tf_op jit(solution)/shard_map/ppermute | solution.py:402
  95.1 17.0 %collective-permute-start.9 = (bf16[256,512]{1,0:T(8,128)(2,1)S(1)}, bf16[256,512]{1,0:T(8,128)(2,1)S(1)}, u32[]{:S(2)}, u32[]{:S(2)}) collective-permute-start(bf16[256,512]{1,0:T(8,128)(2,1)S(1)} %get-tuple-element.47), channel_id=1, source_target_pairs={{0,16},{8,24},{16,0},{24,8},{1,17},{9,25},{17,1},{25,9},{2,18},{10... | collective-permute-start | bytes 786440 | tf_op jit(solution)/shard_map/ppermute | solution.py:402
  95.9 16.2 %collective-permute-start.10 = (bf16[256,512]{1,0:T(8,128)(2,1)S(1)}, bf16[256,512]{1,0:T(8,128)(2,1)S(1)}, u32[]{:S(2)}, u32[]{:S(2)}) collective-permute-start(bf16[256,512]{1,0:T(8,128)(2,1)S(1)} %get-tuple-element.48), channel_id=1, source_target_pairs={{0,24},{8,0},{16,8},{24,16},{1,25},{9,1},{17,9},{25,17},{2,26},{10... | collective-permute-start | bytes 786440 | tf_op jit(solution)/shard_map/ppermute | solution.py:402
  112.8 27.7 %collective-permute-start.14 = (bf16[1024,512]{1,0:T(8,128)(2,1)S(1)}, bf16[1024,512]{1,0:T(8,128)(2,1)S(1)}, u32[]{:S(2)}, u32[]{:S(2)}) collective-permute-start(bf16[1024,512]{1,0:T(8,128)(2,1)S(1)} %get-tuple-element.52), channel_id=1, source_target_pairs={{4,1},{6,3},{0,5},{2,7},{5,6},{1,2},{12,9},{14,11},{8,13},{10,15},... | collective-permute-start | bytes 3145736 | tf_op jit(solution)/shard_map/ppermute | solution.py:430
  121.3 19.1 %collective-permute-start.16 = (bf16[256,512]{1,0:T(8,128)(2,1)S(1)}, bf16[256,512]{1,0:T(8,128)(2,1)S(1)}, u32[]{:S(2)}, u32[]{:S(2)}) collective-permute-start(bf16[256,512]{1,0:T(8,128)(2,1)S(1)} %get-tuple-element.54), channel_id=1, source_target_pairs={{0,16},{8,24},{16,0},{24,8},{1,17},{9,25},{17,1},{25,9},{2,18},{10... | collective-permute-start | bytes 786440 | tf_op jit(solution)/shard_map/ppermute | solution.py:402
  122.7 28.4 %collective-permute-start.18 = (bf16[1024,512]{1,0:T(8,128)(2,1)S(1)}, bf16[1024,512]{1,0:T(8,128)(2,1)S(1)}, u32[]{:S(2)}, u32[]{:S(2)}) collective-permute-start(bf16[1024,512]{1,0:T(8,128)(2,1)S(1)} %get-tuple-element.56.own_ref), channel_id=1, source_target_pairs={{1,7},{2,0},{3,1},{5,3},{6,4},{7,5},{9,15},{10,8},{11,9},{13,11},{... | collective-permute-start | bytes 3145736 | tf_op jit(solution)/shard_map/ppermute | solution.py:429
  151.6 15.0 %collective-permute-start.21 = (bf16[768,512]{1,0:T(8,128)(2,1)S(1)}, bf16[768,512]{1,0:T(8,128)(2,1)S(1)}, u32[]{:S(2)}, u32[]{:S(2)}) collective-permute-start(bf16[768,512]{1,0:T(8,128)(2,1)S(1)} %join.11.own_ref), channel_id=1, source_target_pairs={{4,1},{6,3},{0,5},{2,7},{12,9},{14,11},{8,13},{10,15},{20,17},{22,... | collective-permute-start | bytes 2359304 | tf_op jit(solution)/shard_map/ppermute | solution.py:430
  158.2 30.9 %collective-permute-start.23 = (bf16[2,1280,512]{2,1,0:T(8,128)(2,1)S(1)}, bf16[2,1280,512]{2,1,0:T(8,128)(2,1)S(1)}, u32[]{:S(2)}, u32[]{:S(2)}) collective-permute-start(bf16[2,1280,512]{2,1,0:T(8,128)(2,1)S(1)} %pick.4.refs_6_), channel_id=1, source_target_pairs={{0,1},{1,0},{2,3},{3,2},{4,5},{5,4},{6,7},{7,6},{8,9},{9,8},{10,11... | collective-permute-start | bytes 7864328 | tf_op jit(solution)/shard_map/ppermute | solution.py:445
  158.2 22.4 %collective-permute-start.20 = (bf16[768,512]{1,0:T(8,128)(2,1)S(1)}, bf16[768,512]{1,0:T(8,128)(2,1)S(1)}, u32[]{:S(2)}, u32[]{:S(2)}) collective-permute-start(bf16[768,512]{1,0:T(8,128)(2,1)S(1)} %join.11.own_ref), channel_id=1, source_target_pairs={{1,7},{2,0},{3,1},{5,3},{6,4},{7,5},{9,15},{10,8},{11,9},{13,11},{... | collective-permute-start | bytes 2359304 | tf_op jit(solution)/shard_map/ppermute | solution.py:429
  166.6 14.0 %collective-permute-start.22 = (bf16[768,512]{1,0:T(8,128)(2,1)S(1)}, bf16[768,512]{1,0:T(8,128)(2,1)S(1)}, u32[]{:S(2)}, u32[]{:S(2)}) collective-permute-start(bf16[768,512]{1,0:T(8,128)(2,1)S(1)} %collective-permute-done.21.refs_17_), channel_id=1, source_target_pairs={{5,6},{1,2},{13,14},{9,10},{21,22},{17,18},{29,30},{25,26}} | collective-permute-start | bytes 2359304 | tf_op jit(solution)/shard_map/ppermute | solution.py:438
  168.2 20.8 %collective-permute-start.24 = (bf16[2,1024,512]{2,1,0:T(8,128)(2,1)S(1)}, bf16[2,1024,512]{2,1,0:T(8,128)(2,1)S(1)}, u32[]{:S(2)}, u32[]{:S(2)}) collective-permute-start(bf16[2,1024,512]{2,1,0:T(8,128)(2,1)S(1)} %pick.5.refs_7_), channel_id=1, source_target_pairs={{0,1},{1,0},{2,3},{3,2},{4,5},{5,4},{6,7},{7,6},{8,9},{9,8},{10,11... | collective-permute-start | bytes 6291464 | tf_op jit(solution)/shard_map/ppermute | solution.py:445
  194.4 18.2 %collective-permute-start.27 = (bf16[256,512]{1,0:T(8,128)(2,1)S(1)}, bf16[256,512]{1,0:T(8,128)(2,1)S(1)}, u32[]{:S(2)}, u32[]{:S(2)}) collective-permute-start(bf16[256,512]{1,0:T(8,128)(2,1)S(1)} %get-tuple-element.58), channel_id=1, source_target_pairs={{0,24},{8,0},{16,8},{24,16},{1,25},{9,1},{17,9},{25,17},{2,26},{10... | collective-permute-start | bytes 786440 | tf_op jit(solution)/shard_map/ppermute | solution.py:402
  198.7 45.5 %collective-permute-start.28 = (bf16[256,512]{1,0:T(8,128)(2,1)S(1)}, bf16[256,512]{1,0:T(8,128)(2,1)S(1)}, u32[]{:S(2)}, u32[]{:S(2)}) collective-permute-start(bf16[256,512]{1,0:T(8,128)(2,1)S(1)} %get-tuple-element.59), channel_id=1, source_target_pairs={{0,16},{8,24},{16,0},{24,8},{1,17},{9,25},{17,1},{25,9},{2,18},{10... | collective-permute-start | bytes 786440 | tf_op jit(solution)/shard_map/ppermute | solution.py:402
  204.7 40.6 %collective-permute-start.29 = (bf16[256,512]{1,0:T(8,128)(2,1)S(1)}, bf16[256,512]{1,0:T(8,128)(2,1)S(1)}, u32[]{:S(2)}, u32[]{:S(2)}) collective-permute-start(bf16[256,512]{1,0:T(8,128)(2,1)S(1)} %get-tuple-element.60), channel_id=1, source_target_pairs={{0,8},{8,16},{16,24},{24,0},{1,9},{9,17},{17,25},{25,1},{2,10},{10... | collective-permute-start | bytes 786440 | tf_op jit(solution)/shard_map/ppermute | solution.py:402
  207.7 40.9 %collective-permute-start.30 = (bf16[256,512]{1,0:T(8,128)(2,1)S(1)}, bf16[256,512]{1,0:T(8,128)(2,1)S(1)}, u32[]{:S(2)}, u32[]{:S(2)}) collective-permute-start(bf16[256,512]{1,0:T(8,128)(2,1)S(1)} %get-tuple-element.62), channel_id=1, source_target_pairs={{0,24},{8,0},{16,8},{24,16},{1,25},{9,1},{17,9},{25,17},{2,26},{10... | collective-permute-start | bytes 786440 | tf_op jit(solution)/shard_map/ppermute | solution.py:402
  209.7 51.4 %collective-permute-start.31 = (bf16[256,512]{1,0:T(8,128)(2,1)S(1)}, bf16[256,512]{1,0:T(8,128)(2,1)S(1)}, u32[]{:S(2)}, u32[]{:S(2)}) collective-permute-start(bf16[256,512]{1,0:T(8,128)(2,1)S(1)} %get-tuple-element.63), channel_id=1, source_target_pairs={{0,16},{8,24},{16,0},{24,8},{1,17},{9,25},{17,1},{25,9},{2,18},{10... | collective-permute-start | bytes 786440 | tf_op jit(solution)/shard_map/ppermute | solution.py:402
  212.7 48.4 %collective-permute-start.32 = (bf16[256,512]{1,0:T(8,128)(2,1)S(1)}, bf16[256,512]{1,0:T(8,128)(2,1)S(1)}, u32[]{:S(2)}, u32[]{:S(2)}) collective-permute-start(bf16[256,512]{1,0:T(8,128)(2,1)S(1)} %get-tuple-element.64), channel_id=1, source_target_pairs={{0,8},{8,16},{16,24},{24,0},{1,9},{9,17},{17,25},{25,1},{2,10},{10... | collective-permute-start | bytes 786440 | tf_op jit(solution)/shard_map/ppermute | solution.py:402
  244.2 18.1 %collective-permute-start.33 = (bf16[256,512]{1,0:T(8,128)(2,1)S(1)}, bf16[256,512]{1,0:T(8,128)(2,1)S(1)}, u32[]{:S(2)}, u32[]{:S(2)}) collective-permute-start(bf16[256,512]{1,0:T(8,128)(2,1)S(1)} %get-tuple-element.66), channel_id=1, source_target_pairs={{0,24},{8,0},{16,8},{24,16},{1,25},{9,1},{17,9},{25,17},{2,26},{10... | collective-permute-start | bytes 786440 | tf_op jit(solution)/shard_map/ppermute | solution.py:402
  245.3 38.2 %collective-permute-start.34 = (bf16[256,512]{1,0:T(8,128)(2,1)S(1)}, bf16[256,512]{1,0:T(8,128)(2,1)S(1)}, u32[]{:S(2)}, u32[]{:S(2)}) collective-permute-start(bf16[256,512]{1,0:T(8,128)(2,1)S(1)} %get-tuple-element.67), channel_id=1, source_target_pairs={{0,16},{8,24},{16,0},{24,8},{1,17},{9,25},{17,1},{25,9},{2,18},{10... | collective-permute-start | bytes 786440 | tf_op jit(solution)/shard_map/ppermute | solution.py:402
  248.6 34.9 %collective-permute-start.35 = (bf16[256,512]{1,0:T(8,128)(2,1)S(1)}, bf16[256,512]{1,0:T(8,128)(2,1)S(1)}, u32[]{:S(2)}, u32[]{:S(2)}) collective-permute-start(bf16[256,512]{1,0:T(8,128)(2,1)S(1)} %get-tuple-element.68), channel_id=1, source_target_pairs={{0,8},{8,16},{16,24},{24,0},{1,9},{9,17},{17,25},{25,1},{2,10},{10... | collective-permute-start | bytes 786440 | tf_op jit(solution)/shard_map/ppermute | solution.py:402
  261.1 22.5 %collective-permute-start.36 = (bf16[256,512]{1,0:T(8,128)(2,1)S(1)}, bf16[256,512]{1,0:T(8,128)(2,1)S(1)}, u32[]{:S(2)}, u32[]{:S(2)}) collective-permute-start(bf16[256,512]{1,0:T(8,128)(2,1)S(1)} %get-tuple-element.70), channel_id=1, source_target_pairs={{0,24},{8,0},{16,8},{24,16},{1,25},{9,1},{17,9},{25,17},{2,26},{10... | collective-permute-start | bytes 786440 | tf_op jit(solution)/shard_map/ppermute | solution.py:402
  261.1 29.9 %collective-permute-start.37 = (bf16[256,512]{1,0:T(8,128)(2,1)S(1)}, bf16[256,512]{1,0:T(8,128)(2,1)S(1)}, u32[]{:S(2)}, u32[]{:S(2)}) collective-permute-start(bf16[256,512]{1,0:T(8,128)(2,1)S(1)} %get-tuple-element.71), channel_id=1, source_target_pairs={{0,16},{8,24},{16,0},{24,8},{1,17},{9,25},{17,1},{25,9},{2,18},{10... | collective-permute-start | bytes 786440 | tf_op jit(solution)/shard_map/ppermute | solution.py:402
  262.3 28.6 %collective-permute-start.38 = (bf16[256,512]{1,0:T(8,128)(2,1)S(1)}, bf16[256,512]{1,0:T(8,128)(2,1)S(1)}, u32[]{:S(2)}, u32[]{:S(2)}) collective-permute-start(bf16[256,512]{1,0:T(8,128)(2,1)S(1)} %get-tuple-element.72), channel_id=1, source_target_pairs={{0,8},{8,16},{16,24},{24,0},{1,9},{9,17},{17,25},{25,1},{2,10},{10... | collective-permute-start | bytes 786440 | tf_op jit(solution)/shard_map/ppermute | solution.py:402
  (13 other events, 139.0 us)

commit v2 on v1

--- a/solution.py
+++ b/solution.py
@@ -137,20 +137,23 @@
 
     @pl.when(place_ref[1] % 2 == 0)
     def _():
-        onward[...] = out[...]
+        onward[: count * rows, :] = out[...]
+        if onward.shape[0] > count * rows:
+            onward[count * rows :, :] = refs[count][count * rows : onward.shape[0], :]
 
     @pl.when(place_ref[1] % 2 == 1)
     def _():
-        onward[...] = refs[count][...]
-
-
-def stacked(pieces, place, held, after):
+        onward[...] = refs[count][: onward.shape[0], :]
+
+
+def stacked(pieces, place, held, after, onward_rows=0):
     rows, virs = pieces[0].shape
     count = len(pieces)
     whole = pl.BlockSpec((count * rows, virs), lambda: (0, 0))
     shape = jax.ShapeDtypeStruct((count * rows, virs), pieces[0].dtype)
     kernel = join_pass_kernel if held else join_kernel
     outs = 1 + len(held)
+    wide = [pl.BlockSpec((onward_rows, virs), lambda: (0, 0))] * len(held)
 
     def entry(place_ref, *refs):
         kernel(count, place_ref, *refs[: count + len(held)], *refs[-outs:])
@@ -159,10 +162,10 @@
         entry,
         in_specs=[pl.BlockSpec(memory_space=pltpu.SMEM)]
         + [pl.BlockSpec((rows, virs), lambda: (0, 0))] * count
-        + [whole] * len(held)
+        + [pl.BlockSpec(value.shape, lambda: (0, 0)) for value in held]
         + [pl.BlockSpec(memory_space=pl.ANY)] * len(after),
-        out_specs=[whole] * outs,
-        out_shape=[shape] * outs,
+        out_specs=[whole] + wide,
+        out_shape=[shape] + [jax.ShapeDtypeStruct((onward_rows, virs), pieces[0].dtype)] * len(held),
         compiler_params=pltpu.CompilerParams(vmem_limit_bytes=20 * MIB),
         cost_estimate=pl.CostEstimate(flops=0, bytes_accessed=4 * count * rows * virs * outs, transcendentals=0),
         name="join",
@@ -423,9 +426,10 @@
         if chunk < OCC_DEV:
             parts.append(pieces)
             message = pieces[0 if chunk == 0 else 1 :] + coming[:1]
-            rides = bool(last) and 1 < chunk < OCC_DEV - 1
-            ready = nears[-1:] + ([] if rides else thirds[-1:] + lates[-1:])
-            own, *onward = stacked(message, place, thirds[-1:] if rides else [], ready)
+            rides = bool(last) and 0 < chunk < OCC_DEV - 1
+            ready = nears[-1:] + ([] if rides else thirds[-1:])
+            onward_rows = max(sum(piece.shape[0] for piece in message), owns[-1].shape[0]) if rides else 0
+            own, *onward = stacked(message, place, thirds[-1:] if rides else [], ready, onward_rows)
             near = lax.ppermute(own, "occ", direct)
             third = lax.ppermute(onward[0], "occ", far + last) if rides else lax.ppermute(own, "occ", far)
             owns.append(own)
@@ -433,9 +437,8 @@
             thirds.append(third)
             if rides:
                 lates.append(third)
-            if last and chunk != 1:
-                onward = stacked([third], place, [], coming[1:3])[0] if coming else third
-                lates.append(lax.ppermute(onward, "occ", last))
+            if last and chunk >= OCC_DEV - 2:
+                lates.append(lax.ppermute(third, "occ", last))
             if not last:
                 lates.append(near)
         if chunk >= 1:

time: 296 us -> 277 us (0.936)
  starting transfers between devices: 129 us -> 94.9 us
  Pallas kernels: 64 us -> 85.8 us
  waiting for transfers between devices: 100 us -> 93.7 us
    ppermute x24, waiting for transfers between devices: 89.7 us -> 61.9 us  [along_aux(): lax.ppermute(value, 'aux', [(z, (z + steps) % aux_count) for z in range(a...]
    ppermute x4, waiting for transfers between devices: 1.11 us -> 25.3 us  [body(): near = lax.ppermute(own, 'occ', direct)]
    pallas_call x4, Pallas kernels: 8.35 us -> 31.2 us  [densities(): pl.pallas_call(functools.partial(pair_kernel, chunk, count, occ_count), i...]
    ppermute x3 -> x2, starting transfers between devices: 22.8 us -> 5.56 us  [body(): lax.ppermute(own, 'occ', far)]
    ppermute x24, starting transfers between devices: 77.3 us -> 67 us  [along_aux(): lax.ppermute(value, 'aux', [(z, (z + steps) % aux_count) for z in range(a...]
    ppermute x4, starting transfers between devices: 18.5 us -> 12.2 us  [body(): swaps.append(lax.ppermute(both, 'occ', twin))]
    ppermute x3 -> x2, waiting for transfers between devices: 7.11 us -> 4.15 us  [body(): lax.ppermute(own, 'occ', far)]
  transfers between devices with their start and end apart: 39 -> 38, of which waited for: 14 -> 17; matrix products, arithmetic and copies ran while one was open for 0% -> 0% of each run, Pallas kernels for 15% -> 24%
where the time goes in v2:
time: 277 us; the launch traced here: 276 us
  starting transfers between devices  94.9 us (34%)
  waiting for transfers between devices  93.7 us (34%)
  Pallas kernels  85.8 us (31%)
    ppermute x24, starting transfers between devices, along_aux(): lax.ppermute(value, 'aux', [(z, (z + steps) % aux_count) for z in range(a...  67 us
    ppermute x24, waiting for transfers between devices, along_aux(): lax.ppermute(value, 'aux', [(z, (z + steps) % aux_count) for z in range(a...  61.9 us
    pallas_call x7, Pallas kernels, transformed(): pl.pallas_call(functools.partial(transform_kernel, count, orbitals, orbit...  36.8 us
    pallas_call x4, Pallas kernels, densities(): pl.pallas_call(functools.partial(pair_kernel, chunk, count, occ_count), i...  31.2 us
    ppermute x4, waiting for transfers between devices, body(): near = lax.ppermute(own, 'occ', direct)  25.3 us
    ppermute x4, starting transfers between devices, body(): swaps.append(lax.ppermute(both, 'occ', twin))  12.2 us
    pallas_call x1, Pallas kernels, sorted_rows(): pl.pallas_call(sort_kernel, grid=(rows // block,), in_specs=[smem, smem,...  6.67 us
    ppermute x2, starting transfers between devices, body(): lax.ppermute(own, 'occ', far)  5.56 us
  transfers between devices with their start and end apart: 38, of which 17 were waited for; matrix products, arithmetic and copies ran while one was open for 0% of the time, Pallas kernels for 24%

profile of v2, /device:TPU:0, one launch (start us, length us, event | category | flops | bytes accessed | tf_op | source)
XLA Modules:
  0.0 276.1 jit_solution(16497379664079641249)
XLA Ops:
  0.7 6.7 %sort_rows.1 = (bf16[16,256,1024]{2,1,0:T(8,128)(2,1)S(1)}, s32[2]{0:T(128)S(1)}) custom-call(s32[4,16]{1,0:T(4,128)S(1)} %copy-done.5, s32[1]{0:T(128)} %bitcast.aux_ref, s32[1]{0:T(128)} %bitcast.1.occ_ref, bf16[256,16,1024]{2,1,0:T(8,128)(2,1)} %x_ref.1), custom_call_target="tpu_custom_call" | custom-call | flops 2147483648 | bytes 16777216 | tf_op jit(solution)/shard_map/sort_rows/pallas_call | solution.py:44
  10.0 5.1 %collective-permute-start.2 = (bf16[256,512]{1,0:T(8,128)(2,1)S(1)}, bf16[256,512]{1,0:T(8,128)(2,1)S(1)}, u32[]{:S(2)}, u32[]{:S(2)}) collective-permute-start(bf16[256,512]{1,0:T(8,128)(2,1)S(1)} %transform.10), channel_id=1, source_target_pairs={{0,24},{8,0},{16,8},{24,16},{1,25},{9,1},{17,9},{25,17},{2,26},{10... | collective-permute-start | bytes 786440 | tf_op jit(solution)/shard_map/ppermute | solution.py:405
  23.9 8.9 %transform.11 = (bf16[256,512]{1,0:T(8,128)(2,1)S(1)}, bf16[256,512]{1,0:T(8,128)(2,1)S(1)}, bf16[256,512]{1,0:T(8,128)(2,1)S(1)}, bf16[256,512]{1,0:T(8,128)(2,1)S(1)}) custom-call(s32[2]{0:T(128)S(1)} %get-tuple-element.41.pos_ref.place_ref, bf16[16,256,1024]{2,1,0:T(8,128)(2,1)S(1)} %get-tuple-element.42.x_ref, s32[128,512]{1,0:T(8,128)S(1)} %copy-done.1, ...), custom_call_target="tpu_custom_call" | custom-call | flops 6442450944 | bytes 7340032 | tf_op jit(solution)/shard_map/transform/pallas_call | solution.py:101
  32.8 4.6 %collective-permute-done.1.refs_2_ = bf16[256,512]{1,0:T(8,128)(2,1)S(1)} collective-permute-done((bf16[256,512]{1,0:T(8,128)(2,1)S(1)}, bf16[256,512]{1,0:T(8,128)(2,1)S(1)}, u32[]{:S(2)}, u32[]{:S(2)}) %collective-permute-start.1) | collective-permute-done | bytes 262176 | tf_op jit(solution)/shard_map/ppermute | solution.py:405
  39.4 4.2 %collective-permute-start.7 = (bf16[1280,512]{1,0:T(8,128)(2,1)S(1)}, bf16[1280,512]{1,0:T(8,128)(2,1)S(1)}, u32[]{:S(2)}, u32[]{:S(2)}) collective-permute-start(bf16[1280,512]{1,0:T(8,128)(2,1)S(1)} %join.4.refs_0_.own_ref), channel_id=1, source_target_pairs={{4,1},{6,3},{0,5},{2,7},{12,9},{14,11},{8,13},{10,15},{20,17},{22,... | collective-permute-start | bytes 3932168 | tf_op jit(solution)/shard_map/ppermute | solution.py:434
  51.8 8.9 %transform.12 = (bf16[256,512]{1,0:T(8,128)(2,1)S(1)}, bf16[256,512]{1,0:T(8,128)(2,1)S(1)}, bf16[256,512]{1,0:T(8,128)(2,1)S(1)}, bf16[256,512]{1,0:T(8,128)(2,1)S(1)}) custom-call(s32[2]{0:T(128)S(1)} %get-tuple-element.41.pos_ref.place_ref, bf16[16,256,1024]{2,1,0:T(8,128)(2,1)S(1)} %get-tuple-element.42.x_ref, s32[128,512]{1,0:T(8,128)S(1)} %copy-done.1, ...), custom_call_target="tpu_custom_call" | custom-call | flops 6442450944 | bytes 7340032 | tf_op jit(solution)/shard_map/transform/pallas_call | solution.py:101
  60.6 3.6 %collective-permute-done.5.refs_1_.refs_2_ = bf16[256,512]{1,0:T(8,128)(2,1)S(1)} collective-permute-done((bf16[256,512]{1,0:T(8,128)(2,1)S(1)}, bf16[256,512]{1,0:T(8,128)(2,1)S(1)}, u32[]{:S(2)}, u32[]{:S(2)}) %collective-permute-start.5) | collective-permute-done | bytes 262176 | tf_op jit(solution)/shard_map/ppermute | solution.py:405
  64.2 5.8 %collective-permute-done.3.refs_5_.near_ref = bf16[1280,512]{1,0:T(8,128)(2,1)S(1)} collective-permute-done((bf16[1280,512]{1,0:T(8,128)(2,1)S(1)}, bf16[1280,512]{1,0:T(8,128)(2,1)S(1)}, u32[]{:S(2)}, u32[]{:S(2)}) %collective-permute-start.3) | collective-permute-done | bytes 1310752 | tf_op jit(solution)/shard_map/ppermute | solution.py:433
  73.6 5.0 %collective-permute-start.10 = (bf16[256,512]{1,0:T(8,128)(2,1)S(1)}, bf16[256,512]{1,0:T(8,128)(2,1)S(1)}, u32[]{:S(2)}, u32[]{:S(2)}) collective-permute-start(bf16[256,512]{1,0:T(8,128)(2,1)S(1)} %get-tuple-element.52), channel_id=1, source_target_pairs={{0,16},{8,24},{16,0},{24,8},{1,17},{9,25},{17,1},{25,9},{2,18},{10... | collective-permute-start | bytes 786440 | tf_op jit(solution)/shard_map/ppermute | solution.py:405
  80.5 8.8 %transform.13 = (bf16[256,512]{1,0:T(8,128)(2,1)S(1)}, bf16[256,512]{1,0:T(8,128)(2,1)S(1)}, bf16[256,512]{1,0:T(8,128)(2,1)S(1)}, bf16[256,512]{1,0:T(8,128)(2,1)S(1)}) custom-call(s32[2]{0:T(128)S(1)} %get-tuple-element.41.pos_ref.place_ref, bf16[16,256,1024]{2,1,0:T(8,128)(2,1)S(1)} %get-tuple-element.42.x_ref, s32[128,512]{1,0:T(8,128)S(1)} %copy-done.1, ...), custom_call_target="tpu_custom_call" | custom-call | flops 6442450944 | bytes 7340032 | tf_op jit(solution)/shard_map/transform/pallas_call | solution.py:101
  91.8 4.1 %collective-permute-done.9.refs_0_.refs_1_ = bf16[256,512]{1,0:T(8,128)(2,1)S(1)} collective-permute-done((bf16[256,512]{1,0:T(8,128)(2,1)S(1)}, bf16[256,512]{1,0:T(8,128)(2,1)S(1)}, u32[]{:S(2)}, u32[]{:S(2)}) %collective-permute-start.9) | collective-permute-done | bytes 262176 | tf_op jit(solution)/shard_map/ppermute | solution.py:405
  96.0 5.1 %collective-permute-done.12.refs_3_.refs_5_.near_ref = bf16[1024,512]{1,0:T(8,128)(2,1)S(1)} collective-permute-done((bf16[1024,512]{1,0:T(8,128)(2,1)S(1)}, bf16[1024,512]{1,0:T(8,128)(2,1)S(1)}, u32[]{:S(2)}, u32[]{:S(2)}) %collective-permute-start.12) | collective-permute-done | bytes 1048608 | tf_op jit(solution)/shard_map/ppermute | solution.py:433
  114.9 12.5 %collective-permute-done.15.refs_1_.refs_2_ = bf16[256,512]{1,0:T(8,128)(2,1)S(1)} collective-permute-done((bf16[256,512]{1,0:T(8,128)(2,1)S(1)}, bf16[256,512]{1,0:T(8,128)(2,1)S(1)}, u32[]{:S(2)}, u32[]{:S(2)}) %collective-permute-start.15) | collective-permute-done | bytes 262176 | tf_op jit(solution)/shard_map/ppermute | solution.py:405
  127.4 4.6 %collective-permute-done.17.refs_3_.near_ref = bf16[1024,512]{1,0:T(8,128)(2,1)S(1)} collective-permute-done((bf16[1024,512]{1,0:T(8,128)(2,1)S(1)}, bf16[1024,512]{1,0:T(8,128)(2,1)S(1)}, u32[]{:S(2)}, u32[]{:S(2)}) %collective-permute-start.17) | collective-permute-done | bytes 1048608 | tf_op jit(solution)/shard_map/ppermute | solution.py:433
  139.2 4.1 %collective-permute-done.20.refs_17_ = bf16[768,512]{1,0:T(8,128)(2,1)S(1)} collective-permute-done((bf16[768,512]{1,0:T(8,128)(2,1)S(1)}, bf16[768,512]{1,0:T(8,128)(2,1)S(1)}, u32[]{:S(2)}, u32[]{:S(2)}) %collective-permute-start.20) | collective-permute-done | bytes 786464 | tf_op jit(solution)/shard_map/ppermute | solution.py:434
  145.0 3.5 %collective-permute-start.23 = (bf16[2,1024,512]{2,1,0:T(8,128)(2,1)S(1)}, bf16[2,1024,512]{2,1,0:T(8,128)(2,1)S(1)}, u32[]{:S(2)}, u32[]{:S(2)}) collective-permute-start(bf16[2,1024,512]{2,1,0:T(8,128)(2,1)S(1)} %pick.5.refs_7_), channel_id=1, source_target_pairs={{0,1},{1,0},{2,3},{3,2},{4,5},{5,4},{6,7},{7,6},{8,9},{9,8},{10,11... | collective-permute-start | bytes 6291464 | tf_op jit(solution)/shard_map/ppermute | solution.py:448
  149.5 9.8 %collective-permute-done.19.near_ref = bf16[768,512]{1,0:T(8,128)(2,1)S(1)} collective-permute-done((bf16[768,512]{1,0:T(8,128)(2,1)S(1)}, bf16[768,512]{1,0:T(8,128)(2,1)S(1)}, u32[]{:S(2)}, u32[]{:S(2)}) %collective-permute-start.19) | collective-permute-done | bytes 786464 | tf_op jit(solution)/shard_map/ppermute | solution.py:433
  160.1 6.2 %collective-permute-start.25 = (bf16[2,768,512]{2,1,0:T(8,128)(2,1)S(1)}, bf16[2,768,512]{2,1,0:T(8,128)(2,1)S(1)}, u32[]{:S(2)}, u32[]{:S(2)}) collective-permute-start(bf16[2,768,512]{2,1,0:T(8,128)(2,1)S(1)} %pick.7.refs_9_), channel_id=1, source_target_pairs={{0,1},{1,0},{2,3},{3,2},{4,5},{5,4},{6,7},{7,6},{8,9},{9,8},{10,11... | collective-permute-start | bytes 4718600 | tf_op jit(solution)/shard_map/ppermute | solution.py:448
  169.3 4.6 %pairs.7 = (bf16[256,512]{1,0:T(8,128)(2,1)S(1)}, bf16[256,512]{1,0:T(8,128)(2,1)S(1)}, bf16[256,512]{1,0:T(8,128)(2,1)S(1)}, bf16[256,512]{1,0:T(8,128)(2,1)S(1)}) custom-call(s32[1,1]{1,0:T(1,128)S(6)} %copy.9.live_ref, s32[16]{0:T(128)S(1)} %bitcast.4, s32[2]{0:T(128)S(1)} %get-tuple-element.41.pos_ref.place_ref, f32[128]{0:T(128)S(1)} %copy-done.3, ...), custom_call_target="tpu_custom_call" | custom-call | flops 4294967296 | bytes 3145728 | tf_op jit(solution)/shard_map/pairs/pallas_call | solution.py:338
  173.9 4.5 %collective-permute-start.35 = (bf16[256,512]{1,0:T(8,128)(2,1)S(1)}, bf16[256,512]{1,0:T(8,128)(2,1)S(1)}, u32[]{:S(2)}, u32[]{:S(2)}) collective-permute-start(bf16[256,512]{1,0:T(8,128)(2,1)S(1)} %get-tuple-element.74), channel_id=1, source_target_pairs={{0,24},{8,0},{16,8},{24,16},{1,25},{9,1},{17,9},{25,17},{2,26},{10... | collective-permute-start | bytes 786440 | tf_op jit(solution)/shard_map/ppermute | solution.py:405
  178.4 7.6 %collective-permute-start.36 = (bf16[256,512]{1,0:T(8,128)(2,1)S(1)}, bf16[256,512]{1,0:T(8,128)(2,1)S(1)}, u32[]{:S(2)}, u32[]{:S(2)}) collective-permute-start(bf16[256,512]{1,0:T(8,128)(2,1)S(1)} %get-tuple-element.75), channel_id=1, source_target_pairs={{0,16},{8,24},{16,0},{24,8},{1,17},{9,25},{17,1},{25,9},{2,18},{10... | collective-permute-start | bytes 786440 | tf_op jit(solution)/shard_map/ppermute | solution.py:405
  186.0 14.1 %pairs.6 = (bf16[256,512]{1,0:T(8,128)(2,1)S(1)}, bf16[256,512]{1,0:T(8,128)(2,1)S(1)}, bf16[256,512]{1,0:T(8,128)(2,1)S(1)}, bf16[256,512]{1,0:T(8,128)(2,1)S(1)}) custom-call(s32[1,1]{1,0:T(1,128)S(6)} %copy.9.live_ref, s32[16]{0:T(128)S(1)} %bitcast.5, s32[2]{0:T(128)S(1)} %get-tuple-element.41.pos_ref.place_ref, f32[128]{0:T(128)S(1)} %copy-done.3, ...), custom_call_target="tpu_custom_call" | custom-call | flops 4294967296 | bytes 3145728 | tf_op jit(solution)/shard_map/pairs/pallas_call | solution.py:338
  200.2 4.8 %pairs.5 = (bf16[256,512]{1,0:T(8,128)(2,1)S(1)}, bf16[256,512]{1,0:T(8,128)(2,1)S(1)}, bf16[256,512]{1,0:T(8,128)(2,1)S(1)}, bf16[256,512]{1,0:T(8,128)(2,1)S(1)}) custom-call(s32[1,1]{1,0:T(1,128)S(6)} %copy.9.live_ref, s32[16]{0:T(128)S(1)} %bitcast.6, s32[2]{0:T(128)S(1)} %get-tuple-element.41.pos_ref.place_ref, f32[128]{0:T(128)S(1)} %copy-done.3, ...), custom_call_target="tpu_custom_call" | custom-call | flops 4294967296 | bytes 3145728 | tf_op jit(solution)/shard_map/pairs/pallas_call | solution.py:338
  205.0 5.9 %collective-permute-start.34 = (bf16[256,512]{1,0:T(8,128)(2,1)S(1)}, bf16[256,512]{1,0:T(8,128)(2,1)S(1)}, u32[]{:S(2)}, u32[]{:S(2)}) collective-permute-start(bf16[256,512]{1,0:T(8,128)(2,1)S(1)} %get-tuple-element.72), channel_id=1, source_target_pairs={{0,8},{8,16},{16,24},{24,0},{1,9},{9,17},{17,25},{25,1},{2,10},{10... | collective-permute-start | bytes 786440 | tf_op jit(solution)/shard_map/ppermute | solution.py:405
  210.9 8.5 %collective-permute-done.36.refs_14_ = bf16[256,512]{1,0:T(8,128)(2,1)S(1)} collective-permute-done((bf16[256,512]{1,0:T(8,128)(2,1)S(1)}, bf16[256,512]{1,0:T(8,128)(2,1)S(1)}, u32[]{:S(2)}, u32[]{:S(2)}) %collective-permute-start.36) | collective-permute-done | bytes 262176 | tf_op jit(solution)/shard_map/ppermute | solution.py:405
  219.5 7.7 %pairs.4 = (bf16[256,512]{1,0:T(8,128)(2,1)S(1)}, bf16[256,512]{1,0:T(8,128)(2,1)S(1)}, bf16[256,512]{1,0:T(8,128)(2,1)S(1)}, bf16[256,512]{1,0:T(8,128)(2,1)S(1)}) custom-call(s32[1,1]{1,0:T(1,128)S(6)} %copy.9.live_ref, s32[16]{0:T(128)S(1)} %bitcast.7, s32[2]{0:T(128)S(1)} %get-tuple-element.41.pos_ref.place_ref, f32[128]{0:T(128)S(1)} %copy-done.3, ...), custom_call_target="tpu_custom_call" | custom-call | flops 4294967296 | bytes 3145728 | tf_op jit(solution)/shard_map/pairs/pallas_call | solution.py:338
  227.3 3.9 %collective-permute-start.31 = (bf16[256,512]{1,0:T(8,128)(2,1)S(1)}, bf16[256,512]{1,0:T(8,128)(2,1)S(1)}, u32[]{:S(2)}, u32[]{:S(2)}) collective-permute-start(bf16[256,512]{1,0:T(8,128)(2,1)S(1)} %get-tuple-element.68), channel_id=1, source_target_pairs={{0,8},{8,16},{16,24},{24,0},{1,9},{9,17},{17,25},{25,1},{2,10},{10... | collective-permute-start | bytes 786440 | tf_op jit(solution)/shard_map/ppermute | solution.py:405
  231.3 10.7 %collective-permute-done.33.refs_10_ = bf16[256,512]{1,0:T(8,128)(2,1)S(1)} collective-permute-done((bf16[256,512]{1,0:T(8,128)(2,1)S(1)}, bf16[256,512]{1,0:T(8,128)(2,1)S(1)}, u32[]{:S(2)}, u32[]{:S(2)}) %collective-permute-start.33) | collective-permute-done | bytes 262176 | tf_op jit(solution)/shard_map/ppermute | solution.py:405
  242.0 17.3 %collective-permute-start.28 = (bf16[256,512]{1,0:T(8,128)(2,1)S(1)}, bf16[256,512]{1,0:T(8,128)(2,1)S(1)}, u32[]{:S(2)}, u32[]{:S(2)}) collective-permute-start(bf16[256,512]{1,0:T(8,128)(2,1)S(1)} %get-tuple-element.64), channel_id=1, source_target_pairs={{0,8},{8,16},{16,24},{24,0},{1,9},{9,17},{17,25},{25,1},{2,10},{10... | collective-permute-start | bytes 786440 | tf_op jit(solution)/shard_map/ppermute | solution.py:405
  259.4 5.1 %collective-permute-done.30.refs_6_ = bf16[256,512]{1,0:T(8,128)(2,1)S(1)} collective-permute-done((bf16[256,512]{1,0:T(8,128)(2,1)S(1)}, bf16[256,512]{1,0:T(8,128)(2,1)S(1)}, u32[]{:S(2)}, u32[]{:S(2)}) %collective-permute-start.30) | collective-permute-done | bytes 262176 | tf_op jit(solution)/shard_map/ppermute | solution.py:405
  264.4 7.8 %collective-permute-done.27.refs_2_ = bf16[256,512]{1,0:T(8,128)(2,1)S(1)} collective-permute-done((bf16[256,512]{1,0:T(8,128)(2,1)S(1)}, bf16[256,512]{1,0:T(8,128)(2,1)S(1)}, u32[]{:S(2)}, u32[]{:S(2)}) %collective-permute-start.27) | collective-permute-done | bytes 262176 | tf_op jit(solution)/shard_map/ppermute | solution.py:405
  272.2 3.9 %assemble.1 = bf16[256,16,512]{2,1,0:T(8,128)(2,1)} custom-call(s32[2]{0:T(128)S(1)} %get-tuple-element.41.pos_ref.place_ref, bf16[256,512]{1,0:T(8,128)(2,1)S(1)} %get-tuple-element.61.refs_0_, bf16[256,512]{1,0:T(8,128)(2,1)S(1)} %collective-permute-done.26.refs_1_, bf16[256,512]{1,0:T(8,128)(2,1)S(1)} %collective-permute-done.27.refs_2_, ...), custom_call_target="tpu_custom_call" | custom-call | flops 1073741824 | bytes 8388608 | tf_op jit(solution)/shard_map/assemble/pallas_call | solution.py:379
  (78 shorter events, 57.2 us)
Async XLA Ops:
  10.0 22.9 %collective-permute-start.2 = (bf16[256,512]{1,0:T(8,128)(2,1)S(1)}, bf16[256,512]{1,0:T(8,128)(2,1)S(1)}, u32[]{:S(2)}, u32[]{:S(2)}) collective-permute-start(bf16[256,512]{1,0:T(8,128)(2,1)S(1)} %transform.10), channel_id=1, source_target_pairs={{0,24},{8,0},{16,8},{24,16},{1,25},{9,1},{17,9},{25,17},{2,26},{10... | collective-permute-start | bytes 786440 | tf_op jit(solution)/shard_map/ppermute | solution.py:405
  17.6 19.8 %collective-permute-start.1 = (bf16[256,512]{1,0:T(8,128)(2,1)S(1)}, bf16[256,512]{1,0:T(8,128)(2,1)S(1)}, u32[]{:S(2)}, u32[]{:S(2)}) collective-permute-start(bf16[256,512]{1,0:T(8,128)(2,1)S(1)} %transform.9), channel_id=1, source_target_pairs={{0,16},{8,24},{16,0},{24,8},{1,17},{9,25},{17,1},{25,9},{2,18},{10... | collective-permute-start | bytes 786440 | tf_op jit(solution)/shard_map/ppermute | solution.py:405
  20.3 17.1 %collective-permute-start = (bf16[256,512]{1,0:T(8,128)(2,1)S(1)}, bf16[256,512]{1,0:T(8,128)(2,1)S(1)}, u32[]{:S(2)}, u32[]{:S(2)}) collective-permute-start(bf16[256,512]{1,0:T(8,128)(2,1)S(1)} %transform.8), channel_id=1, source_target_pairs={{0,8},{8,16},{16,24},{24,0},{1,9},{9,17},{17,25},{25,1},{2,10},{10... | collective-permute-start | bytes 786440 | tf_op jit(solution)/shard_map/ppermute | solution.py:405
  38.1 31.9 %collective-permute-start.3 = (bf16[1280,512]{1,0:T(8,128)(2,1)S(1)}, bf16[1280,512]{1,0:T(8,128)(2,1)S(1)}, u32[]{:S(2)}, u32[]{:S(2)}) collective-permute-start(bf16[1280,512]{1,0:T(8,128)(2,1)S(1)} %join.4.refs_0_.own_ref), channel_id=1, source_target_pairs={{1,7},{2,0},{3,1},{5,3},{6,4},{7,5},{9,15},{10,8},{11,9},{13,11},{... | collective-permute-start | bytes 3932168 | tf_op jit(solution)/shard_map/ppermute | solution.py:433
  39.4 30.6 %collective-permute-start.7 = (bf16[1280,512]{1,0:T(8,128)(2,1)S(1)}, bf16[1280,512]{1,0:T(8,128)(2,1)S(1)}, u32[]{:S(2)}, u32[]{:S(2)}) collective-permute-start(bf16[1280,512]{1,0:T(8,128)(2,1)S(1)} %join.4.refs_0_.own_ref), channel_id=1, source_target_pairs={{4,1},{6,3},{0,5},{2,7},{12,9},{14,11},{8,13},{10,15},{20,17},{22,... | collective-permute-start | bytes 3932168 | tf_op jit(solution)/shard_map/ppermute | solution.py:434
  43.6 17.0 %collective-permute-start.4 = (bf16[256,512]{1,0:T(8,128)(2,1)S(1)}, bf16[256,512]{1,0:T(8,128)(2,1)S(1)}, u32[]{:S(2)}, u32[]{:S(2)}) collective-permute-start(bf16[256,512]{1,0:T(8,128)(2,1)S(1)} %get-tuple-element.46), channel_id=1, source_target_pairs={{0,8},{8,16},{16,24},{24,0},{1,9},{9,17},{17,25},{25,1},{2,10},{10... | collective-permute-start | bytes 786440 | tf_op jit(solution)/shard_map/ppermute | solution.py:405
  45.9 18.3 %collective-permute-start.5 = (bf16[256,512]{1,0:T(8,128)(2,1)S(1)}, bf16[256,512]{1,0:T(8,128)(2,1)S(1)}, u32[]{:S(2)}, u32[]{:S(2)}) collective-permute-start(bf16[256,512]{1,0:T(8,128)(2,1)S(1)} %get-tuple-element.47), channel_id=1, source_target_pairs={{0,16},{8,24},{16,0},{24,8},{1,17},{9,25},{17,1},{25,9},{2,18},{10... | collective-permute-start | bytes 786440 | tf_op jit(solution)/shard_map/ppermute | solution.py:405
  47.9 16.3 %collective-permute-start.6 = (bf16[256,512]{1,0:T(8,128)(2,1)S(1)}, bf16[256,512]{1,0:T(8,128)(2,1)S(1)}, u32[]{:S(2)}, u32[]{:S(2)}) collective-permute-start(bf16[256,512]{1,0:T(8,128)(2,1)S(1)} %get-tuple-element.48), channel_id=1, source_target_pairs={{0,24},{8,0},{16,8},{24,16},{1,25},{9,1},{17,9},{25,17},{2,26},{10... | collective-permute-start | bytes 786440 | tf_op jit(solution)/shard_map/ppermute | solution.py:405
  70.7 30.4 %collective-permute-start.8 = (bf16[1280,512]{1,0:T(8,128)(2,1)S(1)}, bf16[1280,512]{1,0:T(8,128)(2,1)S(1)}, u32[]{:S(2)}, u32[]{:S(2)}) collective-permute-start(bf16[1280,512]{1,0:T(8,128)(2,1)S(1)} %get-tuple-element.50), channel_id=1, source_target_pairs={{4,1},{6,3},{0,5},{2,7},{5,6},{1,2},{12,9},{14,11},{8,13},{10,15},... | collective-permute-start | bytes 3932168 | tf_op jit(solution)/shard_map/ppermute | solution.py:434
  72.3 28.9 %collective-permute-start.12 = (bf16[1024,512]{1,0:T(8,128)(2,1)S(1)}, bf16[1024,512]{1,0:T(8,128)(2,1)S(1)}, u32[]{:S(2)}, u32[]{:S(2)}) collective-permute-start(bf16[1024,512]{1,0:T(8,128)(2,1)S(1)} %get-tuple-element.54.refs_0_.own_ref), channel_id=1, source_target_pairs={{1,7},{2,0},{3,1},{5,3},{6,4},{7,5},{9,15},{10,8},{11,9},{13,11},{... | collective-permute-start | bytes 3145736 | tf_op jit(solution)/shard_map/ppermute | solution.py:433
  73.6 17.7 %collective-permute-start.10 = (bf16[256,512]{1,0:T(8,128)(2,1)S(1)}, bf16[256,512]{1,0:T(8,128)(2,1)S(1)}, u32[]{:S(2)}, u32[]{:S(2)}) collective-permute-start(bf16[256,512]{1,0:T(8,128)(2,1)S(1)} %get-tuple-element.52), channel_id=1, source_target_pairs={{0,16},{8,24},{16,0},{24,8},{1,17},{9,25},{17,1},{25,9},{2,18},{10... | collective-permute-start | bytes 786440 | tf_op jit(solution)/shard_map/ppermute | solution.py:405
  79.0 17.0 %collective-permute-start.9 = (bf16[256,512]{1,0:T(8,128)(2,1)S(1)}, bf16[256,512]{1,0:T(8,128)(2,1)S(1)}, u32[]{:S(2)}, u32[]{:S(2)}) collective-permute-start(bf16[256,512]{1,0:T(8,128)(2,1)S(1)} %get-tuple-element.51), channel_id=1, source_target_pairs={{0,8},{8,16},{16,24},{24,0},{1,9},{9,17},{17,25},{25,1},{2,10},{10... | collective-permute-start | bytes 786440 | tf_op jit(solution)/shard_map/ppermute | solution.py:405
  101.8 25.6 %collective-permute-start.13 = (bf16[1024,512]{1,0:T(8,128)(2,1)S(1)}, bf16[1024,512]{1,0:T(8,128)(2,1)S(1)}, u32[]{:S(2)}, u32[]{:S(2)}) collective-permute-start(bf16[1024,512]{1,0:T(8,128)(2,1)S(1)} %get-tuple-element.56), channel_id=1, source_target_pairs={{4,1},{6,3},{0,5},{2,7},{5,6},{1,2},{12,9},{14,11},{8,13},{10,15},... | collective-permute-start | bytes 3145736 | tf_op jit(solution)/shard_map/ppermute | solution.py:434
  103.9 28.1 %collective-permute-start.17 = (bf16[1024,512]{1,0:T(8,128)(2,1)S(1)}, bf16[1024,512]{1,0:T(8,128)(2,1)S(1)}, u32[]{:S(2)}, u32[]{:S(2)}) collective-permute-start(bf16[1024,512]{1,0:T(8,128)(2,1)S(1)} %get-tuple-element.60.own_ref), channel_id=1, source_target_pairs={{1,7},{2,0},{3,1},{5,3},{6,4},{7,5},{9,15},{10,8},{11,9},{13,11},{... | collective-permute-start | bytes 3145736 | tf_op jit(solution)/shard_map/ppermute | solution.py:433
  107.5 19.9 %collective-permute-start.15 = (bf16[256,512]{1,0:T(8,128)(2,1)S(1)}, bf16[256,512]{1,0:T(8,128)(2,1)S(1)}, u32[]{:S(2)}, u32[]{:S(2)}) collective-permute-start(bf16[256,512]{1,0:T(8,128)(2,1)S(1)} %get-tuple-element.58), channel_id=1, source_target_pairs={{0,16},{8,24},{16,0},{24,8},{1,17},{9,25},{17,1},{25,9},{2,18},{10... | collective-permute-start | bytes 786440 | tf_op jit(solution)/shard_map/ppermute | solution.py:405
  109.5 17.9 %collective-permute-start.16 = (bf16[256,512]{1,0:T(8,128)(2,1)S(1)}, bf16[256,512]{1,0:T(8,128)(2,1)S(1)}, u32[]{:S(2)}, u32[]{:S(2)}) collective-permute-start(bf16[256,512]{1,0:T(8,128)(2,1)S(1)} %get-tuple-element.59), channel_id=1, source_target_pairs={{0,24},{8,0},{16,8},{24,16},{1,25},{9,1},{17,9},{25,17},{2,26},{10... | collective-permute-start | bytes 786440 | tf_op jit(solution)/shard_map/ppermute | solution.py:405
  135.6 31.3 %collective-permute-start.22 = (bf16[2,1280,512]{2,1,0:T(8,128)(2,1)S(1)}, bf16[2,1280,512]{2,1,0:T(8,128)(2,1)S(1)}, u32[]{:S(2)}, u32[]{:S(2)}) collective-permute-start(bf16[2,1280,512]{2,1,0:T(8,128)(2,1)S(1)} %pick.4.refs_6_), channel_id=1, source_target_pairs={{0,1},{1,0},{2,3},{3,2},{4,5},{5,4},{6,7},{7,6},{8,9},{9,8},{10,11... | collective-permute-start | bytes 7864328 | tf_op jit(solution)/shard_map/ppermute | solution.py:448
  137.9 21.4 %collective-permute-start.19 = (bf16[768,512]{1,0:T(8,128)(2,1)S(1)}, bf16[768,512]{1,0:T(8,128)(2,1)S(1)}, u32[]{:S(2)}, u32[]{:S(2)}) collective-permute-start(bf16[768,512]{1,0:T(8,128)(2,1)S(1)} %join.7.own_ref), channel_id=1, source_target_pairs={{1,7},{2,0},{3,1},{5,3},{6,4},{7,5},{9,15},{10,8},{11,9},{13,11},{... | collective-permute-start | bytes 2359304 | tf_op jit(solution)/shard_map/ppermute | solution.py:433
  145.0 22.0 %collective-permute-start.23 = (bf16[2,1024,512]{2,1,0:T(8,128)(2,1)S(1)}, bf16[2,1024,512]{2,1,0:T(8,128)(2,1)S(1)}, u32[]{:S(2)}, u32[]{:S(2)}) collective-permute-start(bf16[2,1024,512]{2,1,0:T(8,128)(2,1)S(1)} %pick.5.refs_7_), channel_id=1, source_target_pairs={{0,1},{1,0},{2,3},{3,2},{4,5},{5,4},{6,7},{7,6},{8,9},{9,8},{10,11... | collective-permute-start | bytes 6291464 | tf_op jit(solution)/shard_map/ppermute | solution.py:448
  149.4 20.0 %collective-permute-start.24 = (bf16[2,1024,512]{2,1,0:T(8,128)(2,1)S(1)}, bf16[2,1024,512]{2,1,0:T(8,128)(2,1)S(1)}, u32[]{:S(2)}, u32[]{:S(2)}) collective-permute-start(bf16[2,1024,512]{2,1,0:T(8,128)(2,1)S(1)} %pick.6.refs_8_), channel_id=1, source_target_pairs={{0,1},{1,0},{2,3},{3,2},{4,5},{5,4},{6,7},{7,6},{8,9},{9,8},{10,11... | collective-permute-start | bytes 6291464 | tf_op jit(solution)/shard_map/ppermute | solution.py:448
  173.9 31.1 %collective-permute-start.35 = (bf16[256,512]{1,0:T(8,128)(2,1)S(1)}, bf16[256,512]{1,0:T(8,128)(2,1)S(1)}, u32[]{:S(2)}, u32[]{:S(2)}) collective-permute-start(bf16[256,512]{1,0:T(8,128)(2,1)S(1)} %get-tuple-element.74), channel_id=1, source_target_pairs={{0,24},{8,0},{16,8},{24,16},{1,25},{9,1},{17,9},{25,17},{2,26},{10... | collective-permute-start | bytes 786440 | tf_op jit(solution)/shard_map/ppermute | solution.py:405
  178.4 41.1 %collective-permute-start.36 = (bf16[256,512]{1,0:T(8,128)(2,1)S(1)}, bf16[256,512]{1,0:T(8,128)(2,1)S(1)}, u32[]{:S(2)}, u32[]{:S(2)}) collective-permute-start(bf16[256,512]{1,0:T(8,128)(2,1)S(1)} %get-tuple-element.75), channel_id=1, source_target_pairs={{0,16},{8,24},{16,0},{24,8},{1,17},{9,25},{17,1},{25,9},{2,18},{10... | collective-permute-start | bytes 786440 | tf_op jit(solution)/shard_map/ppermute | solution.py:405
  186.0 41.3 %collective-permute-start.37 = (bf16[256,512]{1,0:T(8,128)(2,1)S(1)}, bf16[256,512]{1,0:T(8,128)(2,1)S(1)}, u32[]{:S(2)}, u32[]{:S(2)}) collective-permute-start(bf16[256,512]{1,0:T(8,128)(2,1)S(1)} %get-tuple-element.76), channel_id=1, source_target_pairs={{0,8},{8,16},{16,24},{24,0},{1,9},{9,17},{17,25},{25,1},{2,10},{10... | collective-permute-start | bytes 786440 | tf_op jit(solution)/shard_map/ppermute | solution.py:405
  200.1 27.2 %collective-permute-start.32 = (bf16[256,512]{1,0:T(8,128)(2,1)S(1)}, bf16[256,512]{1,0:T(8,128)(2,1)S(1)}, u32[]{:S(2)}, u32[]{:S(2)}) collective-permute-start(bf16[256,512]{1,0:T(8,128)(2,1)S(1)} %get-tuple-element.70), channel_id=1, source_target_pairs={{0,24},{8,0},{16,8},{24,16},{1,25},{9,1},{17,9},{25,17},{2,26},{10... | collective-permute-start | bytes 786440 | tf_op jit(solution)/shard_map/ppermute | solution.py:405
  200.1 41.8 %collective-permute-start.33 = (bf16[256,512]{1,0:T(8,128)(2,1)S(1)}, bf16[256,512]{1,0:T(8,128)(2,1)S(1)}, u32[]{:S(2)}, u32[]{:S(2)}) collective-permute-start(bf16[256,512]{1,0:T(8,128)(2,1)S(1)} %get-tuple-element.71), channel_id=1, source_target_pairs={{0,16},{8,24},{16,0},{24,8},{1,17},{9,25},{17,1},{25,9},{2,18},{10... | collective-permute-start | bytes 786440 | tf_op jit(solution)/shard_map/ppermute | solution.py:405
  205.0 36.9 %collective-permute-start.34 = (bf16[256,512]{1,0:T(8,128)(2,1)S(1)}, bf16[256,512]{1,0:T(8,128)(2,1)S(1)}, u32[]{:S(2)}, u32[]{:S(2)}) collective-permute-start(bf16[256,512]{1,0:T(8,128)(2,1)S(1)} %get-tuple-element.72), channel_id=1, source_target_pairs={{0,8},{8,16},{16,24},{24,0},{1,9},{9,17},{17,25},{25,1},{2,10},{10... | collective-permute-start | bytes 786440 | tf_op jit(solution)/shard_map/ppermute | solution.py:405
  219.5 22.6 %collective-permute-start.29 = (bf16[256,512]{1,0:T(8,128)(2,1)S(1)}, bf16[256,512]{1,0:T(8,128)(2,1)S(1)}, u32[]{:S(2)}, u32[]{:S(2)}) collective-permute-start(bf16[256,512]{1,0:T(8,128)(2,1)S(1)} %get-tuple-element.66), channel_id=1, source_target_pairs={{0,24},{8,0},{16,8},{24,16},{1,25},{9,1},{17,9},{25,17},{2,26},{10... | collective-permute-start | bytes 786440 | tf_op jit(solution)/shard_map/ppermute | solution.py:405
  227.2 37.2 %collective-permute-start.30 = (bf16[256,512]{1,0:T(8,128)(2,1)S(1)}, bf16[256,512]{1,0:T(8,128)(2,1)S(1)}, u32[]{:S(2)}, u32[]{:S(2)}) collective-permute-start(bf16[256,512]{1,0:T(8,128)(2,1)S(1)} %get-tuple-element.67), channel_id=1, source_target_pairs={{0,16},{8,24},{16,0},{24,8},{1,17},{9,25},{17,1},{25,9},{2,18},{10... | collective-permute-start | bytes 786440 | tf_op jit(solution)/shard_map/ppermute | solution.py:405
  227.3 37.1 %collective-permute-start.31 = (bf16[256,512]{1,0:T(8,128)(2,1)S(1)}, bf16[256,512]{1,0:T(8,128)(2,1)S(1)}, u32[]{:S(2)}, u32[]{:S(2)}) collective-permute-start(bf16[256,512]{1,0:T(8,128)(2,1)S(1)} %get-tuple-element.68), channel_id=1, source_target_pairs={{0,8},{8,16},{16,24},{24,0},{1,9},{9,17},{17,25},{25,1},{2,10},{10... | collective-permute-start | bytes 786440 | tf_op jit(solution)/shard_map/ppermute | solution.py:405
  241.9 22.5 %collective-permute-start.26 = (bf16[256,512]{1,0:T(8,128)(2,1)S(1)}, bf16[256,512]{1,0:T(8,128)(2,1)S(1)}, u32[]{:S(2)}, u32[]{:S(2)}) collective-permute-start(bf16[256,512]{1,0:T(8,128)(2,1)S(1)} %get-tuple-element.62), channel_id=1, source_target_pairs={{0,24},{8,0},{16,8},{24,16},{1,25},{9,1},{17,9},{25,17},{2,26},{10... | collective-permute-start | bytes 786440 | tf_op jit(solution)/shard_map/ppermute | solution.py:405
  242.0 30.3 %collective-permute-start.27 = (bf16[256,512]{1,0:T(8,128)(2,1)S(1)}, bf16[256,512]{1,0:T(8,128)(2,1)S(1)}, u32[]{:S(2)}, u32[]{:S(2)}) collective-permute-start(bf16[256,512]{1,0:T(8,128)(2,1)S(1)} %get-tuple-element.63), channel_id=1, source_target_pairs={{0,16},{8,24},{16,0},{24,8},{1,17},{9,25},{17,1},{25,9},{2,18},{10... | collective-permute-start | bytes 786440 | tf_op jit(solution)/shard_map/ppermute | solution.py:405
  242.0 30.2 %collective-permute-start.28 = (bf16[256,512]{1,0:T(8,128)(2,1)S(1)}, bf16[256,512]{1,0:T(8,128)(2,1)S(1)}, u32[]{:S(2)}, u32[]{:S(2)}) collective-permute-start(bf16[256,512]{1,0:T(8,128)(2,1)S(1)} %get-tuple-element.64), channel_id=1, source_target_pairs={{0,8},{8,16},{16,24},{24,0},{1,9},{9,17},{17,25},{25,1},{2,10},{10... | collective-permute-start | bytes 786440 | tf_op jit(solution)/shard_map/ppermute | solution.py:405
  (12 other events, 145.4 us)

commit v3 on v2

--- a/solution.py
+++ b/solution.py
@@ -143,7 +143,10 @@
 
     @pl.when(place_ref[1] % 2 == 1)
     def _():
-        onward[...] = refs[count][: onward.shape[0], :]
+        known = min(onward.shape[0], refs[count].shape[0])
+        onward[:known, :] = refs[count][:known, :]
+        if onward.shape[0] > known:
+            onward[known:, :] = out[known : onward.shape[0], :]
 
 
 def stacked(pieces, place, held, after, onward_rows=0):
@@ -286,10 +289,10 @@
             for orbital in range(OCC_DEV):
                 @pl.when(place == kind * OCC_DEV + orbital)
                 def _():
-                    if orbital == 0:
-                        first, rest = parts[0].at[pl.ds(0, split)], parts[0].at[pl.ds(split, aux - split)]
+                    if orbital <= 1:
+                        first, rest = (parts[orbital].at[pl.ds(start, size)] for start, size in ((0, split), (split, aux - split)))
                     else:
-                        start = aux if orbital == 1 else aux - split
+                        start = aux if orbital == 2 else aux - split
                         first = parts[orbital - 1].at[pl.ds(start, split)]
                         rest = parts[orbital].at[pl.ds(0, aux - split)]
                     pltpu.make_async_copy(first, held.at[buffer, pl.ds(0, split)], sems.at[buffer, 0]).start()
@@ -316,12 +319,15 @@
         energy = lambda which: occ_ref[slot_orbital(place_ref, count, occ_count, which)]
         shift = energy(chunk) + energy(slot)
         other = held[buffer]
-        exchange = jnp.dot(turned[...], other, preferred_element_type=jnp.float32)
-        denom = (col_ref[:, chunk : chunk + 1] + row_ref[slot]) - shift
-        amplitude = (exchange / denom).astype(jnp.bfloat16)
-        total[...] += lax.dot_general(
-            other, amplitude, (((1,), (1,)), ((), ())), preferred_element_type=jnp.float32
-        )
+        half = turned.shape[0] // 2
+        halves = [slice(0, half), slice(half, 2 * half)]
+        exchanges = [jnp.dot(turned[span, :], other, preferred_element_type=jnp.float32) for span in halves]
+        for span, exchange in zip(halves, exchanges):
+            denom = (col_ref[span, chunk : chunk + 1] + row_ref[slot]) - shift
+            amplitude = (exchange / denom).astype(jnp.bfloat16)
+            total[:, span] += lax.dot_general(
+                other, amplitude, (((1,), (1,)), ((), ())), preferred_element_type=jnp.float32
+            )
         return carry
 
     lax.fori_loop(0, pairs, step, jnp.int32(0))
@@ -425,9 +431,9 @@
             coming = [sent[0]] + [along_aux(sent[step], step) for step in range(1, aux_count)]
         if chunk < OCC_DEV:
             parts.append(pieces)
-            message = pieces[0 if chunk == 0 else 1 :] + coming[:1]
+            message = pieces[0 if chunk <= 1 else 1 :] + (coming[:1] if chunk >= 1 else [])
             rides = bool(last) and 0 < chunk < OCC_DEV - 1
-            ready = nears[-1:] + ([] if rides else thirds[-1:])
+            ready = nears[-1:] + ([] if rides else thirds[-1:]) + (coming[:1] if chunk == 0 else [])
             onward_rows = max(sum(piece.shape[0] for piece in message), owns[-1].shape[0]) if rides else 0
             own, *onward = stacked(message, place, thirds[-1:] if rides else [], ready, onward_rows)
             near = lax.ppermute(own, "occ", direct)

time: 277 us -> 274 us (0.989)
  Pallas kernels: 85.8 us -> 74.8 us
  starting transfers between devices: 94.9 us -> 104 us
  waiting for transfers between devices: 93.7 us -> 90.9 us
    ppermute x4, waiting for transfers between devices: 25.3 us -> 5.31 us  [body(): near = lax.ppermute(own, 'occ', direct)]
    pallas_call x4, Pallas kernels: 31.2 us -> 20.2 us  [densities(): pl.pallas_call(functools.partial(pair_kernel, chunk, count, occ_count), i...]
    ppermute x24, waiting for transfers between devices: 61.9 us -> 72.3 us  [along_aux(): lax.ppermute(value, 'aux', [(z, (z + steps) % aux_count) for z in range(a...]
    ppermute x4, starting transfers between devices: 12.2 us -> 19.1 us  [body(): swaps.append(lax.ppermute(both, 'occ', twin))]
    ppermute x2, waiting for transfers between devices: 0.01 us -> 3.8 us  [body(): lax.ppermute(onward[0], 'occ', far + last)]
    ppermute x2, waiting for transfers between devices: 4.15 us -> 7.1 us  [body(): lax.ppermute(own, 'occ', far)]
  transfers between devices with their start and end apart: 38 -> 38, of which waited for: 17 -> 13; matrix products, arithmetic and copies ran while one was open for 0% -> 0% of each run, Pallas kernels for 24% -> 21%
where the time goes in v3:
time: 274 us; the launch traced here: 272 us
  starting transfers between devices  104 us (38%)
  waiting for transfers between devices  90.9 us (33%)
  Pallas kernels  74.8 us (27%)
    ppermute x24, waiting for transfers between devices, along_aux(): lax.ppermute(value, 'aux', [(z, (z + steps) % aux_count) for z in range(a...  72.3 us
    ppermute x24, starting transfers between devices, along_aux(): lax.ppermute(value, 'aux', [(z, (z + steps) % aux_count) for z in range(a...  68.3 us
    pallas_call x7, Pallas kernels, transformed(): pl.pallas_call(functools.partial(transform_kernel, count, orbitals, orbit...  36.9 us
    pallas_call x4, Pallas kernels, densities(): pl.pallas_call(functools.partial(pair_kernel, chunk, count, occ_count), i...  20.2 us
    ppermute x4, starting transfers between devices, body(): swaps.append(lax.ppermute(both, 'occ', twin))  19.1 us
    ppermute x2, waiting for transfers between devices, body(): lax.ppermute(own, 'occ', far)  7.1 us
    ppermute x2, starting transfers between devices, body(): lax.ppermute(own, 'occ', far)  6.75 us
    pallas_call x1, Pallas kernels, sorted_rows(): pl.pallas_call(sort_kernel, grid=(rows // block,), in_specs=[smem, smem,...  6.67 us
  transfers between devices with their start and end apart: 38, of which 13 were waited for; matrix products, arithmetic and copies ran while one was open for 0% of the time, Pallas kernels for 21%

profile of v3, /device:TPU:0, one launch (start us, length us, event | category | flops | bytes accessed | tf_op | source)
XLA Modules:
  0.0 271.6 jit_solution(13399288128650471779)
XLA Ops:
  0.7 6.7 %sort_rows.1 = (bf16[16,256,1024]{2,1,0:T(8,128)(2,1)S(1)}, s32[2]{0:T(128)S(1)}) custom-call(s32[4,16]{1,0:T(4,128)S(1)} %copy-done.5, s32[1]{0:T(128)} %bitcast.aux_ref, s32[1]{0:T(128)} %bitcast.1.occ_ref, bf16[256,16,1024]{2,1,0:T(8,128)(2,1)} %x_ref.1), custom_call_target="tpu_custom_call" | custom-call | flops 2147483648 | bytes 16777216 | tf_op jit(solution)/shard_map/sort_rows/pallas_call | solution.py:44
  10.0 3.1 %collective-permute-start = (bf16[256,512]{1,0:T(8,128)(2,1)S(1)}, bf16[256,512]{1,0:T(8,128)(2,1)S(1)}, u32[]{:S(2)}, u32[]{:S(2)}) collective-permute-start(bf16[256,512]{1,0:T(8,128)(2,1)S(1)} %transform.8), channel_id=1, source_target_pairs={{0,8},{8,16},{16,24},{24,0},{1,9},{9,17},{17,25},{25,1},{2,10},{10... | collective-permute-start | bytes 786440 | tf_op jit(solution)/shard_map/ppermute | solution.py:411
  24.9 8.9 %transform.11 = (bf16[256,512]{1,0:T(8,128)(2,1)S(1)}, bf16[256,512]{1,0:T(8,128)(2,1)S(1)}, bf16[256,512]{1,0:T(8,128)(2,1)S(1)}, bf16[256,512]{1,0:T(8,128)(2,1)S(1)}) custom-call(s32[2]{0:T(128)S(1)} %get-tuple-element.41.pos_ref.place_ref, bf16[16,256,1024]{2,1,0:T(8,128)(2,1)S(1)} %get-tuple-element.42.x_ref, s32[128,512]{1,0:T(8,128)S(1)} %copy-done.1, ...), custom_call_target="tpu_custom_call" | custom-call | flops 6442450944 | bytes 7340032 | tf_op jit(solution)/shard_map/transform/pallas_call | solution.py:101
  35.8 3.7 %collective-permute-start.7 = (bf16[1024,512]{1,0:T(8,128)(2,1)S(1)}, bf16[1024,512]{1,0:T(8,128)(2,1)S(1)}, u32[]{:S(2)}, u32[]{:S(2)}) collective-permute-start(bf16[1024,512]{1,0:T(8,128)(2,1)S(1)} %join.4.refs_0_.own_ref), channel_id=1, source_target_pairs={{4,1},{6,3},{0,5},{2,7},{12,9},{14,11},{8,13},{10,15},{20,17},{22,... | collective-permute-start | bytes 3145736 | tf_op jit(solution)/shard_map/ppermute | solution.py:440
  39.5 6.2 %collective-permute-start.4 = (bf16[256,512]{1,0:T(8,128)(2,1)S(1)}, bf16[256,512]{1,0:T(8,128)(2,1)S(1)}, u32[]{:S(2)}, u32[]{:S(2)}) collective-permute-start(bf16[256,512]{1,0:T(8,128)(2,1)S(1)} %get-tuple-element.46), channel_id=1, source_target_pairs={{0,8},{8,16},{16,24},{24,0},{1,9},{9,17},{17,25},{25,1},{2,10},{10... | collective-permute-start | bytes 786440 | tf_op jit(solution)/shard_map/ppermute | solution.py:411
  49.2 8.9 %transform.12 = (bf16[256,512]{1,0:T(8,128)(2,1)S(1)}, bf16[256,512]{1,0:T(8,128)(2,1)S(1)}, bf16[256,512]{1,0:T(8,128)(2,1)S(1)}, bf16[256,512]{1,0:T(8,128)(2,1)S(1)}) custom-call(s32[2]{0:T(128)S(1)} %get-tuple-element.41.pos_ref.place_ref, bf16[16,256,1024]{2,1,0:T(8,128)(2,1)S(1)} %get-tuple-element.42.x_ref, s32[128,512]{1,0:T(8,128)S(1)} %copy-done.1, ...), custom_call_target="tpu_custom_call" | custom-call | flops 6442450944 | bytes 7340032 | tf_op jit(solution)/shard_map/transform/pallas_call | solution.py:101
  58.1 4.7 %collective-permute-done.5.refs_2_ = bf16[256,512]{1,0:T(8,128)(2,1)S(1)} collective-permute-done((bf16[256,512]{1,0:T(8,128)(2,1)S(1)}, bf16[256,512]{1,0:T(8,128)(2,1)S(1)}, u32[]{:S(2)}, u32[]{:S(2)}) %collective-permute-start.5) | collective-permute-done | bytes 262176 | tf_op jit(solution)/shard_map/ppermute | solution.py:411
  66.7 6.2 %collective-permute-start.9 = (bf16[256,512]{1,0:T(8,128)(2,1)S(1)}, bf16[256,512]{1,0:T(8,128)(2,1)S(1)}, u32[]{:S(2)}, u32[]{:S(2)}) collective-permute-start(bf16[256,512]{1,0:T(8,128)(2,1)S(1)} %get-tuple-element.51), channel_id=1, source_target_pairs={{0,8},{8,16},{16,24},{24,0},{1,9},{9,17},{17,25},{25,1},{2,10},{10... | collective-permute-start | bytes 786440 | tf_op jit(solution)/shard_map/ppermute | solution.py:411
  75.4 8.9 %transform.13 = (bf16[256,512]{1,0:T(8,128)(2,1)S(1)}, bf16[256,512]{1,0:T(8,128)(2,1)S(1)}, bf16[256,512]{1,0:T(8,128)(2,1)S(1)}, bf16[256,512]{1,0:T(8,128)(2,1)S(1)}) custom-call(s32[2]{0:T(128)S(1)} %get-tuple-element.41.pos_ref.place_ref, bf16[16,256,1024]{2,1,0:T(8,128)(2,1)S(1)} %get-tuple-element.42.x_ref, s32[128,512]{1,0:T(8,128)S(1)} %copy-done.1, ...), custom_call_target="tpu_custom_call" | custom-call | flops 6442450944 | bytes 7340032 | tf_op jit(solution)/shard_map/transform/pallas_call | solution.py:101
  84.3 8.3 %collective-permute-done.10.refs_1_.refs_2_ = bf16[256,512]{1,0:T(8,128)(2,1)S(1)} collective-permute-done((bf16[256,512]{1,0:T(8,128)(2,1)S(1)}, bf16[256,512]{1,0:T(8,128)(2,1)S(1)}, u32[]{:S(2)}, u32[]{:S(2)}) %collective-permute-start.10) | collective-permute-done | bytes 262176 | tf_op jit(solution)/shard_map/ppermute | solution.py:411
  92.6 5.3 %collective-permute-done.12.refs_3_.refs_5_.near_ref = bf16[1280,512]{1,0:T(8,128)(2,1)S(1)} collective-permute-done((bf16[1280,512]{1,0:T(8,128)(2,1)S(1)}, bf16[1280,512]{1,0:T(8,128)(2,1)S(1)}, u32[]{:S(2)}, u32[]{:S(2)}) %collective-permute-start.12) | collective-permute-done | bytes 1310752 | tf_op jit(solution)/shard_map/ppermute | solution.py:439
  101.4 6.1 %collective-permute-start.14 = (bf16[256,512]{1,0:T(8,128)(2,1)S(1)}, bf16[256,512]{1,0:T(8,128)(2,1)S(1)}, u32[]{:S(2)}, u32[]{:S(2)}) collective-permute-start(bf16[256,512]{1,0:T(8,128)(2,1)S(1)} %get-tuple-element.57), channel_id=1, source_target_pairs={{0,8},{8,16},{16,24},{24,0},{1,9},{9,17},{17,25},{25,1},{2,10},{10... | collective-permute-start | bytes 786440 | tf_op jit(solution)/shard_map/ppermute | solution.py:411
  107.5 3.8 %collective-permute-start.15 = (bf16[256,512]{1,0:T(8,128)(2,1)S(1)}, bf16[256,512]{1,0:T(8,128)(2,1)S(1)}, u32[]{:S(2)}, u32[]{:S(2)}) collective-permute-start(bf16[256,512]{1,0:T(8,128)(2,1)S(1)} %get-tuple-element.58), channel_id=1, source_target_pairs={{0,16},{8,24},{16,0},{24,8},{1,17},{9,25},{17,1},{25,9},{2,18},{10... | collective-permute-start | bytes 786440 | tf_op jit(solution)/shard_map/ppermute | solution.py:411
  111.4 3.8 %collective-permute-done.13.late_ref.refs_4_.refs_16_ = bf16[1280,512]{1,0:T(8,128)(2,1)S(1)} collective-permute-done((bf16[1280,512]{1,0:T(8,128)(2,1)S(1)}, bf16[1280,512]{1,0:T(8,128)(2,1)S(1)}, u32[]{:S(2)}, u32[]{:S(2)}) %collective-permute-start.13) | collective-permute-done | bytes 1310752 | tf_op jit(solution)/shard_map/ppermute | solution.py:440
  118.2 9.5 %collective-permute-done.15.refs_1_.refs_2_ = bf16[256,512]{1,0:T(8,128)(2,1)S(1)} collective-permute-done((bf16[256,512]{1,0:T(8,128)(2,1)S(1)}, bf16[256,512]{1,0:T(8,128)(2,1)S(1)}, u32[]{:S(2)}, u32[]{:S(2)}) %collective-permute-start.15) | collective-permute-done | bytes 262176 | tf_op jit(solution)/shard_map/ppermute | solution.py:411
  128.3 3.1 %collective-permute-start.20 = (bf16[768,512]{1,0:T(8,128)(2,1)S(1)}, bf16[768,512]{1,0:T(8,128)(2,1)S(1)}, u32[]{:S(2)}, u32[]{:S(2)}) collective-permute-start(bf16[768,512]{1,0:T(8,128)(2,1)S(1)} %join.7.own_ref), channel_id=1, source_target_pairs={{4,1},{6,3},{0,5},{2,7},{12,9},{14,11},{8,13},{10,15},{20,17},{22,... | collective-permute-start | bytes 2359304 | tf_op jit(solution)/shard_map/ppermute | solution.py:440
  133.7 7.1 %collective-permute-done.20.refs_17_ = bf16[768,512]{1,0:T(8,128)(2,1)S(1)} collective-permute-done((bf16[768,512]{1,0:T(8,128)(2,1)S(1)}, bf16[768,512]{1,0:T(8,128)(2,1)S(1)}, u32[]{:S(2)}, u32[]{:S(2)}) %collective-permute-start.20) | collective-permute-done | bytes 786464 | tf_op jit(solution)/shard_map/ppermute | solution.py:440
  142.4 11.9 %collective-permute-start.22 = (bf16[2,1024,512]{2,1,0:T(8,128)(2,1)S(1)}, bf16[2,1024,512]{2,1,0:T(8,128)(2,1)S(1)}, u32[]{:S(2)}, u32[]{:S(2)}) collective-permute-start(bf16[2,1024,512]{2,1,0:T(8,128)(2,1)S(1)} %pick.4.refs_6_), channel_id=1, source_target_pairs={{0,1},{1,0},{2,3},{3,2},{4,5},{5,4},{6,7},{7,6},{8,9},{9,8},{10,11... | collective-permute-start | bytes 6291464 | tf_op jit(solution)/shard_map/ppermute | solution.py:454
  156.1 7.0 %collective-permute-start.25 = (bf16[2,768,512]{2,1,0:T(8,128)(2,1)S(1)}, bf16[2,768,512]{2,1,0:T(8,128)(2,1)S(1)}, u32[]{:S(2)}, u32[]{:S(2)}) collective-permute-start(bf16[2,768,512]{2,1,0:T(8,128)(2,1)S(1)} %pick.7.refs_9_), channel_id=1, source_target_pairs={{0,1},{1,0},{2,3},{3,2},{4,5},{5,4},{6,7},{7,6},{8,9},{9,8},{10,11... | collective-permute-start | bytes 4718600 | tf_op jit(solution)/shard_map/ppermute | solution.py:454
  166.1 3.0 %pairs.4 = (bf16[256,512]{1,0:T(8,128)(2,1)S(1)}, bf16[256,512]{1,0:T(8,128)(2,1)S(1)}, bf16[256,512]{1,0:T(8,128)(2,1)S(1)}, bf16[256,512]{1,0:T(8,128)(2,1)S(1)}) custom-call(s32[1,1]{1,0:T(1,128)S(6)} %copy.9.live_ref, s32[16]{0:T(128)S(1)} %bitcast.4, s32[2]{0:T(128)S(1)} %get-tuple-element.41.pos_ref.place_ref, f32[128]{0:T(128)S(1)} %copy-done.3, ...), custom_call_target="tpu_custom_call" | custom-call | flops 4294967296 | bytes 3145728 | tf_op jit(solution)/shard_map/pairs/pallas_call | solution.py:344
  169.2 8.1 %collective-permute-start.26 = (bf16[256,512]{1,0:T(8,128)(2,1)S(1)}, bf16[256,512]{1,0:T(8,128)(2,1)S(1)}, u32[]{:S(2)}, u32[]{:S(2)}) collective-permute-start(bf16[256,512]{1,0:T(8,128)(2,1)S(1)} %get-tuple-element.62), channel_id=1, source_target_pairs={{0,24},{8,0},{16,8},{24,16},{1,25},{9,1},{17,9},{25,17},{2,26},{10... | collective-permute-start | bytes 786440 | tf_op jit(solution)/shard_map/ppermute | solution.py:411
  177.9 4.6 %pairs.5 = (bf16[256,512]{1,0:T(8,128)(2,1)S(1)}, bf16[256,512]{1,0:T(8,128)(2,1)S(1)}, bf16[256,512]{1,0:T(8,128)(2,1)S(1)}, bf16[256,512]{1,0:T(8,128)(2,1)S(1)}) custom-call(s32[1,1]{1,0:T(1,128)S(6)} %copy.9.live_ref, s32[16]{0:T(128)S(1)} %bitcast.5, s32[2]{0:T(128)S(1)} %get-tuple-element.41.pos_ref.place_ref, f32[128]{0:T(128)S(1)} %copy-done.3, ...), custom_call_target="tpu_custom_call" | custom-call | flops 4294967296 | bytes 3145728 | tf_op jit(solution)/shard_map/pairs/pallas_call | solution.py:344
  182.5 4.8 %collective-permute-start.29 = (bf16[256,512]{1,0:T(8,128)(2,1)S(1)}, bf16[256,512]{1,0:T(8,128)(2,1)S(1)}, u32[]{:S(2)}, u32[]{:S(2)}) collective-permute-start(bf16[256,512]{1,0:T(8,128)(2,1)S(1)} %get-tuple-element.66), channel_id=1, source_target_pairs={{0,24},{8,0},{16,8},{24,16},{1,25},{9,1},{17,9},{25,17},{2,26},{10... | collective-permute-start | bytes 786440 | tf_op jit(solution)/shard_map/ppermute | solution.py:411
  188.1 3.2 %pairs.6 = (bf16[256,512]{1,0:T(8,128)(2,1)S(1)}, bf16[256,512]{1,0:T(8,128)(2,1)S(1)}, bf16[256,512]{1,0:T(8,128)(2,1)S(1)}, bf16[256,512]{1,0:T(8,128)(2,1)S(1)}) custom-call(s32[1,1]{1,0:T(1,128)S(6)} %copy.9.live_ref, s32[16]{0:T(128)S(1)} %bitcast.6, s32[2]{0:T(128)S(1)} %get-tuple-element.41.pos_ref.place_ref, f32[128]{0:T(128)S(1)} %copy-done.3, ...), custom_call_target="tpu_custom_call" | custom-call | flops 4294967296 | bytes 3145728 | tf_op jit(solution)/shard_map/pairs/pallas_call | solution.py:344
  191.4 3.8 %collective-permute-start.31 = (bf16[256,512]{1,0:T(8,128)(2,1)S(1)}, bf16[256,512]{1,0:T(8,128)(2,1)S(1)}, u32[]{:S(2)}, u32[]{:S(2)}) collective-permute-start(bf16[256,512]{1,0:T(8,128)(2,1)S(1)} %get-tuple-element.68), channel_id=1, source_target_pairs={{0,8},{8,16},{16,24},{24,0},{1,9},{9,17},{17,25},{25,1},{2,10},{10... | collective-permute-start | bytes 786440 | tf_op jit(solution)/shard_map/ppermute | solution.py:411
  195.2 16.2 %collective-permute-done.27.refs_2_ = bf16[256,512]{1,0:T(8,128)(2,1)S(1)} collective-permute-done((bf16[256,512]{1,0:T(8,128)(2,1)S(1)}, bf16[256,512]{1,0:T(8,128)(2,1)S(1)}, u32[]{:S(2)}, u32[]{:S(2)}) %collective-permute-start.27) | collective-permute-done | bytes 262176 | tf_op jit(solution)/shard_map/ppermute | solution.py:411
  211.4 9.4 %pairs.7 = (bf16[256,512]{1,0:T(8,128)(2,1)S(1)}, bf16[256,512]{1,0:T(8,128)(2,1)S(1)}, bf16[256,512]{1,0:T(8,128)(2,1)S(1)}, bf16[256,512]{1,0:T(8,128)(2,1)S(1)}) custom-call(s32[1,1]{1,0:T(1,128)S(6)} %copy.9.live_ref, s32[16]{0:T(128)S(1)} %bitcast.7, s32[2]{0:T(128)S(1)} %get-tuple-element.41.pos_ref.place_ref, f32[128]{0:T(128)S(1)} %copy-done.3, ...), custom_call_target="tpu_custom_call" | custom-call | flops 4294967296 | bytes 3145728 | tf_op jit(solution)/shard_map/pairs/pallas_call | solution.py:344
  223.6 9.7 %collective-permute-done.30.refs_6_ = bf16[256,512]{1,0:T(8,128)(2,1)S(1)} collective-permute-done((bf16[256,512]{1,0:T(8,128)(2,1)S(1)}, bf16[256,512]{1,0:T(8,128)(2,1)S(1)}, u32[]{:S(2)}, u32[]{:S(2)}) %collective-permute-start.30) | collective-permute-done | bytes 262176 | tf_op jit(solution)/shard_map/ppermute | solution.py:411
  233.3 11.1 %collective-permute-start.36 = (bf16[256,512]{1,0:T(8,128)(2,1)S(1)}, bf16[256,512]{1,0:T(8,128)(2,1)S(1)}, u32[]{:S(2)}, u32[]{:S(2)}) collective-permute-start(bf16[256,512]{1,0:T(8,128)(2,1)S(1)} %get-tuple-element.75), channel_id=1, source_target_pairs={{0,16},{8,24},{16,0},{24,8},{1,17},{9,25},{17,1},{25,9},{2,18},{10... | collective-permute-start | bytes 786440 | tf_op jit(solution)/shard_map/ppermute | solution.py:411
  246.4 10.7 %collective-permute-done.33.refs_10_ = bf16[256,512]{1,0:T(8,128)(2,1)S(1)} collective-permute-done((bf16[256,512]{1,0:T(8,128)(2,1)S(1)}, bf16[256,512]{1,0:T(8,128)(2,1)S(1)}, u32[]{:S(2)}, u32[]{:S(2)}) %collective-permute-start.33) | collective-permute-done | bytes 262176 | tf_op jit(solution)/shard_map/ppermute | solution.py:411
  257.1 10.7 %collective-permute-done.36.refs_14_ = bf16[256,512]{1,0:T(8,128)(2,1)S(1)} collective-permute-done((bf16[256,512]{1,0:T(8,128)(2,1)S(1)}, bf16[256,512]{1,0:T(8,128)(2,1)S(1)}, u32[]{:S(2)}, u32[]{:S(2)}) %collective-permute-start.36) | collective-permute-done | bytes 262176 | tf_op jit(solution)/shard_map/ppermute | solution.py:411
  267.7 3.9 %assemble.1 = bf16[256,16,512]{2,1,0:T(8,128)(2,1)} custom-call(s32[2]{0:T(128)S(1)} %get-tuple-element.41.pos_ref.place_ref, bf16[256,512]{1,0:T(8,128)(2,1)S(1)} %get-tuple-element.61.refs_0_, bf16[256,512]{1,0:T(8,128)(2,1)S(1)} %collective-permute-done.26.refs_1_, bf16[256,512]{1,0:T(8,128)(2,1)S(1)} %collective-permute-done.27.refs_2_, ...), custom_call_target="tpu_custom_call" | custom-call | flops 1073741824 | bytes 8388608 | tf_op jit(solution)/shard_map/assemble/pallas_call | solution.py:385
  (78 shorter events, 48.3 us)
Async XLA Ops:
  10.0 23.8 %collective-permute-start = (bf16[256,512]{1,0:T(8,128)(2,1)S(1)}, bf16[256,512]{1,0:T(8,128)(2,1)S(1)}, u32[]{:S(2)}, u32[]{:S(2)}) collective-permute-start(bf16[256,512]{1,0:T(8,128)(2,1)S(1)} %transform.8), channel_id=1, source_target_pairs={{0,8},{8,16},{16,24},{24,0},{1,9},{9,17},{17,25},{25,1},{2,10},{10... | collective-permute-start | bytes 786440 | tf_op jit(solution)/shard_map/ppermute | solution.py:411
  15.6 18.1 %collective-permute-start.1 = (bf16[256,512]{1,0:T(8,128)(2,1)S(1)}, bf16[256,512]{1,0:T(8,128)(2,1)S(1)}, u32[]{:S(2)}, u32[]{:S(2)}) collective-permute-start(bf16[256,512]{1,0:T(8,128)(2,1)S(1)} %transform.9), channel_id=1, source_target_pairs={{0,16},{8,24},{16,0},{24,8},{1,17},{9,25},{17,1},{25,9},{2,18},{10... | collective-permute-start | bytes 786440 | tf_op jit(solution)/shard_map/ppermute | solution.py:411
  34.5 28.2 %collective-permute-start.3 = (bf16[1024,512]{1,0:T(8,128)(2,1)S(1)}, bf16[1024,512]{1,0:T(8,128)(2,1)S(1)}, u32[]{:S(2)}, u32[]{:S(2)}) collective-permute-start(bf16[1024,512]{1,0:T(8,128)(2,1)S(1)} %join.4.refs_0_.own_ref), channel_id=1, source_target_pairs={{1,7},{2,0},{3,1},{5,3},{6,4},{7,5},{9,15},{10,8},{11,9},{13,11},{... | collective-permute-start | bytes 3145736 | tf_op jit(solution)/shard_map/ppermute | solution.py:439
  35.8 26.9 %collective-permute-start.7 = (bf16[1024,512]{1,0:T(8,128)(2,1)S(1)}, bf16[1024,512]{1,0:T(8,128)(2,1)S(1)}, u32[]{:S(2)}, u32[]{:S(2)}) collective-permute-start(bf16[1024,512]{1,0:T(8,128)(2,1)S(1)} %join.4.refs_0_.own_ref), channel_id=1, source_target_pairs={{4,1},{6,3},{0,5},{2,7},{12,9},{14,11},{8,13},{10,15},{20,17},{22,... | collective-permute-start | bytes 3145736 | tf_op jit(solution)/shard_map/ppermute | solution.py:440
  39.5 18.5 %collective-permute-start.4 = (bf16[256,512]{1,0:T(8,128)(2,1)S(1)}, bf16[256,512]{1,0:T(8,128)(2,1)S(1)}, u32[]{:S(2)}, u32[]{:S(2)}) collective-permute-start(bf16[256,512]{1,0:T(8,128)(2,1)S(1)} %get-tuple-element.46), channel_id=1, source_target_pairs={{0,8},{8,16},{16,24},{24,0},{1,9},{9,17},{17,25},{25,1},{2,10},{10... | collective-permute-start | bytes 786440 | tf_op jit(solution)/shard_map/ppermute | solution.py:411
  45.7 17.0 %collective-permute-start.5 = (bf16[256,512]{1,0:T(8,128)(2,1)S(1)}, bf16[256,512]{1,0:T(8,128)(2,1)S(1)}, u32[]{:S(2)}, u32[]{:S(2)}) collective-permute-start(bf16[256,512]{1,0:T(8,128)(2,1)S(1)} %get-tuple-element.47), channel_id=1, source_target_pairs={{0,16},{8,24},{16,0},{24,8},{1,17},{9,25},{17,1},{25,9},{2,18},{10... | collective-permute-start | bytes 786440 | tf_op jit(solution)/shard_map/ppermute | solution.py:411
  46.2 16.5 %collective-permute-start.6 = (bf16[256,512]{1,0:T(8,128)(2,1)S(1)}, bf16[256,512]{1,0:T(8,128)(2,1)S(1)}, u32[]{:S(2)}, u32[]{:S(2)}) collective-permute-start(bf16[256,512]{1,0:T(8,128)(2,1)S(1)} %get-tuple-element.48), channel_id=1, source_target_pairs={{0,24},{8,0},{16,8},{24,16},{1,25},{9,1},{17,9},{25,17},{2,26},{10... | collective-permute-start | bytes 786440 | tf_op jit(solution)/shard_map/ppermute | solution.py:411
  63.5 29.1 %collective-permute-start.8 = (bf16[1280,512]{1,0:T(8,128)(2,1)S(1)}, bf16[1280,512]{1,0:T(8,128)(2,1)S(1)}, u32[]{:S(2)}, u32[]{:S(2)}) collective-permute-start(bf16[1280,512]{1,0:T(8,128)(2,1)S(1)} %get-tuple-element.50), channel_id=1, source_target_pairs={{4,1},{6,3},{0,5},{2,7},{5,6},{1,2},{12,9},{14,11},{8,13},{10,15},... | collective-permute-start | bytes 3932168 | tf_op jit(solution)/shard_map/ppermute | solution.py:440
  65.4 32.4 %collective-permute-start.12 = (bf16[1280,512]{1,0:T(8,128)(2,1)S(1)}, bf16[1280,512]{1,0:T(8,128)(2,1)S(1)}, u32[]{:S(2)}, u32[]{:S(2)}) collective-permute-start(bf16[1280,512]{1,0:T(8,128)(2,1)S(1)} %get-tuple-element.54.refs_0_.own_ref), channel_id=1, source_target_pairs={{1,7},{2,0},{3,1},{5,3},{6,4},{7,5},{9,15},{10,8},{11,9},{13,11},{... | collective-permute-start | bytes 3932168 | tf_op jit(solution)/shard_map/ppermute | solution.py:439
  66.7 17.5 %collective-permute-start.9 = (bf16[256,512]{1,0:T(8,128)(2,1)S(1)}, bf16[256,512]{1,0:T(8,128)(2,1)S(1)}, u32[]{:S(2)}, u32[]{:S(2)}) collective-permute-start(bf16[256,512]{1,0:T(8,128)(2,1)S(1)} %get-tuple-element.51), channel_id=1, source_target_pairs={{0,8},{8,16},{16,24},{24,0},{1,9},{9,17},{17,25},{25,1},{2,10},{10... | collective-permute-start | bytes 786440 | tf_op jit(solution)/shard_map/ppermute | solution.py:411
  73.0 19.6 %collective-permute-start.10 = (bf16[256,512]{1,0:T(8,128)(2,1)S(1)}, bf16[256,512]{1,0:T(8,128)(2,1)S(1)}, u32[]{:S(2)}, u32[]{:S(2)}) collective-permute-start(bf16[256,512]{1,0:T(8,128)(2,1)S(1)} %get-tuple-element.52), channel_id=1, source_target_pairs={{0,16},{8,24},{16,0},{24,8},{1,17},{9,25},{17,1},{25,9},{2,18},{10... | collective-permute-start | bytes 786440 | tf_op jit(solution)/shard_map/ppermute | solution.py:411
  74.6 17.9 %collective-permute-start.11 = (bf16[256,512]{1,0:T(8,128)(2,1)S(1)}, bf16[256,512]{1,0:T(8,128)(2,1)S(1)}, u32[]{:S(2)}, u32[]{:S(2)}) collective-permute-start(bf16[256,512]{1,0:T(8,128)(2,1)S(1)} %get-tuple-element.53), channel_id=1, source_target_pairs={{0,24},{8,0},{16,8},{24,16},{1,25},{9,1},{17,9},{25,17},{2,26},{10... | collective-permute-start | bytes 786440 | tf_op jit(solution)/shard_map/ppermute | solution.py:411
  98.6 16.6 %collective-permute-start.13 = (bf16[1280,512]{1,0:T(8,128)(2,1)S(1)}, bf16[1280,512]{1,0:T(8,128)(2,1)S(1)}, u32[]{:S(2)}, u32[]{:S(2)}) collective-permute-start(bf16[1280,512]{1,0:T(8,128)(2,1)S(1)} %get-tuple-element.56), channel_id=1, source_target_pairs={{4,1},{6,3},{0,5},{2,7},{5,6},{1,2},{12,9},{14,11},{8,13},{10,15},... | collective-permute-start | bytes 3932168 | tf_op jit(solution)/shard_map/ppermute | solution.py:440
  100.1 27.5 %collective-permute-start.17 = (bf16[1024,512]{1,0:T(8,128)(2,1)S(1)}, bf16[1024,512]{1,0:T(8,128)(2,1)S(1)}, u32[]{:S(2)}, u32[]{:S(2)}) collective-permute-start(bf16[1024,512]{1,0:T(8,128)(2,1)S(1)} %get-tuple-element.60.own_ref), channel_id=1, source_target_pairs={{1,7},{2,0},{3,1},{5,3},{6,4},{7,5},{9,15},{10,8},{11,9},{13,11},{... | collective-permute-start | bytes 3145736 | tf_op jit(solution)/shard_map/ppermute | solution.py:439
  101.4 16.7 %collective-permute-start.14 = (bf16[256,512]{1,0:T(8,128)(2,1)S(1)}, bf16[256,512]{1,0:T(8,128)(2,1)S(1)}, u32[]{:S(2)}, u32[]{:S(2)}) collective-permute-start(bf16[256,512]{1,0:T(8,128)(2,1)S(1)} %get-tuple-element.57), channel_id=1, source_target_pairs={{0,8},{8,16},{16,24},{24,0},{1,9},{9,17},{17,25},{25,1},{2,10},{10... | collective-permute-start | bytes 786440 | tf_op jit(solution)/shard_map/ppermute | solution.py:411
  107.5 20.1 %collective-permute-start.15 = (bf16[256,512]{1,0:T(8,128)(2,1)S(1)}, bf16[256,512]{1,0:T(8,128)(2,1)S(1)}, u32[]{:S(2)}, u32[]{:S(2)}) collective-permute-start(bf16[256,512]{1,0:T(8,128)(2,1)S(1)} %get-tuple-element.58), channel_id=1, source_target_pairs={{0,16},{8,24},{16,0},{24,8},{1,17},{9,25},{17,1},{25,9},{2,18},{10... | collective-permute-start | bytes 786440 | tf_op jit(solution)/shard_map/ppermute | solution.py:411
  115.2 39.2 %collective-permute-start.18 = (bf16[1280,512]{1,0:T(8,128)(2,1)S(1)}, bf16[1280,512]{1,0:T(8,128)(2,1)S(1)}, u32[]{:S(2)}, u32[]{:S(2)}) collective-permute-start(bf16[1280,512]{1,0:T(8,128)(2,1)S(1)} %collective-permute-done.13.late_ref.refs_4_.refs_16_), channel_id=1, source_target_pairs={{5,6},{1,2},{13,14},{9,10},{21,22},{17,18},{29,30},{25,26}} | collective-permute-start | bytes 3932168 | tf_op jit(solution)/shard_map/ppermute | solution.py:447
  132.3 31.5 %collective-permute-start.23 = (bf16[2,1280,512]{2,1,0:T(8,128)(2,1)S(1)}, bf16[2,1280,512]{2,1,0:T(8,128)(2,1)S(1)}, u32[]{:S(2)}, u32[]{:S(2)}) collective-permute-start(bf16[2,1280,512]{2,1,0:T(8,128)(2,1)S(1)} %pick.5.refs_7_), channel_id=1, source_target_pairs={{0,1},{1,0},{2,3},{3,2},{4,5},{5,4},{6,7},{7,6},{8,9},{9,8},{10,11... | collective-permute-start | bytes 7864328 | tf_op jit(solution)/shard_map/ppermute | solution.py:454
  132.4 22.9 %collective-permute-start.19 = (bf16[768,512]{1,0:T(8,128)(2,1)S(1)}, bf16[768,512]{1,0:T(8,128)(2,1)S(1)}, u32[]{:S(2)}, u32[]{:S(2)}) collective-permute-start(bf16[768,512]{1,0:T(8,128)(2,1)S(1)} %join.7.own_ref), channel_id=1, source_target_pairs={{1,7},{2,0},{3,1},{5,3},{6,4},{7,5},{9,15},{10,8},{11,9},{13,11},{... | collective-permute-start | bytes 2359304 | tf_op jit(solution)/shard_map/ppermute | solution.py:439
  142.4 21.4 %collective-permute-start.22 = (bf16[2,1024,512]{2,1,0:T(8,128)(2,1)S(1)}, bf16[2,1024,512]{2,1,0:T(8,128)(2,1)S(1)}, u32[]{:S(2)}, u32[]{:S(2)}) collective-permute-start(bf16[2,1024,512]{2,1,0:T(8,128)(2,1)S(1)} %pick.4.refs_6_), channel_id=1, source_target_pairs={{0,1},{1,0},{2,3},{3,2},{4,5},{5,4},{6,7},{7,6},{8,9},{9,8},{10,11... | collective-permute-start | bytes 6291464 | tf_op jit(solution)/shard_map/ppermute | solution.py:454
  169.2 22.2 %collective-permute-start.26 = (bf16[256,512]{1,0:T(8,128)(2,1)S(1)}, bf16[256,512]{1,0:T(8,128)(2,1)S(1)}, u32[]{:S(2)}, u32[]{:S(2)}) collective-permute-start(bf16[256,512]{1,0:T(8,128)(2,1)S(1)} %get-tuple-element.62), channel_id=1, source_target_pairs={{0,24},{8,0},{16,8},{24,16},{1,25},{9,1},{17,9},{25,17},{2,26},{10... | collective-permute-start | bytes 786440 | tf_op jit(solution)/shard_map/ppermute | solution.py:411
  177.3 34.2 %collective-permute-start.27 = (bf16[256,512]{1,0:T(8,128)(2,1)S(1)}, bf16[256,512]{1,0:T(8,128)(2,1)S(1)}, u32[]{:S(2)}, u32[]{:S(2)}) collective-permute-start(bf16[256,512]{1,0:T(8,128)(2,1)S(1)} %get-tuple-element.63), channel_id=1, source_target_pairs={{0,16},{8,24},{16,0},{24,8},{1,17},{9,25},{17,1},{25,9},{2,18},{10... | collective-permute-start | bytes 786440 | tf_op jit(solution)/shard_map/ppermute | solution.py:411
  177.3 43.5 %collective-permute-start.28 = (bf16[256,512]{1,0:T(8,128)(2,1)S(1)}, bf16[256,512]{1,0:T(8,128)(2,1)S(1)}, u32[]{:S(2)}, u32[]{:S(2)}) collective-permute-start(bf16[256,512]{1,0:T(8,128)(2,1)S(1)} %get-tuple-element.64), channel_id=1, source_target_pairs={{0,8},{8,16},{16,24},{24,0},{1,9},{9,17},{17,25},{25,1},{2,10},{10... | collective-permute-start | bytes 786440 | tf_op jit(solution)/shard_map/ppermute | solution.py:411
  182.5 39.4 %collective-permute-start.29 = (bf16[256,512]{1,0:T(8,128)(2,1)S(1)}, bf16[256,512]{1,0:T(8,128)(2,1)S(1)}, u32[]{:S(2)}, u32[]{:S(2)}) collective-permute-start(bf16[256,512]{1,0:T(8,128)(2,1)S(1)} %get-tuple-element.66), channel_id=1, source_target_pairs={{0,24},{8,0},{16,8},{24,16},{1,25},{9,1},{17,9},{25,17},{2,26},{10... | collective-permute-start | bytes 786440 | tf_op jit(solution)/shard_map/ppermute | solution.py:411
  187.3 46.0 %collective-permute-start.30 = (bf16[256,512]{1,0:T(8,128)(2,1)S(1)}, bf16[256,512]{1,0:T(8,128)(2,1)S(1)}, u32[]{:S(2)}, u32[]{:S(2)}) collective-permute-start(bf16[256,512]{1,0:T(8,128)(2,1)S(1)} %get-tuple-element.67), channel_id=1, source_target_pairs={{0,16},{8,24},{16,0},{24,8},{1,17},{9,25},{17,1},{25,9},{2,18},{10... | collective-permute-start | bytes 786440 | tf_op jit(solution)/shard_map/ppermute | solution.py:411
  191.4 42.0 %collective-permute-start.31 = (bf16[256,512]{1,0:T(8,128)(2,1)S(1)}, bf16[256,512]{1,0:T(8,128)(2,1)S(1)}, u32[]{:S(2)}, u32[]{:S(2)}) collective-permute-start(bf16[256,512]{1,0:T(8,128)(2,1)S(1)} %get-tuple-element.68), channel_id=1, source_target_pairs={{0,8},{8,16},{16,24},{24,0},{1,9},{9,17},{17,25},{25,1},{2,10},{10... | collective-permute-start | bytes 786440 | tf_op jit(solution)/shard_map/ppermute | solution.py:411
  211.4 33.0 %collective-permute-start.32 = (bf16[256,512]{1,0:T(8,128)(2,1)S(1)}, bf16[256,512]{1,0:T(8,128)(2,1)S(1)}, u32[]{:S(2)}, u32[]{:S(2)}) collective-permute-start(bf16[256,512]{1,0:T(8,128)(2,1)S(1)} %get-tuple-element.70), channel_id=1, source_target_pairs={{0,24},{8,0},{16,8},{24,16},{1,25},{9,1},{17,9},{25,17},{2,26},{10... | collective-permute-start | bytes 786440 | tf_op jit(solution)/shard_map/ppermute | solution.py:411
  220.8 36.2 %collective-permute-start.33 = (bf16[256,512]{1,0:T(8,128)(2,1)S(1)}, bf16[256,512]{1,0:T(8,128)(2,1)S(1)}, u32[]{:S(2)}, u32[]{:S(2)}) collective-permute-start(bf16[256,512]{1,0:T(8,128)(2,1)S(1)} %get-tuple-element.71), channel_id=1, source_target_pairs={{0,16},{8,24},{16,0},{24,8},{1,17},{9,25},{17,1},{25,9},{2,18},{10... | collective-permute-start | bytes 786440 | tf_op jit(solution)/shard_map/ppermute | solution.py:411
  221.9 35.1 %collective-permute-start.34 = (bf16[256,512]{1,0:T(8,128)(2,1)S(1)}, bf16[256,512]{1,0:T(8,128)(2,1)S(1)}, u32[]{:S(2)}, u32[]{:S(2)}) collective-permute-start(bf16[256,512]{1,0:T(8,128)(2,1)S(1)} %get-tuple-element.72), channel_id=1, source_target_pairs={{0,8},{8,16},{16,24},{24,0},{1,9},{9,17},{17,25},{25,1},{2,10},{10... | collective-permute-start | bytes 786440 | tf_op jit(solution)/shard_map/ppermute | solution.py:411
  233.3 23.7 %collective-permute-start.35 = (bf16[256,512]{1,0:T(8,128)(2,1)S(1)}, bf16[256,512]{1,0:T(8,128)(2,1)S(1)}, u32[]{:S(2)}, u32[]{:S(2)}) collective-permute-start(bf16[256,512]{1,0:T(8,128)(2,1)S(1)} %get-tuple-element.74), channel_id=1, source_target_pairs={{0,24},{8,0},{16,8},{24,16},{1,25},{9,1},{17,9},{25,17},{2,26},{10... | collective-permute-start | bytes 786440 | tf_op jit(solution)/shard_map/ppermute | solution.py:411
  233.3 34.4 %collective-permute-start.36 = (bf16[256,512]{1,0:T(8,128)(2,1)S(1)}, bf16[256,512]{1,0:T(8,128)(2,1)S(1)}, u32[]{:S(2)}, u32[]{:S(2)}) collective-permute-start(bf16[256,512]{1,0:T(8,128)(2,1)S(1)} %get-tuple-element.75), channel_id=1, source_target_pairs={{0,16},{8,24},{16,0},{24,8},{1,17},{9,25},{17,1},{25,9},{2,18},{10... | collective-permute-start | bytes 786440 | tf_op jit(solution)/shard_map/ppermute | solution.py:411
  244.5 23.3 %collective-permute-start.37 = (bf16[256,512]{1,0:T(8,128)(2,1)S(1)}, bf16[256,512]{1,0:T(8,128)(2,1)S(1)}, u32[]{:S(2)}, u32[]{:S(2)}) collective-permute-start(bf16[256,512]{1,0:T(8,128)(2,1)S(1)} %get-tuple-element.76), channel_id=1, source_target_pairs={{0,8},{8,16},{16,24},{24,0},{1,9},{9,17},{17,25},{25,1},{2,10},{10... | collective-permute-start | bytes 786440 | tf_op jit(solution)/shard_map/ppermute | solution.py:411
  (12 other events, 127.7 us)

commit v4 on v3

--- a/solution.py
+++ b/solution.py
@@ -249,21 +249,43 @@
     )(place, domains, vir_energy.reshape(-1, 128))
 
 
-def pair_kernel(chunk, count, occ_count, live_ref, code_ref, place_ref, occ_ref, *refs):
-    own_refs, (col_ref, row_ref), refs = refs[:count], refs[count : count + 2], refs[count + 2 :]
+def ranked(code_at, live, slots):
+    span = PARTNERS * OCC_DEV
+
+    def tally(slot, counts):
+        own = code_at(slot) // span
+        return tuple(
+            count + ((own == orbital) & (slot < live)).astype(jnp.int32) for orbital, count in enumerate(counts)
+        )
+
+    counts = lax.fori_loop(0, slots, tally, (jnp.int32(0),) * OCC_DEV)
+    places = []
+    for orbital, count in enumerate(counts):
+        place = jnp.int32(0)
+        for other, value in enumerate(counts):
+            ahead = (value < count) | (value == count) if other < orbital else value < count
+            place += ahead.astype(jnp.int32)
+        places.append(place)
+    return [
+        sum(jnp.where(place == rank, orbital, 0) for orbital, place in enumerate(places)) for rank in range(OCC_DEV)
+    ]
+
+
+def pair_kernel(rank, count, occ_count, live_ref, code_ref, place_ref, occ_ref, col_ref, row_ref, *refs):
     sets = 3
     blocks = refs[: sets * OCC_DEV]
     outs = refs[sets * OCC_DEV : sets * OCC_DEV + count]
     turned, total, held, sems, todo = refs[sets * OCC_DEV + count :]
-    split = own_refs[0].shape[0]
-    aux = split * count
+    aux = held.shape[1]
+    split = aux // count
     span = PARTNERS * OCC_DEV
     slots = code_ref.shape[0]
     odd = place_ref[1] % 2
+    own = ranked(lambda slot: code_ref[slot], live_ref[0, 0], slots)[rank]
 
     def scan(slot, found):
         code = code_ref[slot]
-        mine = (slot < live_ref[0, 0]) & (code // span == chunk)
+        mine = (slot < live_ref[0, 0]) & (code // span == own)
 
         @pl.when(mine)
         def _():
@@ -280,9 +302,8 @@
         kind = jnp.where(offset == 0, 0, jnp.where(offset == 1, one, jnp.where(offset == 2, 1, three)))
         return kind * OCC_DEV + slot % OCC_DEV
 
-    def fetch(index):
-        place = source(todo[index])
-        buffer = lax.rem(index, 2)
+    def fetch(slot, buffer):
+        place = source(slot)
         for kind in range(5):
             parts = [blocks[kind // 2 * OCC_DEV + orbital] for orbital in range(OCC_DEV)]
             parts = [part.at[kind % 2] for part in parts] if kind < 4 else parts
@@ -298,32 +319,43 @@
                     pltpu.make_async_copy(first, held.at[buffer, pl.ds(0, split)], sems.at[buffer, 0]).start()
                     pltpu.make_async_copy(rest, held.at[buffer, pl.ds(split, aux - split)], sems.at[buffer, 1]).start()
 
-    @pl.when(pairs > 0)
-    def _():
-        fetch(0)
-        for index, own_ref in enumerate(own_refs):
-            turned[:, index * split : (index + 1) * split] = own_ref[...].T
-
-    total[...] = jnp.zeros_like(total)
-
-    def step(index, carry):
-        @pl.when(index + 1 < pairs)
-        def _():
-            fetch(index + 1)
-
-        buffer = lax.rem(index, 2)
+    def arrived(buffer):
         first, rest = held.at[buffer, pl.ds(0, split)], held.at[buffer, pl.ds(split, aux - split)]
         pltpu.make_async_copy(blocks[0].at[0, pl.ds(0, split)], first, sems.at[buffer, 0]).wait()
         pltpu.make_async_copy(blocks[0].at[0, pl.ds(split, aux - split)], rest, sems.at[buffer, 1]).wait()
+
+    @pl.when(pairs > 0)
+    def _():
+        fetch(own, 1)
+        fetch(todo[0], 0)
+
+    total[...] = jnp.zeros_like(total)
+
+    @pl.when(pairs > 0)
+    def _():
+        arrived(1)
+        turned[...] = held[1].T
+
+    lane = lax.broadcasted_iota(jnp.int32, col_ref.shape, 1)
+    column = jnp.sum(jnp.where(lane == own, col_ref[...], 0.0), axis=1, keepdims=True)
+
+    def step(index, carry):
+        buffer = lax.rem(index, 2)
+
+        @pl.when(index + 1 < pairs)
+        def _():
+            fetch(todo[index + 1], lax.rem(index + 1, 2))
+
+        arrived(buffer)
         slot = todo[index]
         energy = lambda which: occ_ref[slot_orbital(place_ref, count, occ_count, which)]
-        shift = energy(chunk) + energy(slot)
+        shift = energy(own) + energy(slot)
         other = held[buffer]
         half = turned.shape[0] // 2
         halves = [slice(0, half), slice(half, 2 * half)]
         exchanges = [jnp.dot(turned[span, :], other, preferred_element_type=jnp.float32) for span in halves]
         for span, exchange in zip(halves, exchanges):
-            denom = (col_ref[span, chunk : chunk + 1] + row_ref[slot]) - shift
+            denom = (column[span, :] + row_ref[slot]) - shift
             amplitude = (exchange / denom).astype(jnp.bfloat16)
             total[:, span] += lax.dot_general(
                 other, amplitude, (((1,), (1,)), ((), ())), preferred_element_type=jnp.float32
@@ -331,19 +363,19 @@
         return carry
 
     lax.fori_loop(0, pairs, step, jnp.int32(0))
-    part = outs[0].shape[0]
     for index, out in enumerate(outs):
-        out[...] = total[index * part : (index + 1) * part, :].astype(jnp.bfloat16)
-
-
-def densities(chunk, count, occ_count, live, codes, place, occ_energy, own, own_vir, vir_rows, blocks):
-    rows, virs = own[0].shape
+        out[...] = total[index * split : (index + 1) * split, :].astype(jnp.bfloat16)
+
+
+def densities(rank, count, occ_count, live, codes, place, occ_energy, rows, own_vir, vir_rows, blocks):
+    virs = own_vir.shape[0]
     aux = rows * count
     whole = lambda shape: pl.BlockSpec(shape, lambda: (0,) * len(shape))
     smem = pl.BlockSpec(memory_space=pltpu.SMEM)
     return pl.pallas_call(
-        functools.partial(pair_kernel, chunk, count, occ_count),
-        in_specs=[smem] * 4 + [whole((rows, virs))] * count + [whole(own_vir.shape), whole(vir_rows.shape)]
+        functools.partial(pair_kernel, rank, count, occ_count),
+        in_specs=[smem] * 4
+        + [whole(own_vir.shape), whole(vir_rows.shape)]
         + [pl.BlockSpec(memory_space=pl.ANY)] * len(blocks),
         out_specs=[whole((rows, virs))] * count,
         out_shape=[jax.ShapeDtypeStruct((rows, virs), jnp.bfloat16)] * count,
@@ -359,17 +391,28 @@
             flops=4 * 4 * aux * virs * virs, bytes_accessed=6 * aux * virs, transcendentals=0
         ),
         name="pairs",
-    )(live, codes, place, occ_energy, *own, own_vir, vir_rows, *blocks)
-
-
-def spread_kernel(count, pos_ref, *refs):
-    pieces, out = refs[:-1], refs[-1]
+    )(live, codes, place, occ_energy, own_vir, vir_rows, *blocks)
+
+
+def spread_kernel(count, pos_ref, live_ref, code_ref, *refs):
+    *pieces, out, where_ref = refs
+
+    @pl.when(pl.program_id(0) == 0)
+    def _():
+        for owner in range(count):
+            order = ranked(lambda slot: code_ref[owner, slot], live_ref[owner], code_ref.shape[1])
+            for rank, orbital in enumerate(reversed(order)):
+                where_ref[owner * OCC_DEV + rank] = owner * OCC_DEV + orbital
+
     orbitals = count * OCC_DEV
     width = orbitals * ROWS
     row = lax.broadcasted_iota(jnp.int32, (width, width), 0)
     col = lax.broadcasted_iota(jnp.int32, (width, width), 1)
-    group = col // ROWS
-    place = lax.rem(pos_ref[0] + group % count, count) * OCC_DEV + group // count
+    group = lax.broadcasted_iota(jnp.int32, (1, width), 1) // ROWS
+    place = jnp.zeros((1, width), jnp.int32)
+    for number in range(orbitals):
+        owner = lax.rem(pos_ref[0] + number % count, count)
+        place = jnp.where(group == number, where_ref[owner * OCC_DEV + number // count], place)
     hit = jnp.where((row % orbitals == place) & (row // orbitals == col % ROWS), 1.0, 0.0).astype(jnp.bfloat16)
     for part in range(out.shape[0] // ROWS):
         span = pl.ds(part * ROWS, ROWS)
@@ -378,17 +421,18 @@
         out[span] = moved.reshape(ROWS, orbitals, -1)
 
 
-def assembled(pieces, aux_pos, count):
+def assembled(pieces, aux_pos, count, live, codes):
     rows, virs = pieces[0].shape
     orbitals = count * OCC_DEV
     block = 4 * ROWS
     return pl.pallas_call(
         functools.partial(spread_kernel, count),
         grid_spec=pltpu.PrefetchScalarGridSpec(
-            num_scalar_prefetch=1,
+            num_scalar_prefetch=3,
             grid=(rows // block,),
-            in_specs=[pl.BlockSpec((block, virs), lambda g, pos: (g, 0))] * len(pieces),
-            out_specs=pl.BlockSpec((block, orbitals, virs), lambda g, pos: (g, 0, 0)),
+            in_specs=[pl.BlockSpec((block, virs), lambda g, *_: (g, 0))] * len(pieces),
+            out_specs=pl.BlockSpec((block, orbitals, virs), lambda g, *_: (g, 0, 0)),
+            scratch_shapes=[pltpu.SMEM((orbitals,), jnp.int32)],
         ),
         out_shape=jax.ShapeDtypeStruct((rows, orbitals, virs), jnp.bfloat16),
         compiler_params=pltpu.CompilerParams(vmem_limit_bytes=20 * MIB),
@@ -398,7 +442,7 @@
             transcendentals=0,
         ),
         name="assemble",
-    )(aux_pos, *pieces)
+    )(aux_pos, live, codes, *pieces)
 
 
 def body(half_ints, block_mask, vir_coef, domains, vir_energy, occ_energy, pair_count, pair_code):
@@ -414,6 +458,7 @@
         half_ints, block_mask, aux_pos.astype(jnp.int32).reshape(1), occ_pos.astype(jnp.int32).reshape(1)
     )
     vir_rows, vir_cols = energies(place, domains, vir_energy, aux_count, occ_count)
+    lists = lax.all_gather(jnp.concatenate([pair_code[0, 0], pair_count[0]]), "aux")
     twin, direct, far, last, late = routes(occ_count)
     transform = functools.partial(transformed, rows_of, domains, vir_coef, place, aux_count)
 
@@ -456,12 +501,13 @@
     blocks = sets + swaps + thirds
     codes = pair_code[0, 0]
     results = []
-    for chunk in range(OCC_DEV):
+    for turn in range(OCC_DEV):
         pieces = densities(
-            chunk, aux_count, occ_count, pair_count, codes, place, occ_energy, parts[chunk], vir_cols, vir_rows, blocks
+            OCC_DEV - 1 - turn, aux_count, occ_count, pair_count, codes, place, occ_energy, parts[0][0].shape[0],
+            vir_cols, vir_rows, blocks,
         )
         results += [pieces[0]] + [along_aux(pieces[step], -step) for step in range(1, aux_count)]
-    return assembled(results, place, aux_count)
+    return assembled(results, place, aux_count, lists[:, -1], lists[:, :-1])
 
 
 def routes(count):

time: 274 us -> 274 us (level)
  starting transfers between devices: 104 us -> 79.4 us
  blocking collectives: 0 us -> 21.1 us
  waiting for transfers between devices: 90.9 us -> 73.1 us
  Pallas kernels: 74.8 us -> 91.7 us
    ppermute x24, waiting for transfers between devices: 72.3 us -> 44.1 us  [along_aux(): lax.ppermute(value, 'aux', [(z, (z + steps) % aux_count) for z in range(a...]
    unnamed x0 -> x1, blocking collectives: none -> 21.1 us
    ppermute x24, starting transfers between devices: 68.3 us -> 48.3 us  [along_aux(): lax.ppermute(value, 'aux', [(z, (z + steps) % aux_count) for z in range(a...]
    pallas_call x4, Pallas kernels: 20.2 us -> 35.1 us  [densities(): pl.pallas_call(functools.partial(pair_kernel, rank, count, occ_count), in...]
    ppermute x4, starting transfers between devices: 19.1 us -> 8.51 us  [body(): swaps.append(lax.ppermute(both, 'occ', twin))]
    ppermute x4, waiting for transfers between devices: 5.31 us -> 13 us  [body(): near = lax.ppermute(own, 'occ', direct)]
    ppermute x2, starting transfers between devices: 3.5 us -> 8.37 us  [body(): lax.ppermute(onward[0], 'occ', far + last)]
    ppermute x2, waiting for transfers between devices: 3.8 us -> 6.59 us  [body(): lax.ppermute(onward[0], 'occ', far + last)]
  transfers between devices with their start and end apart: 38 -> 38, of which waited for: 13 -> 14; matrix products, arithmetic and copies ran while one was open for 0% -> 0% of each run, Pallas kernels for 21% -> 26%
where the time goes in v4:
time: 274 us; the launch traced here: 269 us
  Pallas kernels  91.7 us (33%)
  starting transfers between devices  79.4 us (29%)
  waiting for transfers between devices  73.1 us (27%)
  blocking collectives  21.1 us (8%)
    ppermute x24, starting transfers between devices, along_aux(): lax.ppermute(value, 'aux', [(z, (z + steps) % aux_count) for z in range(a...  48.3 us
    ppermute x24, waiting for transfers between devices, along_aux(): lax.ppermute(value, 'aux', [(z, (z + steps) % aux_count) for z in range(a...  44.1 us
    pallas_call x7, Pallas kernels, transformed(): pl.pallas_call(functools.partial(transform_kernel, count, orbitals, orbit...  36.8 us
    pallas_call x4, Pallas kernels, densities(): pl.pallas_call(functools.partial(pair_kernel, rank, count, occ_count), in...  35.1 us
    unnamed x1, blocking collectives  21.1 us
    ppermute x4, waiting for transfers between devices, body(): near = lax.ppermute(own, 'occ', direct)  13 us
    ppermute x4, starting transfers between devices, body(): swaps.append(lax.ppermute(both, 'occ', twin))  8.51 us
    ppermute x2, starting transfers between devices, body(): lax.ppermute(onward[0], 'occ', far + last)  8.37 us
  transfers between devices with their start and end apart: 38, of which 14 were waited for; matrix products, arithmetic and copies ran while one was open for 0% of the time, Pallas kernels for 26%

profile of v4, /device:TPU:0, one launch (start us, length us, event | category | flops | bytes accessed | tf_op | source)
XLA Modules:
  0.0 269.0 jit_solution(18020381378082746831)
XLA Ops:
  0.7 6.7 %sort_rows.1 = (bf16[16,256,1024]{2,1,0:T(8,128)(2,1)S(1)}, s32[2]{0:T(128)S(1)}) custom-call(s32[4,16]{1,0:T(4,128)S(1)} %copy-done.5, s32[1]{0:T(128)} %bitcast.aux_ref, s32[1]{0:T(128)} %bitcast.1.occ_ref, bf16[256,16,1024]{2,1,0:T(8,128)(2,1)} %x_ref.1), custom_call_target="tpu_custom_call" | custom-call | flops 2147483648 | bytes 16777216 | tf_op jit(solution)/shard_map/sort_rows/pallas_call | solution.py:44
  10.0 5.1 %collective-permute-start.2 = (bf16[256,512]{1,0:T(8,128)(2,1)S(1)}, bf16[256,512]{1,0:T(8,128)(2,1)S(1)}, u32[]{:S(2)}, u32[]{:S(2)}) collective-permute-start(bf16[256,512]{1,0:T(8,128)(2,1)S(1)} %transform.10), channel_id=1, source_target_pairs={{0,24},{8,0},{16,8},{24,16},{1,25},{9,1},{17,9},{25,17},{2,26},{10... | collective-permute-start | bytes 786440 | tf_op jit(solution)/shard_map/ppermute | solution.py:455
  23.9 8.9 %transform.11 = (bf16[256,512]{1,0:T(8,128)(2,1)S(1)}, bf16[256,512]{1,0:T(8,128)(2,1)S(1)}, bf16[256,512]{1,0:T(8,128)(2,1)S(1)}, bf16[256,512]{1,0:T(8,128)(2,1)S(1)}) custom-call(s32[2]{0:T(128)S(1)} %get-tuple-element.41.place_ref.pos_ref, bf16[16,256,1024]{2,1,0:T(8,128)(2,1)S(1)} %get-tuple-element.44.x_ref, s32[128,512]{1,0:T(8,128)S(1)} %copy-done.1, ...), custom_call_target="tpu_custom_call" | custom-call | flops 6442450944 | bytes 7340032 | tf_op jit(solution)/shard_map/transform/pallas_call | solution.py:101
  32.8 4.6 %collective-permute-done.1.refs_2_ = bf16[256,512]{1,0:T(8,128)(2,1)S(1)} collective-permute-done((bf16[256,512]{1,0:T(8,128)(2,1)S(1)}, bf16[256,512]{1,0:T(8,128)(2,1)S(1)}, u32[]{:S(2)}, u32[]{:S(2)}) %collective-permute-start.1) | collective-permute-done | bytes 262176 | tf_op jit(solution)/shard_map/ppermute | solution.py:455
  39.4 4.2 %collective-permute-start.7 = (bf16[1024,512]{1,0:T(8,128)(2,1)S(1)}, bf16[1024,512]{1,0:T(8,128)(2,1)S(1)}, u32[]{:S(2)}, u32[]{:S(2)}) collective-permute-start(bf16[1024,512]{1,0:T(8,128)(2,1)S(1)} %join.4.refs_0_.own_ref), channel_id=1, source_target_pairs={{4,1},{6,3},{0,5},{2,7},{12,9},{14,11},{8,13},{10,15},{20,17},{22,... | collective-permute-start | bytes 3145736 | tf_op jit(solution)/shard_map/ppermute | solution.py:485
  47.9 2.8 %collective-permute-start.6 = (bf16[256,512]{1,0:T(8,128)(2,1)S(1)}, bf16[256,512]{1,0:T(8,128)(2,1)S(1)}, u32[]{:S(2)}, u32[]{:S(2)}) collective-permute-start(bf16[256,512]{1,0:T(8,128)(2,1)S(1)} %get-tuple-element.48), channel_id=1, source_target_pairs={{0,24},{8,0},{16,8},{24,16},{1,25},{9,1},{17,9},{25,17},{2,26},{10... | collective-permute-start | bytes 786440 | tf_op jit(solution)/shard_map/ppermute | solution.py:455
  51.7 8.9 %transform.12 = (bf16[256,512]{1,0:T(8,128)(2,1)S(1)}, bf16[256,512]{1,0:T(8,128)(2,1)S(1)}, bf16[256,512]{1,0:T(8,128)(2,1)S(1)}, bf16[256,512]{1,0:T(8,128)(2,1)S(1)}) custom-call(s32[2]{0:T(128)S(1)} %get-tuple-element.41.place_ref.pos_ref, bf16[16,256,1024]{2,1,0:T(8,128)(2,1)S(1)} %get-tuple-element.44.x_ref, s32[128,512]{1,0:T(8,128)S(1)} %copy-done.1, ...), custom_call_target="tpu_custom_call" | custom-call | flops 6442450944 | bytes 7340032 | tf_op jit(solution)/shard_map/transform/pallas_call | solution.py:101
  60.6 3.6 %collective-permute-done.5.refs_2_ = bf16[256,512]{1,0:T(8,128)(2,1)S(1)} collective-permute-done((bf16[256,512]{1,0:T(8,128)(2,1)S(1)}, bf16[256,512]{1,0:T(8,128)(2,1)S(1)}, u32[]{:S(2)}, u32[]{:S(2)}) %collective-permute-start.5) | collective-permute-done | bytes 262176 | tf_op jit(solution)/shard_map/ppermute | solution.py:455
  66.4 5.6 %collective-permute-start.8 = (bf16[1280,512]{1,0:T(8,128)(2,1)S(1)}, bf16[1280,512]{1,0:T(8,128)(2,1)S(1)}, u32[]{:S(2)}, u32[]{:S(2)}) collective-permute-start(bf16[1280,512]{1,0:T(8,128)(2,1)S(1)} %get-tuple-element.50), channel_id=1, source_target_pairs={{4,1},{6,3},{0,5},{2,7},{5,6},{1,2},{12,9},{14,11},{8,13},{10,15},... | collective-permute-start | bytes 3932168 | tf_op jit(solution)/shard_map/ppermute | solution.py:485
  72.0 4.2 %collective-permute-start.10 = (bf16[256,512]{1,0:T(8,128)(2,1)S(1)}, bf16[256,512]{1,0:T(8,128)(2,1)S(1)}, u32[]{:S(2)}, u32[]{:S(2)}) collective-permute-start(bf16[256,512]{1,0:T(8,128)(2,1)S(1)} %get-tuple-element.52), channel_id=1, source_target_pairs={{0,16},{8,24},{16,0},{24,8},{1,17},{9,25},{17,1},{25,9},{2,18},{10... | collective-permute-start | bytes 786440 | tf_op jit(solution)/shard_map/ppermute | solution.py:455
  78.2 8.8 %transform.13 = (bf16[256,512]{1,0:T(8,128)(2,1)S(1)}, bf16[256,512]{1,0:T(8,128)(2,1)S(1)}, bf16[256,512]{1,0:T(8,128)(2,1)S(1)}, bf16[256,512]{1,0:T(8,128)(2,1)S(1)}) custom-call(s32[2]{0:T(128)S(1)} %get-tuple-element.41.place_ref.pos_ref, bf16[16,256,1024]{2,1,0:T(8,128)(2,1)S(1)} %get-tuple-element.44.x_ref, s32[128,512]{1,0:T(8,128)S(1)} %copy-done.1, ...), custom_call_target="tpu_custom_call" | custom-call | flops 6442450944 | bytes 7340032 | tf_op jit(solution)/shard_map/transform/pallas_call | solution.py:101
  89.0 5.8 %collective-permute-done.9.refs_0_ = bf16[256,512]{1,0:T(8,128)(2,1)S(1)} collective-permute-done((bf16[256,512]{1,0:T(8,128)(2,1)S(1)}, bf16[256,512]{1,0:T(8,128)(2,1)S(1)}, u32[]{:S(2)}, u32[]{:S(2)}) %collective-permute-start.9) | collective-permute-done | bytes 262176 | tf_op jit(solution)/shard_map/ppermute | solution.py:455
  94.8 3.3 %collective-permute-done.12.refs_3_.refs_5_.near_ref = bf16[1280,512]{1,0:T(8,128)(2,1)S(1)} collective-permute-done((bf16[1280,512]{1,0:T(8,128)(2,1)S(1)}, bf16[1280,512]{1,0:T(8,128)(2,1)S(1)}, u32[]{:S(2)}, u32[]{:S(2)}) %collective-permute-start.12) | collective-permute-done | bytes 1310752 | tf_op jit(solution)/shard_map/ppermute | solution.py:484
  102.9 4.1 %collective-permute-start.14 = (bf16[256,512]{1,0:T(8,128)(2,1)S(1)}, bf16[256,512]{1,0:T(8,128)(2,1)S(1)}, u32[]{:S(2)}, u32[]{:S(2)}) collective-permute-start(bf16[256,512]{1,0:T(8,128)(2,1)S(1)} %get-tuple-element.57), channel_id=1, source_target_pairs={{0,8},{8,16},{16,24},{24,0},{1,9},{9,17},{17,25},{25,1},{2,10},{10... | collective-permute-start | bytes 786440 | tf_op jit(solution)/shard_map/ppermute | solution.py:455
  110.1 6.6 %collective-permute-done.13.late_ref.refs_4_.refs_10_ = bf16[1280,512]{1,0:T(8,128)(2,1)S(1)} collective-permute-done((bf16[1280,512]{1,0:T(8,128)(2,1)S(1)}, bf16[1280,512]{1,0:T(8,128)(2,1)S(1)}, u32[]{:S(2)}, u32[]{:S(2)}) %collective-permute-start.13) | collective-permute-done | bytes 1310752 | tf_op jit(solution)/shard_map/ppermute | solution.py:485
  117.4 9.0 %collective-permute-done.15.refs_1_ = bf16[256,512]{1,0:T(8,128)(2,1)S(1)} collective-permute-done((bf16[256,512]{1,0:T(8,128)(2,1)S(1)}, bf16[256,512]{1,0:T(8,128)(2,1)S(1)}, u32[]{:S(2)}, u32[]{:S(2)}) %collective-permute-start.15) | collective-permute-done | bytes 262176 | tf_op jit(solution)/shard_map/ppermute | solution.py:455
  129.3 3.5 %collective-permute-start.20 = (bf16[768,512]{1,0:T(8,128)(2,1)S(1)}, bf16[768,512]{1,0:T(8,128)(2,1)S(1)}, u32[]{:S(2)}, u32[]{:S(2)}) collective-permute-start(bf16[768,512]{1,0:T(8,128)(2,1)S(1)} %join.7.own_ref), channel_id=1, source_target_pairs={{4,1},{6,3},{0,5},{2,7},{12,9},{14,11},{8,13},{10,15},{20,17},{22,... | collective-permute-start | bytes 2359304 | tf_op jit(solution)/shard_map/ppermute | solution.py:485
  135.1 7.1 %collective-permute-done.20.refs_11_ = bf16[768,512]{1,0:T(8,128)(2,1)S(1)} collective-permute-done((bf16[768,512]{1,0:T(8,128)(2,1)S(1)}, bf16[768,512]{1,0:T(8,128)(2,1)S(1)}, u32[]{:S(2)}, u32[]{:S(2)}) %collective-permute-start.20) | collective-permute-done | bytes 786464 | tf_op jit(solution)/shard_map/ppermute | solution.py:485
  143.8 3.9 %collective-permute-start.22 = (bf16[2,1024,512]{2,1,0:T(8,128)(2,1)S(1)}, bf16[2,1024,512]{2,1,0:T(8,128)(2,1)S(1)}, u32[]{:S(2)}, u32[]{:S(2)}) collective-permute-start(bf16[2,1024,512]{2,1,0:T(8,128)(2,1)S(1)} %pick.4.refs_0_), channel_id=1, source_target_pairs={{0,1},{1,0},{2,3},{3,2},{4,5},{5,4},{6,7},{7,6},{8,9},{9,8},{10,11... | collective-permute-start | bytes 6291464 | tf_op jit(solution)/shard_map/ppermute | solution.py:499
  148.7 7.2 %collective-permute-done.19.near_ref = bf16[768,512]{1,0:T(8,128)(2,1)S(1)} collective-permute-done((bf16[768,512]{1,0:T(8,128)(2,1)S(1)}, bf16[768,512]{1,0:T(8,128)(2,1)S(1)}, u32[]{:S(2)}, u32[]{:S(2)}) %collective-permute-start.19) | collective-permute-done | bytes 786464 | tf_op jit(solution)/shard_map/ppermute | solution.py:484
  156.7 4.5 %collective-permute-start.25 = (bf16[2,768,512]{2,1,0:T(8,128)(2,1)S(1)}, bf16[2,768,512]{2,1,0:T(8,128)(2,1)S(1)}, u32[]{:S(2)}, u32[]{:S(2)}) collective-permute-start(bf16[2,768,512]{2,1,0:T(8,128)(2,1)S(1)} %pick.7.refs_3_), channel_id=1, source_target_pairs={{0,1},{1,0},{2,3},{3,2},{4,5},{5,4},{6,7},{7,6},{8,9},{9,8},{10,11... | collective-permute-start | bytes 4718600 | tf_op jit(solution)/shard_map/ppermute | solution.py:499
  164.2 5.2 %pairs.7 = (bf16[256,512]{1,0:T(8,128)(2,1)S(1)}, bf16[256,512]{1,0:T(8,128)(2,1)S(1)}, bf16[256,512]{1,0:T(8,128)(2,1)S(1)}, bf16[256,512]{1,0:T(8,128)(2,1)S(1)}) custom-call(s32[1,1]{1,0:T(1,128)} %copy.10.live_ref, s32[16]{0:T(128)S(1)} %bitcast.9, s32[2]{0:T(128)S(1)} %get-tuple-element.41.place_ref.pos_ref, f32[128]{0:T(128)S(1)} %copy-done.3, ...), custom_call_target="tpu_custom_call" | custom-call | flops 4294967296 | bytes 3145728 | tf_op jit(solution)/shard_map/pairs/pallas_call | solution.py:375
  169.4 5.2 %collective-permute-start.35 = (bf16[256,512]{1,0:T(8,128)(2,1)S(1)}, bf16[256,512]{1,0:T(8,128)(2,1)S(1)}, u32[]{:S(2)}, u32[]{:S(2)}) collective-permute-start(bf16[256,512]{1,0:T(8,128)(2,1)S(1)} %get-tuple-element.74), channel_id=1, source_target_pairs={{0,24},{8,0},{16,8},{24,16},{1,25},{9,1},{17,9},{25,17},{2,26},{10... | collective-permute-start | bytes 786440 | tf_op jit(solution)/shard_map/ppermute | solution.py:455
  175.2 8.6 %pairs.6 = (bf16[256,512]{1,0:T(8,128)(2,1)S(1)}, bf16[256,512]{1,0:T(8,128)(2,1)S(1)}, bf16[256,512]{1,0:T(8,128)(2,1)S(1)}, bf16[256,512]{1,0:T(8,128)(2,1)S(1)}) custom-call(s32[1,1]{1,0:T(1,128)} %copy.10.live_ref, s32[16]{0:T(128)S(1)} %bitcast.10, s32[2]{0:T(128)S(1)} %get-tuple-element.41.place_ref.pos_ref, f32[128]{0:T(128)S(1)} %copy-done.3, ...), custom_call_target="tpu_custom_call" | custom-call | flops 4294967296 | bytes 3145728 | tf_op jit(solution)/shard_map/pairs/pallas_call | solution.py:375
  183.9 9.1 %pairs.5 = (bf16[256,512]{1,0:T(8,128)(2,1)S(1)}, bf16[256,512]{1,0:T(8,128)(2,1)S(1)}, bf16[256,512]{1,0:T(8,128)(2,1)}, bf16[256,512]{1,0:T(8,128)(2,1)}) custom-call(s32[1,1]{1,0:T(1,128)} %copy.10.live_ref, s32[16]{0:T(128)S(1)} %bitcast.11, s32[2]{0:T(128)S(1)} %get-tuple-element.41.place_ref.pos_ref, f32[128]{0:T(128)S(1)} %copy-done.3, ...), custom_call_target="tpu_custom_call" | custom-call | flops 4294967296 | bytes 3145728 | tf_op jit(solution)/shard_map/pairs/pallas_call | solution.py:375
  193.1 2.8 %collective-permute-done.36.refs_14_ = bf16[256,512]{1,0:T(8,128)(2,1)S(1)} collective-permute-done((bf16[256,512]{1,0:T(8,128)(2,1)S(1)}, bf16[256,512]{1,0:T(8,128)(2,1)S(1)}, u32[]{:S(2)}, u32[]{:S(2)}) %collective-permute-start.36) | collective-permute-done | bytes 262176 | tf_op jit(solution)/shard_map/ppermute | solution.py:455
  196.9 12.3 %pairs.4 = (bf16[256,512]{1,0:T(8,128)(2,1)S(1)}, bf16[256,512]{1,0:T(8,128)(2,1)}, bf16[256,512]{1,0:T(8,128)(2,1)}, bf16[256,512]{1,0:T(8,128)(2,1)}) custom-call(s32[1,1]{1,0:T(1,128)} %copy.10.live_ref, s32[16]{0:T(128)S(1)} %bitcast.12, s32[2]{0:T(128)S(1)} %get-tuple-element.41.place_ref.pos_ref, f32[128]{0:T(128)S(1)} %copy-done.3, ...), custom_call_target="tpu_custom_call" | custom-call | flops 4294967296 | bytes 3145728 | tf_op jit(solution)/shard_map/pairs/pallas_call | solution.py:375
  209.2 2.9 %collective-permute-start.30 = (bf16[256,512]{1,0:T(8,128)(2,1)}, bf16[256,512]{1,0:T(8,128)(2,1)S(1)}, u32[]{:S(2)}, u32[]{:S(2)}) collective-permute-start(bf16[256,512]{1,0:T(8,128)(2,1)} %get-tuple-element.67), channel_id=1, source_target_pairs={{0,16},{8,24},{16,0},{24,8},{1,17},{9,25},{17,1},{25,9},{2,18},{10... | collective-permute-start | bytes 786440 | tf_op jit(solution)/shard_map/ppermute | solution.py:455
  213.3 16.3 %collective-permute-done.33.refs_10_ = bf16[256,512]{1,0:T(8,128)(2,1)S(1)} collective-permute-done((bf16[256,512]{1,0:T(8,128)(2,1)S(1)}, bf16[256,512]{1,0:T(8,128)(2,1)S(1)}, u32[]{:S(2)}, u32[]{:S(2)}) %collective-permute-start.33) | collective-permute-done | bytes 262176 | tf_op jit(solution)/shard_map/ppermute | solution.py:455
  229.7 10.3 %collective-permute-start.27 = (bf16[256,512]{1,0:T(8,128)(2,1)}, bf16[256,512]{1,0:T(8,128)(2,1)}, u32[]{:S(2)}, u32[]{:S(2)}) collective-permute-start(bf16[256,512]{1,0:T(8,128)(2,1)} %get-tuple-element.63), channel_id=1, source_target_pairs={{0,16},{8,24},{16,0},{24,8},{1,17},{9,25},{17,1},{25,9},{2,18},{10... | collective-permute-start | bytes 786440 | tf_op jit(solution)/shard_map/ppermute | solution.py:455
  241.6 21.1 %all-reduce = s32[68]{0:T(128)S(1)} all-reduce(s32[68]{0:T(128)S(1)} %add_dynamic-update-slice_fusion), channel_id=2, replica_groups=mesh['aux'=4,'occ'=8] {'aux'}, use_global_device_ids=true, to_apply=%add | all-reduce | flops 68 | bytes 544
  263.1 5.9 %assemble.1 = bf16[256,16,512]{2,1,0:T(8,128)(2,1)} custom-call(s32[2]{0:T(128)S(1)} %get-tuple-element.41.place_ref.pos_ref, s32[4]{0:T(128)S(1)} %slice_reduce_fusion.live_ref, s32[4,16]{1,0:T(4,128)S(1)} %bitcast.8, bf16[256,512]{1,0:T(8,128)(2,1)S(1)} %get-tuple-element.61.refs_0_, bf16[256,512]{1,0:T(8,128)(2,1)} %collective-permute-done.26.refs_1_, ...), custom_call_target="tpu_custom_call" | custom-call | flops 1073741824 | bytes 8388608 | tf_op jit(solution)/shard_map/assemble/pallas_call | solution.py:428
  (86 shorter events, 49.2 us)
Async XLA Ops:
  10.0 22.9 %collective-permute-start.2 = (bf16[256,512]{1,0:T(8,128)(2,1)S(1)}, bf16[256,512]{1,0:T(8,128)(2,1)S(1)}, u32[]{:S(2)}, u32[]{:S(2)}) collective-permute-start(bf16[256,512]{1,0:T(8,128)(2,1)S(1)} %transform.10), channel_id=1, source_target_pairs={{0,24},{8,0},{16,8},{24,16},{1,25},{9,1},{17,9},{25,17},{2,26},{10... | collective-permute-start | bytes 786440 | tf_op jit(solution)/shard_map/ppermute | solution.py:455
  17.6 19.8 %collective-permute-start.1 = (bf16[256,512]{1,0:T(8,128)(2,1)S(1)}, bf16[256,512]{1,0:T(8,128)(2,1)S(1)}, u32[]{:S(2)}, u32[]{:S(2)}) collective-permute-start(bf16[256,512]{1,0:T(8,128)(2,1)S(1)} %transform.9), channel_id=1, source_target_pairs={{0,16},{8,24},{16,0},{24,8},{1,17},{9,25},{17,1},{25,9},{2,18},{10... | collective-permute-start | bytes 786440 | tf_op jit(solution)/shard_map/ppermute | solution.py:455
  20.3 17.1 %collective-permute-start = (bf16[256,512]{1,0:T(8,128)(2,1)S(1)}, bf16[256,512]{1,0:T(8,128)(2,1)S(1)}, u32[]{:S(2)}, u32[]{:S(2)}) collective-permute-start(bf16[256,512]{1,0:T(8,128)(2,1)S(1)} %transform.8), channel_id=1, source_target_pairs={{0,8},{8,16},{16,24},{24,0},{1,9},{9,17},{17,25},{25,1},{2,10},{10... | collective-permute-start | bytes 786440 | tf_op jit(solution)/shard_map/ppermute | solution.py:455
  38.1 26.3 %collective-permute-start.3 = (bf16[1024,512]{1,0:T(8,128)(2,1)S(1)}, bf16[1024,512]{1,0:T(8,128)(2,1)S(1)}, u32[]{:S(2)}, u32[]{:S(2)}) collective-permute-start(bf16[1024,512]{1,0:T(8,128)(2,1)S(1)} %join.4.refs_0_.own_ref), channel_id=1, source_target_pairs={{1,7},{2,0},{3,1},{5,3},{6,4},{7,5},{9,15},{10,8},{11,9},{13,11},{... | collective-permute-start | bytes 3145736 | tf_op jit(solution)/shard_map/ppermute | solution.py:484
  39.4 25.0 %collective-permute-start.7 = (bf16[1024,512]{1,0:T(8,128)(2,1)S(1)}, bf16[1024,512]{1,0:T(8,128)(2,1)S(1)}, u32[]{:S(2)}, u32[]{:S(2)}) collective-permute-start(bf16[1024,512]{1,0:T(8,128)(2,1)S(1)} %join.4.refs_0_.own_ref), channel_id=1, source_target_pairs={{4,1},{6,3},{0,5},{2,7},{12,9},{14,11},{8,13},{10,15},{20,17},{22,... | collective-permute-start | bytes 3145736 | tf_op jit(solution)/shard_map/ppermute | solution.py:485
  43.6 17.0 %collective-permute-start.4 = (bf16[256,512]{1,0:T(8,128)(2,1)S(1)}, bf16[256,512]{1,0:T(8,128)(2,1)S(1)}, u32[]{:S(2)}, u32[]{:S(2)}) collective-permute-start(bf16[256,512]{1,0:T(8,128)(2,1)S(1)} %get-tuple-element.46), channel_id=1, source_target_pairs={{0,8},{8,16},{16,24},{24,0},{1,9},{9,17},{17,25},{25,1},{2,10},{10... | collective-permute-start | bytes 786440 | tf_op jit(solution)/shard_map/ppermute | solution.py:455
  45.9 18.3 %collective-permute-start.5 = (bf16[256,512]{1,0:T(8,128)(2,1)S(1)}, bf16[256,512]{1,0:T(8,128)(2,1)S(1)}, u32[]{:S(2)}, u32[]{:S(2)}) collective-permute-start(bf16[256,512]{1,0:T(8,128)(2,1)S(1)} %get-tuple-element.47), channel_id=1, source_target_pairs={{0,16},{8,24},{16,0},{24,8},{1,17},{9,25},{17,1},{25,9},{2,18},{10... | collective-permute-start | bytes 786440 | tf_op jit(solution)/shard_map/ppermute | solution.py:455
  47.9 16.3 %collective-permute-start.6 = (bf16[256,512]{1,0:T(8,128)(2,1)S(1)}, bf16[256,512]{1,0:T(8,128)(2,1)S(1)}, u32[]{:S(2)}, u32[]{:S(2)}) collective-permute-start(bf16[256,512]{1,0:T(8,128)(2,1)S(1)} %get-tuple-element.48), channel_id=1, source_target_pairs={{0,24},{8,0},{16,8},{24,16},{1,25},{9,1},{17,9},{25,17},{2,26},{10... | collective-permute-start | bytes 786440 | tf_op jit(solution)/shard_map/ppermute | solution.py:455
  65.1 33.0 %collective-permute-start.12 = (bf16[1280,512]{1,0:T(8,128)(2,1)S(1)}, bf16[1280,512]{1,0:T(8,128)(2,1)S(1)}, u32[]{:S(2)}, u32[]{:S(2)}) collective-permute-start(bf16[1280,512]{1,0:T(8,128)(2,1)S(1)} %get-tuple-element.54.refs_0_.own_ref), channel_id=1, source_target_pairs={{1,7},{2,0},{3,1},{5,3},{6,4},{7,5},{9,15},{10,8},{11,9},{13,11},{... | collective-permute-start | bytes 3932168 | tf_op jit(solution)/shard_map/ppermute | solution.py:484
  66.4 31.7 %collective-permute-start.8 = (bf16[1280,512]{1,0:T(8,128)(2,1)S(1)}, bf16[1280,512]{1,0:T(8,128)(2,1)S(1)}, u32[]{:S(2)}, u32[]{:S(2)}) collective-permute-start(bf16[1280,512]{1,0:T(8,128)(2,1)S(1)} %get-tuple-element.50), channel_id=1, source_target_pairs={{4,1},{6,3},{0,5},{2,7},{5,6},{1,2},{12,9},{14,11},{8,13},{10,15},... | collective-permute-start | bytes 3932168 | tf_op jit(solution)/shard_map/ppermute | solution.py:485
  72.0 17.0 %collective-permute-start.10 = (bf16[256,512]{1,0:T(8,128)(2,1)S(1)}, bf16[256,512]{1,0:T(8,128)(2,1)S(1)}, u32[]{:S(2)}, u32[]{:S(2)}) collective-permute-start(bf16[256,512]{1,0:T(8,128)(2,1)S(1)} %get-tuple-element.52), channel_id=1, source_target_pairs={{0,16},{8,24},{16,0},{24,8},{1,17},{9,25},{17,1},{25,9},{2,18},{10... | collective-permute-start | bytes 786440 | tf_op jit(solution)/shard_map/ppermute | solution.py:455
  77.7 17.1 %collective-permute-start.9 = (bf16[256,512]{1,0:T(8,128)(2,1)S(1)}, bf16[256,512]{1,0:T(8,128)(2,1)S(1)}, u32[]{:S(2)}, u32[]{:S(2)}) collective-permute-start(bf16[256,512]{1,0:T(8,128)(2,1)S(1)} %get-tuple-element.51), channel_id=1, source_target_pairs={{0,8},{8,16},{16,24},{24,0},{1,9},{9,17},{17,25},{25,1},{2,10},{10... | collective-permute-start | bytes 786440 | tf_op jit(solution)/shard_map/ppermute | solution.py:455
  98.8 17.8 %collective-permute-start.13 = (bf16[1280,512]{1,0:T(8,128)(2,1)S(1)}, bf16[1280,512]{1,0:T(8,128)(2,1)S(1)}, u32[]{:S(2)}, u32[]{:S(2)}) collective-permute-start(bf16[1280,512]{1,0:T(8,128)(2,1)S(1)} %get-tuple-element.56), channel_id=1, source_target_pairs={{4,1},{6,3},{0,5},{2,7},{5,6},{1,2},{12,9},{14,11},{8,13},{10,15},... | collective-permute-start | bytes 3932168 | tf_op jit(solution)/shard_map/ppermute | solution.py:485
  101.6 27.0 %collective-permute-start.17 = (bf16[1024,512]{1,0:T(8,128)(2,1)S(1)}, bf16[1024,512]{1,0:T(8,128)(2,1)S(1)}, u32[]{:S(2)}, u32[]{:S(2)}) collective-permute-start(bf16[1024,512]{1,0:T(8,128)(2,1)S(1)} %get-tuple-element.60.own_ref), channel_id=1, source_target_pairs={{1,7},{2,0},{3,1},{5,3},{6,4},{7,5},{9,15},{10,8},{11,9},{13,11},{... | collective-permute-start | bytes 3145736 | tf_op jit(solution)/shard_map/ppermute | solution.py:484
  107.1 19.3 %collective-permute-start.15 = (bf16[256,512]{1,0:T(8,128)(2,1)S(1)}, bf16[256,512]{1,0:T(8,128)(2,1)S(1)}, u32[]{:S(2)}, u32[]{:S(2)}) collective-permute-start(bf16[256,512]{1,0:T(8,128)(2,1)S(1)} %get-tuple-element.58), channel_id=1, source_target_pairs={{0,16},{8,24},{16,0},{24,8},{1,17},{9,25},{17,1},{25,9},{2,18},{10... | collective-permute-start | bytes 786440 | tf_op jit(solution)/shard_map/ppermute | solution.py:455
  108.6 17.8 %collective-permute-start.16 = (bf16[256,512]{1,0:T(8,128)(2,1)S(1)}, bf16[256,512]{1,0:T(8,128)(2,1)S(1)}, u32[]{:S(2)}, u32[]{:S(2)}) collective-permute-start(bf16[256,512]{1,0:T(8,128)(2,1)S(1)} %get-tuple-element.59), channel_id=1, source_target_pairs={{0,24},{8,0},{16,8},{24,16},{1,25},{9,1},{17,9},{25,17},{2,26},{10... | collective-permute-start | bytes 786440 | tf_op jit(solution)/shard_map/ppermute | solution.py:455
  116.7 31.0 %collective-permute-start.18 = (bf16[1280,512]{1,0:T(8,128)(2,1)S(1)}, bf16[1280,512]{1,0:T(8,128)(2,1)S(1)}, u32[]{:S(2)}, u32[]{:S(2)}) collective-permute-start(bf16[1280,512]{1,0:T(8,128)(2,1)S(1)} %collective-permute-done.13.late_ref.refs_4_.refs_10_), channel_id=1, source_target_pairs={{5,6},{1,2},{13,14},{9,10},{21,22},{17,18},{29,30},{25,26}} | collective-permute-start | bytes 3932168 | tf_op jit(solution)/shard_map/ppermute | solution.py:492
  133.7 28.1 %collective-permute-start.23 = (bf16[2,1280,512]{2,1,0:T(8,128)(2,1)S(1)}, bf16[2,1280,512]{2,1,0:T(8,128)(2,1)S(1)}, u32[]{:S(2)}, u32[]{:S(2)}) collective-permute-start(bf16[2,1280,512]{2,1,0:T(8,128)(2,1)S(1)} %pick.5.refs_1_), channel_id=1, source_target_pairs={{0,1},{1,0},{2,3},{3,2},{4,5},{5,4},{6,7},{7,6},{8,9},{9,8},{10,11... | collective-permute-start | bytes 7864328 | tf_op jit(solution)/shard_map/ppermute | solution.py:499
  133.8 22.1 %collective-permute-start.19 = (bf16[768,512]{1,0:T(8,128)(2,1)S(1)}, bf16[768,512]{1,0:T(8,128)(2,1)S(1)}, u32[]{:S(2)}, u32[]{:S(2)}) collective-permute-start(bf16[768,512]{1,0:T(8,128)(2,1)S(1)} %join.7.own_ref), channel_id=1, source_target_pairs={{1,7},{2,0},{3,1},{5,3},{6,4},{7,5},{9,15},{10,8},{11,9},{13,11},{... | collective-permute-start | bytes 2359304 | tf_op jit(solution)/shard_map/ppermute | solution.py:484
  143.8 18.0 %collective-permute-start.22 = (bf16[2,1024,512]{2,1,0:T(8,128)(2,1)S(1)}, bf16[2,1024,512]{2,1,0:T(8,128)(2,1)S(1)}, u32[]{:S(2)}, u32[]{:S(2)}) collective-permute-start(bf16[2,1024,512]{2,1,0:T(8,128)(2,1)S(1)} %pick.4.refs_0_), channel_id=1, source_target_pairs={{0,1},{1,0},{2,3},{3,2},{4,5},{5,4},{6,7},{7,6},{8,9},{9,8},{10,11... | collective-permute-start | bytes 6291464 | tf_op jit(solution)/shard_map/ppermute | solution.py:499
  169.4 23.6 %collective-permute-start.35 = (bf16[256,512]{1,0:T(8,128)(2,1)S(1)}, bf16[256,512]{1,0:T(8,128)(2,1)S(1)}, u32[]{:S(2)}, u32[]{:S(2)}) collective-permute-start(bf16[256,512]{1,0:T(8,128)(2,1)S(1)} %get-tuple-element.74), channel_id=1, source_target_pairs={{0,24},{8,0},{16,8},{24,16},{1,25},{9,1},{17,9},{25,17},{2,26},{10... | collective-permute-start | bytes 786440 | tf_op jit(solution)/shard_map/ppermute | solution.py:455
  174.6 21.3 %collective-permute-start.36 = (bf16[256,512]{1,0:T(8,128)(2,1)S(1)}, bf16[256,512]{1,0:T(8,128)(2,1)S(1)}, u32[]{:S(2)}, u32[]{:S(2)}) collective-permute-start(bf16[256,512]{1,0:T(8,128)(2,1)S(1)} %get-tuple-element.75), channel_id=1, source_target_pairs={{0,16},{8,24},{16,0},{24,8},{1,17},{9,25},{17,1},{25,9},{2,18},{10... | collective-permute-start | bytes 786440 | tf_op jit(solution)/shard_map/ppermute | solution.py:455
  174.6 34.6 %collective-permute-start.37 = (bf16[256,512]{1,0:T(8,128)(2,1)S(1)}, bf16[256,512]{1,0:T(8,128)(2,1)S(1)}, u32[]{:S(2)}, u32[]{:S(2)}) collective-permute-start(bf16[256,512]{1,0:T(8,128)(2,1)S(1)} %get-tuple-element.76), channel_id=1, source_target_pairs={{0,8},{8,16},{16,24},{24,0},{1,9},{9,17},{17,25},{25,1},{2,10},{10... | collective-permute-start | bytes 786440 | tf_op jit(solution)/shard_map/ppermute | solution.py:455
  183.8 28.3 %collective-permute-start.32 = (bf16[256,512]{1,0:T(8,128)(2,1)S(1)}, bf16[256,512]{1,0:T(8,128)(2,1)S(1)}, u32[]{:S(2)}, u32[]{:S(2)}) collective-permute-start(bf16[256,512]{1,0:T(8,128)(2,1)S(1)} %get-tuple-element.70), channel_id=1, source_target_pairs={{0,24},{8,0},{16,8},{24,16},{1,25},{9,1},{17,9},{25,17},{2,26},{10... | collective-permute-start | bytes 786440 | tf_op jit(solution)/shard_map/ppermute | solution.py:455
  183.9 45.8 %collective-permute-start.33 = (bf16[256,512]{1,0:T(8,128)(2,1)S(1)}, bf16[256,512]{1,0:T(8,128)(2,1)S(1)}, u32[]{:S(2)}, u32[]{:S(2)}) collective-permute-start(bf16[256,512]{1,0:T(8,128)(2,1)S(1)} %get-tuple-element.71), channel_id=1, source_target_pairs={{0,16},{8,24},{16,0},{24,8},{1,17},{9,25},{17,1},{25,9},{2,18},{10... | collective-permute-start | bytes 786440 | tf_op jit(solution)/shard_map/ppermute | solution.py:455
  193.0 36.7 %collective-permute-start.34 = (bf16[256,512]{1,0:T(8,128)(2,1)S(1)}, bf16[256,512]{1,0:T(8,128)(2,1)S(1)}, u32[]{:S(2)}, u32[]{:S(2)}) collective-permute-start(bf16[256,512]{1,0:T(8,128)(2,1)S(1)} %get-tuple-element.72), channel_id=1, source_target_pairs={{0,8},{8,16},{16,24},{24,0},{1,9},{9,17},{17,25},{25,1},{2,10},{10... | collective-permute-start | bytes 786440 | tf_op jit(solution)/shard_map/ppermute | solution.py:455
  195.9 44.1 %collective-permute-start.29 = (bf16[256,512]{1,0:T(8,128)(2,1)S(1)}, bf16[256,512]{1,0:T(8,128)(2,1)S(1)}, u32[]{:S(2)}, u32[]{:S(2)}) collective-permute-start(bf16[256,512]{1,0:T(8,128)(2,1)S(1)} %get-tuple-element.66), channel_id=1, source_target_pairs={{0,24},{8,0},{16,8},{24,16},{1,25},{9,1},{17,9},{25,17},{2,26},{10... | collective-permute-start | bytes 786440 | tf_op jit(solution)/shard_map/ppermute | solution.py:455
  209.2 53.8 %collective-permute-start.30 = (bf16[256,512]{1,0:T(8,128)(2,1)}, bf16[256,512]{1,0:T(8,128)(2,1)S(1)}, u32[]{:S(2)}, u32[]{:S(2)}) collective-permute-start(bf16[256,512]{1,0:T(8,128)(2,1)} %get-tuple-element.67), channel_id=1, source_target_pairs={{0,16},{8,24},{16,0},{24,8},{1,17},{9,25},{17,1},{25,9},{2,18},{10... | collective-permute-start | bytes 786440 | tf_op jit(solution)/shard_map/ppermute | solution.py:455
  212.1 50.9 %collective-permute-start.31 = (bf16[256,512]{1,0:T(8,128)(2,1)}, bf16[256,512]{1,0:T(8,128)(2,1)S(1)}, u32[]{:S(2)}, u32[]{:S(2)}) collective-permute-start(bf16[256,512]{1,0:T(8,128)(2,1)} %get-tuple-element.68), channel_id=1, source_target_pairs={{0,8},{8,16},{16,24},{24,0},{1,9},{9,17},{17,25},{25,1},{2,10},{10... | collective-permute-start | bytes 786440 | tf_op jit(solution)/shard_map/ppermute | solution.py:455
  229.6 33.4 %collective-permute-start.26 = (bf16[256,512]{1,0:T(8,128)(2,1)}, bf16[256,512]{1,0:T(8,128)(2,1)}, u32[]{:S(2)}, u32[]{:S(2)}) collective-permute-start(bf16[256,512]{1,0:T(8,128)(2,1)} %get-tuple-element.62), channel_id=1, source_target_pairs={{0,24},{8,0},{16,8},{24,16},{1,25},{9,1},{17,9},{25,17},{2,26},{10... | collective-permute-start | bytes 786440 | tf_op jit(solution)/shard_map/ppermute | solution.py:455
  229.7 33.3 %collective-permute-start.27 = (bf16[256,512]{1,0:T(8,128)(2,1)}, bf16[256,512]{1,0:T(8,128)(2,1)}, u32[]{:S(2)}, u32[]{:S(2)}) collective-permute-start(bf16[256,512]{1,0:T(8,128)(2,1)} %get-tuple-element.63), channel_id=1, source_target_pairs={{0,16},{8,24},{16,0},{24,8},{1,17},{9,25},{17,1},{25,9},{2,18},{10... | collective-permute-start | bytes 786440 | tf_op jit(solution)/shard_map/ppermute | solution.py:455
  240.1 23.0 %collective-permute-start.28 = (bf16[256,512]{1,0:T(8,128)(2,1)}, bf16[256,512]{1,0:T(8,128)(2,1)}, u32[]{:S(2)}, u32[]{:S(2)}) collective-permute-start(bf16[256,512]{1,0:T(8,128)(2,1)} %get-tuple-element.64), channel_id=1, source_target_pairs={{0,8},{8,16},{16,24},{24,0},{1,9},{9,17},{17,25},{25,1},{2,10},{10... | collective-permute-start | bytes 786440 | tf_op jit(solution)/shard_map/ppermute | solution.py:455
  (13 other events, 184.4 us)

commit v5 on v4

--- a/solution.py
+++ b/solution.py
@@ -211,7 +211,9 @@
     return block * OCC_DEV + slot % OCC_DEV
 
 
-def energy_kernel(aux_count, occ_count, place_ref, dom_ref, table_ref, row_ref, col_ref):
+def energy_kernel(aux_count, occ_count, place_ref, live_ref, code_ref, dom_ref, table_ref, row_ref, col_ref, order_ref):
+    for rank, orbital in enumerate(ranked(lambda slot: code_ref[slot], live_ref[0, 0], code_ref.shape[0])):
+        order_ref[rank] = orbital
     slots, _, virs = row_ref.shape
     lanes = table_ref.shape[1]
     rows = []
@@ -232,21 +234,22 @@
         col_ref[span, :] = total.T
 
 
-def energies(place, domains, vir_energy, aux_count, occ_count):
+def energies(place, live, codes, domains, vir_energy, aux_count, occ_count):
     slots, virs = PARTNERS * OCC_DEV, domains.shape[1]
-    vmem = pl.BlockSpec(memory_space=pltpu.VMEM)
+    vmem, smem = pl.BlockSpec(memory_space=pltpu.VMEM), pl.BlockSpec(memory_space=pltpu.SMEM)
     return pl.pallas_call(
         functools.partial(energy_kernel, aux_count, occ_count),
-        in_specs=[pl.BlockSpec(memory_space=pltpu.SMEM), vmem, vmem],
-        out_specs=[vmem, vmem],
+        in_specs=[smem, smem, smem, vmem, vmem],
+        out_specs=[vmem, vmem, smem],
         out_shape=[
             jax.ShapeDtypeStruct((slots, 1, virs), jnp.float32),
             jax.ShapeDtypeStruct((virs, slots), jnp.float32),
+            jax.ShapeDtypeStruct((OCC_DEV,), jnp.int32),
         ],
         compiler_params=pltpu.CompilerParams(vmem_limit_bytes=8 * MIB),
         cost_estimate=pl.CostEstimate(flops=0, bytes_accessed=4 * domains.size, transcendentals=0),
         name="energies",
-    )(place, domains, vir_energy.reshape(-1, 128))
+    )(place, live, codes, domains, vir_energy.reshape(-1, 128))
 
 
 def ranked(code_at, live, slots):
@@ -394,16 +397,8 @@
     )(live, codes, place, occ_energy, own_vir, vir_rows, *blocks)
 
 
-def spread_kernel(count, pos_ref, live_ref, code_ref, *refs):
-    *pieces, out, where_ref = refs
-
-    @pl.when(pl.program_id(0) == 0)
-    def _():
-        for owner in range(count):
-            order = ranked(lambda slot: code_ref[owner, slot], live_ref[owner], code_ref.shape[1])
-            for rank, orbital in enumerate(reversed(order)):
-                where_ref[owner * OCC_DEV + rank] = owner * OCC_DEV + orbital
-
+def spread_kernel(count, pos_ref, order_ref, *refs):
+    pieces, out = refs[:-1], refs[-1]
     orbitals = count * OCC_DEV
     width = orbitals * ROWS
     row = lax.broadcasted_iota(jnp.int32, (width, width), 0)
@@ -412,7 +407,8 @@
     place = jnp.zeros((1, width), jnp.int32)
     for number in range(orbitals):
         owner = lax.rem(pos_ref[0] + number % count, count)
-        place = jnp.where(group == number, where_ref[owner * OCC_DEV + number // count], place)
+        orbital = owner * OCC_DEV + order_ref[owner, OCC_DEV - 1 - number // count]
+        place = jnp.where(group == number, orbital, place)
     hit = jnp.where((row % orbitals == place) & (row // orbitals == col % ROWS), 1.0, 0.0).astype(jnp.bfloat16)
     for part in range(out.shape[0] // ROWS):
         span = pl.ds(part * ROWS, ROWS)
@@ -421,18 +417,17 @@
         out[span] = moved.reshape(ROWS, orbitals, -1)
 
 
-def assembled(pieces, aux_pos, count, live, codes):
+def assembled(pieces, aux_pos, count, orders):
     rows, virs = pieces[0].shape
     orbitals = count * OCC_DEV
     block = 4 * ROWS
     return pl.pallas_call(
         functools.partial(spread_kernel, count),
         grid_spec=pltpu.PrefetchScalarGridSpec(
-            num_scalar_prefetch=3,
+            num_scalar_prefetch=2,
             grid=(rows // block,),
             in_specs=[pl.BlockSpec((block, virs), lambda g, *_: (g, 0))] * len(pieces),
             out_specs=pl.BlockSpec((block, orbitals, virs), lambda g, *_: (g, 0, 0)),
-            scratch_shapes=[pltpu.SMEM((orbitals,), jnp.int32)],
         ),
         out_shape=jax.ShapeDtypeStruct((rows, orbitals, virs), jnp.bfloat16),
         compiler_params=pltpu.CompilerParams(vmem_limit_bytes=20 * MIB),
@@ -442,7 +437,7 @@
             transcendentals=0,
         ),
         name="assemble",
-    )(aux_pos, live, codes, *pieces)
+    )(aux_pos, orders, *pieces)
 
 
 def body(half_ints, block_mask, vir_coef, domains, vir_energy, occ_energy, pair_count, pair_code):
@@ -457,8 +452,9 @@
     rows_of, place = sorted_rows(
         half_ints, block_mask, aux_pos.astype(jnp.int32).reshape(1), occ_pos.astype(jnp.int32).reshape(1)
     )
-    vir_rows, vir_cols = energies(place, domains, vir_energy, aux_count, occ_count)
-    lists = lax.all_gather(jnp.concatenate([pair_code[0, 0], pair_count[0]]), "aux")
+    codes = pair_code[0, 0]
+    vir_rows, vir_cols, order = energies(place, pair_count, codes, domains, vir_energy, aux_count, occ_count)
+    orders = lax.all_gather(order, "aux")
     twin, direct, far, last, late = routes(occ_count)
     transform = functools.partial(transformed, rows_of, domains, vir_coef, place, aux_count)
 
@@ -507,7 +503,7 @@
             vir_cols, vir_rows, blocks,
         )
         results += [pieces[0]] + [along_aux(pieces[step], -step) for step in range(1, aux_count)]
-    return assembled(results, place, aux_count, lists[:, -1], lists[:, :-1])
+    return assembled(results, place, aux_count, orders)
 
 
 def routes(count):

time: 274 us -> 272 us (level)
  waiting for transfers between devices: 73.1 us -> 63.3 us
  starting transfers between devices: 79.4 us -> 88.7 us
    ppermute x24, waiting for transfers between devices: 44.1 us -> 33.6 us  [along_aux(): lax.ppermute(value, 'aux', [(z, (z + steps) % aux_count) for z in range(a...]
    ppermute x24, starting transfers between devices: 48.3 us -> 57.6 us  [along_aux(): lax.ppermute(value, 'aux', [(z, (z + steps) % aux_count) for z in range(a...]
  transfers between devices with their start and end apart: 38 -> 38, of which waited for: 14 -> 14; matrix products, arithmetic and copies ran while one was open for 0% -> 0% of each run, Pallas kernels for 26% -> 27%
where the time goes in v5:
time: 272 us; the launch traced here: 268 us
  Pallas kernels  91.9 us (34%)
  starting transfers between devices  88.7 us (33%)
  waiting for transfers between devices  63.3 us (23%)
  blocking collectives  20.8 us (8%)
    ppermute x24, starting transfers between devices, along_aux(): lax.ppermute(value, 'aux', [(z, (z + steps) % aux_count) for z in range(a...  57.6 us
    pallas_call x7, Pallas kernels, transformed(): pl.pallas_call(functools.partial(transform_kernel, count, orbitals, orbit...  36.8 us
    pallas_call x4, Pallas kernels, densities(): pl.pallas_call(functools.partial(pair_kernel, rank, count, occ_count), in...  35.1 us
    ppermute x24, waiting for transfers between devices, along_aux(): lax.ppermute(value, 'aux', [(z, (z + steps) % aux_count) for z in range(a...  33.6 us
    unnamed x1, blocking collectives  20.8 us
    ppermute x4, waiting for transfers between devices, body(): near = lax.ppermute(own, 'occ', direct)  13 us
    ppermute x4, starting transfers between devices, body(): swaps.append(lax.ppermute(both, 'occ', twin))  8.51 us
    ppermute x2, starting transfers between devices, body(): lax.ppermute(onward[0], 'occ', far + last)  8.37 us
  transfers between devices with their start and end apart: 38, of which 14 were waited for; matrix products, arithmetic and copies ran while one was open for 0% of the time, Pallas kernels for 27%

profile of v5, /device:TPU:0, one launch (start us, length us, event | category | flops | bytes accessed | tf_op | source)
XLA Modules:
  0.0 268.1 jit_solution(16277754138943908981)
XLA Ops:
  0.7 6.7 %sort_rows.1 = (bf16[16,256,1024]{2,1,0:T(8,128)(2,1)S(1)}, s32[2]{0:T(128)S(1)}) custom-call(s32[4,16]{1,0:T(4,128)S(1)} %copy-done.5, s32[1]{0:T(128)} %bitcast.aux_ref, s32[1]{0:T(128)} %bitcast.1.occ_ref, bf16[256,16,1024]{2,1,0:T(8,128)(2,1)} %x_ref.1), custom_call_target="tpu_custom_call" | custom-call | flops 2147483648 | bytes 16777216 | tf_op jit(solution)/shard_map/sort_rows/pallas_call | solution.py:44
  10.0 5.1 %collective-permute-start.2 = (bf16[256,512]{1,0:T(8,128)(2,1)S(1)}, bf16[256,512]{1,0:T(8,128)(2,1)S(1)}, u32[]{:S(2)}, u32[]{:S(2)}) collective-permute-start(bf16[256,512]{1,0:T(8,128)(2,1)S(1)} %transform.10), channel_id=1, source_target_pairs={{0,24},{8,0},{16,8},{24,16},{1,25},{9,1},{17,9},{25,17},{2,26},{10... | collective-permute-start | bytes 786440 | tf_op jit(solution)/shard_map/ppermute | solution.py:450
  23.9 8.9 %transform.11 = (bf16[256,512]{1,0:T(8,128)(2,1)S(1)}, bf16[256,512]{1,0:T(8,128)(2,1)S(1)}, bf16[256,512]{1,0:T(8,128)(2,1)S(1)}, bf16[256,512]{1,0:T(8,128)(2,1)S(1)}) custom-call(s32[2]{0:T(128)S(1)} %get-tuple-element.42.place_ref.pos_ref, bf16[16,256,1024]{2,1,0:T(8,128)(2,1)S(1)} %get-tuple-element.46.x_ref, s32[128,512]{1,0:T(8,128)S(1)} %copy-done.1, ...), custom_call_target="tpu_custom_call" | custom-call | flops 6442450944 | bytes 7340032 | tf_op jit(solution)/shard_map/transform/pallas_call | solution.py:101
  32.8 4.6 %collective-permute-done.1.refs_2_ = bf16[256,512]{1,0:T(8,128)(2,1)S(1)} collective-permute-done((bf16[256,512]{1,0:T(8,128)(2,1)S(1)}, bf16[256,512]{1,0:T(8,128)(2,1)S(1)}, u32[]{:S(2)}, u32[]{:S(2)}) %collective-permute-start.1) | collective-permute-done | bytes 262176 | tf_op jit(solution)/shard_map/ppermute | solution.py:450
  39.4 4.2 %collective-permute-start.7 = (bf16[1024,512]{1,0:T(8,128)(2,1)S(1)}, bf16[1024,512]{1,0:T(8,128)(2,1)S(1)}, u32[]{:S(2)}, u32[]{:S(2)}) collective-permute-start(bf16[1024,512]{1,0:T(8,128)(2,1)S(1)} %join.4.refs_0_.own_ref), channel_id=1, source_target_pairs={{4,1},{6,3},{0,5},{2,7},{12,9},{14,11},{8,13},{10,15},{20,17},{22,... | collective-permute-start | bytes 3145736 | tf_op jit(solution)/shard_map/ppermute | solution.py:481
  47.9 2.8 %collective-permute-start.6 = (bf16[256,512]{1,0:T(8,128)(2,1)S(1)}, bf16[256,512]{1,0:T(8,128)(2,1)S(1)}, u32[]{:S(2)}, u32[]{:S(2)}) collective-permute-start(bf16[256,512]{1,0:T(8,128)(2,1)S(1)} %get-tuple-element.50), channel_id=1, source_target_pairs={{0,24},{8,0},{16,8},{24,16},{1,25},{9,1},{17,9},{25,17},{2,26},{10... | collective-permute-start | bytes 786440 | tf_op jit(solution)/shard_map/ppermute | solution.py:450
  53.3 8.9 %transform.12 = (bf16[256,512]{1,0:T(8,128)(2,1)S(1)}, bf16[256,512]{1,0:T(8,128)(2,1)S(1)}, bf16[256,512]{1,0:T(8,128)(2,1)S(1)}, bf16[256,512]{1,0:T(8,128)(2,1)S(1)}) custom-call(s32[2]{0:T(128)S(1)} %get-tuple-element.42.place_ref.pos_ref, bf16[16,256,1024]{2,1,0:T(8,128)(2,1)S(1)} %get-tuple-element.46.x_ref, s32[128,512]{1,0:T(8,128)S(1)} %copy-done.1, ...), custom_call_target="tpu_custom_call" | custom-call | flops 6442450944 | bytes 7340032 | tf_op jit(solution)/shard_map/transform/pallas_call | solution.py:101
  66.4 5.6 %collective-permute-start.8 = (bf16[1280,512]{1,0:T(8,128)(2,1)S(1)}, bf16[1280,512]{1,0:T(8,128)(2,1)S(1)}, u32[]{:S(2)}, u32[]{:S(2)}) collective-permute-start(bf16[1280,512]{1,0:T(8,128)(2,1)S(1)} %get-tuple-element.52), channel_id=1, source_target_pairs={{4,1},{6,3},{0,5},{2,7},{5,6},{1,2},{12,9},{14,11},{8,13},{10,15},... | collective-permute-start | bytes 3932168 | tf_op jit(solution)/shard_map/ppermute | solution.py:481
  72.0 4.2 %collective-permute-start.10 = (bf16[256,512]{1,0:T(8,128)(2,1)S(1)}, bf16[256,512]{1,0:T(8,128)(2,1)S(1)}, u32[]{:S(2)}, u32[]{:S(2)}) collective-permute-start(bf16[256,512]{1,0:T(8,128)(2,1)S(1)} %get-tuple-element.54), channel_id=1, source_target_pairs={{0,16},{8,24},{16,0},{24,8},{1,17},{9,25},{17,1},{25,9},{2,18},{10... | collective-permute-start | bytes 786440 | tf_op jit(solution)/shard_map/ppermute | solution.py:450
  78.2 8.8 %transform.13 = (bf16[256,512]{1,0:T(8,128)(2,1)S(1)}, bf16[256,512]{1,0:T(8,128)(2,1)S(1)}, bf16[256,512]{1,0:T(8,128)(2,1)S(1)}, bf16[256,512]{1,0:T(8,128)(2,1)S(1)}) custom-call(s32[2]{0:T(128)S(1)} %get-tuple-element.42.place_ref.pos_ref, bf16[16,256,1024]{2,1,0:T(8,128)(2,1)S(1)} %get-tuple-element.46.x_ref, s32[128,512]{1,0:T(8,128)S(1)} %copy-done.1, ...), custom_call_target="tpu_custom_call" | custom-call | flops 6442450944 | bytes 7340032 | tf_op jit(solution)/shard_map/transform/pallas_call | solution.py:101
  89.0 5.8 %collective-permute-done.9.refs_0_ = bf16[256,512]{1,0:T(8,128)(2,1)S(1)} collective-permute-done((bf16[256,512]{1,0:T(8,128)(2,1)S(1)}, bf16[256,512]{1,0:T(8,128)(2,1)S(1)}, u32[]{:S(2)}, u32[]{:S(2)}) %collective-permute-start.9) | collective-permute-done | bytes 262176 | tf_op jit(solution)/shard_map/ppermute | solution.py:450
  94.8 3.3 %collective-permute-done.12.refs_3_.refs_5_.near_ref = bf16[1280,512]{1,0:T(8,128)(2,1)S(1)} collective-permute-done((bf16[1280,512]{1,0:T(8,128)(2,1)S(1)}, bf16[1280,512]{1,0:T(8,128)(2,1)S(1)}, u32[]{:S(2)}, u32[]{:S(2)}) %collective-permute-start.12) | collective-permute-done | bytes 1310752 | tf_op jit(solution)/shard_map/ppermute | solution.py:480
  102.9 4.1 %collective-permute-start.14 = (bf16[256,512]{1,0:T(8,128)(2,1)S(1)}, bf16[256,512]{1,0:T(8,128)(2,1)S(1)}, u32[]{:S(2)}, u32[]{:S(2)}) collective-permute-start(bf16[256,512]{1,0:T(8,128)(2,1)S(1)} %get-tuple-element.59), channel_id=1, source_target_pairs={{0,8},{8,16},{16,24},{24,0},{1,9},{9,17},{17,25},{25,1},{2,10},{10... | collective-permute-start | bytes 786440 | tf_op jit(solution)/shard_map/ppermute | solution.py:450
  110.1 6.6 %collective-permute-done.13.late_ref.refs_4_.refs_10_ = bf16[1280,512]{1,0:T(8,128)(2,1)S(1)} collective-permute-done((bf16[1280,512]{1,0:T(8,128)(2,1)S(1)}, bf16[1280,512]{1,0:T(8,128)(2,1)S(1)}, u32[]{:S(2)}, u32[]{:S(2)}) %collective-permute-start.13) | collective-permute-done | bytes 1310752 | tf_op jit(solution)/shard_map/ppermute | solution.py:481
  117.4 9.0 %collective-permute-done.15.refs_1_ = bf16[256,512]{1,0:T(8,128)(2,1)S(1)} collective-permute-done((bf16[256,512]{1,0:T(8,128)(2,1)S(1)}, bf16[256,512]{1,0:T(8,128)(2,1)S(1)}, u32[]{:S(2)}, u32[]{:S(2)}) %collective-permute-start.15) | collective-permute-done | bytes 262176 | tf_op jit(solution)/shard_map/ppermute | solution.py:450
  129.3 3.5 %collective-permute-start.20 = (bf16[768,512]{1,0:T(8,128)(2,1)S(1)}, bf16[768,512]{1,0:T(8,128)(2,1)S(1)}, u32[]{:S(2)}, u32[]{:S(2)}) collective-permute-start(bf16[768,512]{1,0:T(8,128)(2,1)S(1)} %join.7.own_ref), channel_id=1, source_target_pairs={{4,1},{6,3},{0,5},{2,7},{12,9},{14,11},{8,13},{10,15},{20,17},{22,... | collective-permute-start | bytes 2359304 | tf_op jit(solution)/shard_map/ppermute | solution.py:481
  135.1 7.1 %collective-permute-done.20.refs_11_ = bf16[768,512]{1,0:T(8,128)(2,1)S(1)} collective-permute-done((bf16[768,512]{1,0:T(8,128)(2,1)S(1)}, bf16[768,512]{1,0:T(8,128)(2,1)S(1)}, u32[]{:S(2)}, u32[]{:S(2)}) %collective-permute-start.20) | collective-permute-done | bytes 786464 | tf_op jit(solution)/shard_map/ppermute | solution.py:481
  143.8 3.9 %collective-permute-start.22 = (bf16[2,1024,512]{2,1,0:T(8,128)(2,1)S(1)}, bf16[2,1024,512]{2,1,0:T(8,128)(2,1)S(1)}, u32[]{:S(2)}, u32[]{:S(2)}) collective-permute-start(bf16[2,1024,512]{2,1,0:T(8,128)(2,1)S(1)} %pick.4.refs_0_), channel_id=1, source_target_pairs={{0,1},{1,0},{2,3},{3,2},{4,5},{5,4},{6,7},{7,6},{8,9},{9,8},{10,11... | collective-permute-start | bytes 6291464 | tf_op jit(solution)/shard_map/ppermute | solution.py:495
  148.6 7.2 %collective-permute-done.19.near_ref = bf16[768,512]{1,0:T(8,128)(2,1)S(1)} collective-permute-done((bf16[768,512]{1,0:T(8,128)(2,1)S(1)}, bf16[768,512]{1,0:T(8,128)(2,1)S(1)}, u32[]{:S(2)}, u32[]{:S(2)}) %collective-permute-start.19) | collective-permute-done | bytes 786464 | tf_op jit(solution)/shard_map/ppermute | solution.py:480
  156.7 4.5 %collective-permute-start.25 = (bf16[2,768,512]{2,1,0:T(8,128)(2,1)S(1)}, bf16[2,768,512]{2,1,0:T(8,128)(2,1)S(1)}, u32[]{:S(2)}, u32[]{:S(2)}) collective-permute-start(bf16[2,768,512]{2,1,0:T(8,128)(2,1)S(1)} %pick.7.refs_3_), channel_id=1, source_target_pairs={{0,1},{1,0},{2,3},{3,2},{4,5},{5,4},{6,7},{7,6},{8,9},{9,8},{10,11... | collective-permute-start | bytes 4718600 | tf_op jit(solution)/shard_map/ppermute | solution.py:495
  161.1 3.0 %collective-permute-done.25.refs_7_ = bf16[2,768,512]{2,1,0:T(8,128)(2,1)S(1)} collective-permute-done((bf16[2,768,512]{2,1,0:T(8,128)(2,1)S(1)}, bf16[2,768,512]{2,1,0:T(8,128)(2,1)S(1)}, u32[]{:S(2)}, u32[]{:S(2)}) %collective-permute-start.25) | collective-permute-done | bytes 1572896 | tf_op jit(solution)/shard_map/ppermute | solution.py:495
  164.2 3.6 %pairs.7 = (bf16[256,512]{1,0:T(8,128)(2,1)S(1)}, bf16[256,512]{1,0:T(8,128)(2,1)S(1)}, bf16[256,512]{1,0:T(8,128)(2,1)S(1)}, bf16[256,512]{1,0:T(8,128)(2,1)S(1)}) custom-call(s32[1,1]{1,0:T(1,128)S(6)} %copy.10.live_ref, s32[16]{0:T(128)S(1)} %bitcast.6, s32[2]{0:T(128)S(1)} %get-tuple-element.42.place_ref.pos_ref, f32[128]{0:T(128)S(1)} %copy-done.3, ...), custom_call_target="tpu_custom_call" | custom-call | flops 4294967296 | bytes 3145728 | tf_op jit(solution)/shard_map/pairs/pallas_call | solution.py:378
  167.8 8.8 %collective-permute-start.35 = (bf16[256,512]{1,0:T(8,128)(2,1)S(1)}, bf16[256,512]{1,0:T(8,128)(2,1)S(1)}, u32[]{:S(2)}, u32[]{:S(2)}) collective-permute-start(bf16[256,512]{1,0:T(8,128)(2,1)S(1)} %get-tuple-element.76), channel_id=1, source_target_pairs={{0,24},{8,0},{16,8},{24,16},{1,25},{9,1},{17,9},{25,17},{2,26},{10... | collective-permute-start | bytes 786440 | tf_op jit(solution)/shard_map/ppermute | solution.py:450
  177.3 8.6 %pairs.6 = (bf16[256,512]{1,0:T(8,128)(2,1)S(1)}, bf16[256,512]{1,0:T(8,128)(2,1)S(1)}, bf16[256,512]{1,0:T(8,128)(2,1)S(1)}, bf16[256,512]{1,0:T(8,128)(2,1)S(1)}) custom-call(s32[1,1]{1,0:T(1,128)S(6)} %copy.10.live_ref, s32[16]{0:T(128)S(1)} %bitcast.7, s32[2]{0:T(128)S(1)} %get-tuple-element.42.place_ref.pos_ref, f32[128]{0:T(128)S(1)} %copy-done.3, ...), custom_call_target="tpu_custom_call" | custom-call | flops 4294967296 | bytes 3145728 | tf_op jit(solution)/shard_map/pairs/pallas_call | solution.py:378
  186.0 10.7 %pairs.5 = (bf16[256,512]{1,0:T(8,128)(2,1)S(1)}, bf16[256,512]{1,0:T(8,128)(2,1)S(1)}, bf16[256,512]{1,0:T(8,128)(2,1)}, bf16[256,512]{1,0:T(8,128)(2,1)}) custom-call(s32[1,1]{1,0:T(1,128)S(6)} %copy.10.live_ref, s32[16]{0:T(128)S(1)} %bitcast.8, s32[2]{0:T(128)S(1)} %get-tuple-element.42.place_ref.pos_ref, f32[128]{0:T(128)S(1)} %copy-done.3, ...), custom_call_target="tpu_custom_call" | custom-call | flops 4294967296 | bytes 3145728 | tf_op jit(solution)/shard_map/pairs/pallas_call | solution.py:378
  198.1 6.9 %collective-permute-start.29 = (bf16[256,512]{1,0:T(8,128)(2,1)S(1)}, bf16[256,512]{1,0:T(8,128)(2,1)S(1)}, u32[]{:S(2)}, u32[]{:S(2)}) collective-permute-start(bf16[256,512]{1,0:T(8,128)(2,1)S(1)} %get-tuple-element.68), channel_id=1, source_target_pairs={{0,24},{8,0},{16,8},{24,16},{1,25},{9,1},{17,9},{25,17},{2,26},{10... | collective-permute-start | bytes 786440 | tf_op jit(solution)/shard_map/ppermute | solution.py:450
  205.0 12.3 %pairs.4 = (bf16[256,512]{1,0:T(8,128)(2,1)S(1)}, bf16[256,512]{1,0:T(8,128)(2,1)}, bf16[256,512]{1,0:T(8,128)(2,1)}, bf16[256,512]{1,0:T(8,128)(2,1)}) custom-call(s32[1,1]{1,0:T(1,128)S(6)} %copy.10.live_ref, s32[16]{0:T(128)S(1)} %bitcast.9, s32[2]{0:T(128)S(1)} %get-tuple-element.42.place_ref.pos_ref, f32[128]{0:T(128)S(1)} %copy-done.3, ...), custom_call_target="tpu_custom_call" | custom-call | flops 4294967296 | bytes 3145728 | tf_op jit(solution)/shard_map/pairs/pallas_call | solution.py:378
  217.3 3.4 %collective-permute-start.30 = (bf16[256,512]{1,0:T(8,128)(2,1)}, bf16[256,512]{1,0:T(8,128)(2,1)S(1)}, u32[]{:S(2)}, u32[]{:S(2)}) collective-permute-start(bf16[256,512]{1,0:T(8,128)(2,1)} %get-tuple-element.69), channel_id=1, source_target_pairs={{0,16},{8,24},{16,0},{24,8},{1,17},{9,25},{17,1},{25,9},{2,18},{10... | collective-permute-start | bytes 786440 | tf_op jit(solution)/shard_map/ppermute | solution.py:450
  220.8 8.8 %collective-permute-done.33.refs_10_ = bf16[256,512]{1,0:T(8,128)(2,1)S(1)} collective-permute-done((bf16[256,512]{1,0:T(8,128)(2,1)S(1)}, bf16[256,512]{1,0:T(8,128)(2,1)S(1)}, u32[]{:S(2)}, u32[]{:S(2)}) %collective-permute-start.33) | collective-permute-done | bytes 262176 | tf_op jit(solution)/shard_map/ppermute | solution.py:450
  230.1 10.3 %collective-permute-start.27 = (bf16[256,512]{1,0:T(8,128)(2,1)}, bf16[256,512]{1,0:T(8,128)(2,1)}, u32[]{:S(2)}, u32[]{:S(2)}) collective-permute-start(bf16[256,512]{1,0:T(8,128)(2,1)} %get-tuple-element.65), channel_id=1, source_target_pairs={{0,16},{8,24},{16,0},{24,8},{1,17},{9,25},{17,1},{25,9},{2,18},{10... | collective-permute-start | bytes 786440 | tf_op jit(solution)/shard_map/ppermute | solution.py:450
  242.0 20.8 %all-reduce = s32[16]{0:T(128)S(1)} all-reduce(s32[16]{0:T(128)S(1)} %dynamic-update-slice), channel_id=2, replica_groups=mesh['aux'=4,'occ'=8] {'aux'}, use_global_device_ids=true, to_apply=%add | all-reduce | flops 16 | bytes 128
  262.9 5.2 %assemble.1 = bf16[256,16,512]{2,1,0:T(8,128)(2,1)} custom-call(s32[2]{0:T(128)S(1)} %get-tuple-element.42.place_ref.pos_ref, s32[4,4]{1,0:T(4,128)S(1)} %reshape.12.order_ref, bf16[256,512]{1,0:T(8,128)(2,1)S(1)} %get-tuple-element.63.refs_0_, bf16[256,512]{1,0:T(8,128)(2,1)} %collective-permute-done.26.refs_1_, ...), custom_call_target="tpu_custom_call" | custom-call | flops 1073741824 | bytes 8388608 | tf_op jit(solution)/shard_map/assemble/pallas_call | solution.py:424
  (85 shorter events, 49.2 us)
Async XLA Ops:
  10.0 22.9 %collective-permute-start.2 = (bf16[256,512]{1,0:T(8,128)(2,1)S(1)}, bf16[256,512]{1,0:T(8,128)(2,1)S(1)}, u32[]{:S(2)}, u32[]{:S(2)}) collective-permute-start(bf16[256,512]{1,0:T(8,128)(2,1)S(1)} %transform.10), channel_id=1, source_target_pairs={{0,24},{8,0},{16,8},{24,16},{1,25},{9,1},{17,9},{25,17},{2,26},{10... | collective-permute-start | bytes 786440 | tf_op jit(solution)/shard_map/ppermute | solution.py:450
  17.6 19.8 %collective-permute-start.1 = (bf16[256,512]{1,0:T(8,128)(2,1)S(1)}, bf16[256,512]{1,0:T(8,128)(2,1)S(1)}, u32[]{:S(2)}, u32[]{:S(2)}) collective-permute-start(bf16[256,512]{1,0:T(8,128)(2,1)S(1)} %transform.9), channel_id=1, source_target_pairs={{0,16},{8,24},{16,0},{24,8},{1,17},{9,25},{17,1},{25,9},{2,18},{10... | collective-permute-start | bytes 786440 | tf_op jit(solution)/shard_map/ppermute | solution.py:450
  20.3 17.1 %collective-permute-start = (bf16[256,512]{1,0:T(8,128)(2,1)S(1)}, bf16[256,512]{1,0:T(8,128)(2,1)S(1)}, u32[]{:S(2)}, u32[]{:S(2)}) collective-permute-start(bf16[256,512]{1,0:T(8,128)(2,1)S(1)} %transform.8), channel_id=1, source_target_pairs={{0,8},{8,16},{16,24},{24,0},{1,9},{9,17},{17,25},{25,1},{2,10},{10... | collective-permute-start | bytes 786440 | tf_op jit(solution)/shard_map/ppermute | solution.py:450
  38.1 26.3 %collective-permute-start.3 = (bf16[1024,512]{1,0:T(8,128)(2,1)S(1)}, bf16[1024,512]{1,0:T(8,128)(2,1)S(1)}, u32[]{:S(2)}, u32[]{:S(2)}) collective-permute-start(bf16[1024,512]{1,0:T(8,128)(2,1)S(1)} %join.4.refs_0_.own_ref), channel_id=1, source_target_pairs={{1,7},{2,0},{3,1},{5,3},{6,4},{7,5},{9,15},{10,8},{11,9},{13,11},{... | collective-permute-start | bytes 3145736 | tf_op jit(solution)/shard_map/ppermute | solution.py:480
  39.4 25.0 %collective-permute-start.7 = (bf16[1024,512]{1,0:T(8,128)(2,1)S(1)}, bf16[1024,512]{1,0:T(8,128)(2,1)S(1)}, u32[]{:S(2)}, u32[]{:S(2)}) collective-permute-start(bf16[1024,512]{1,0:T(8,128)(2,1)S(1)} %join.4.refs_0_.own_ref), channel_id=1, source_target_pairs={{4,1},{6,3},{0,5},{2,7},{12,9},{14,11},{8,13},{10,15},{20,17},{22,... | collective-permute-start | bytes 3145736 | tf_op jit(solution)/shard_map/ppermute | solution.py:481
  43.6 18.6 %collective-permute-start.4 = (bf16[256,512]{1,0:T(8,128)(2,1)S(1)}, bf16[256,512]{1,0:T(8,128)(2,1)S(1)}, u32[]{:S(2)}, u32[]{:S(2)}) collective-permute-start(bf16[256,512]{1,0:T(8,128)(2,1)S(1)} %get-tuple-element.48), channel_id=1, source_target_pairs={{0,8},{8,16},{16,24},{24,0},{1,9},{9,17},{17,25},{25,1},{2,10},{10... | collective-permute-start | bytes 786440 | tf_op jit(solution)/shard_map/ppermute | solution.py:450
  45.9 18.3 %collective-permute-start.5 = (bf16[256,512]{1,0:T(8,128)(2,1)S(1)}, bf16[256,512]{1,0:T(8,128)(2,1)S(1)}, u32[]{:S(2)}, u32[]{:S(2)}) collective-permute-start(bf16[256,512]{1,0:T(8,128)(2,1)S(1)} %get-tuple-element.49), channel_id=1, source_target_pairs={{0,16},{8,24},{16,0},{24,8},{1,17},{9,25},{17,1},{25,9},{2,18},{10... | collective-permute-start | bytes 786440 | tf_op jit(solution)/shard_map/ppermute | solution.py:450
  47.9 16.3 %collective-permute-start.6 = (bf16[256,512]{1,0:T(8,128)(2,1)S(1)}, bf16[256,512]{1,0:T(8,128)(2,1)S(1)}, u32[]{:S(2)}, u32[]{:S(2)}) collective-permute-start(bf16[256,512]{1,0:T(8,128)(2,1)S(1)} %get-tuple-element.50), channel_id=1, source_target_pairs={{0,24},{8,0},{16,8},{24,16},{1,25},{9,1},{17,9},{25,17},{2,26},{10... | collective-permute-start | bytes 786440 | tf_op jit(solution)/shard_map/ppermute | solution.py:450
  65.1 33.0 %collective-permute-start.12 = (bf16[1280,512]{1,0:T(8,128)(2,1)S(1)}, bf16[1280,512]{1,0:T(8,128)(2,1)S(1)}, u32[]{:S(2)}, u32[]{:S(2)}) collective-permute-start(bf16[1280,512]{1,0:T(8,128)(2,1)S(1)} %get-tuple-element.56.refs_0_.own_ref), channel_id=1, source_target_pairs={{1,7},{2,0},{3,1},{5,3},{6,4},{7,5},{9,15},{10,8},{11,9},{13,11},{... | collective-permute-start | bytes 3932168 | tf_op jit(solution)/shard_map/ppermute | solution.py:480
  66.4 31.7 %collective-permute-start.8 = (bf16[1280,512]{1,0:T(8,128)(2,1)S(1)}, bf16[1280,512]{1,0:T(8,128)(2,1)S(1)}, u32[]{:S(2)}, u32[]{:S(2)}) collective-permute-start(bf16[1280,512]{1,0:T(8,128)(2,1)S(1)} %get-tuple-element.52), channel_id=1, source_target_pairs={{4,1},{6,3},{0,5},{2,7},{5,6},{1,2},{12,9},{14,11},{8,13},{10,15},... | collective-permute-start | bytes 3932168 | tf_op jit(solution)/shard_map/ppermute | solution.py:481
  72.0 17.0 %collective-permute-start.10 = (bf16[256,512]{1,0:T(8,128)(2,1)S(1)}, bf16[256,512]{1,0:T(8,128)(2,1)S(1)}, u32[]{:S(2)}, u32[]{:S(2)}) collective-permute-start(bf16[256,512]{1,0:T(8,128)(2,1)S(1)} %get-tuple-element.54), channel_id=1, source_target_pairs={{0,16},{8,24},{16,0},{24,8},{1,17},{9,25},{17,1},{25,9},{2,18},{10... | collective-permute-start | bytes 786440 | tf_op jit(solution)/shard_map/ppermute | solution.py:450
  77.7 17.1 %collective-permute-start.9 = (bf16[256,512]{1,0:T(8,128)(2,1)S(1)}, bf16[256,512]{1,0:T(8,128)(2,1)S(1)}, u32[]{:S(2)}, u32[]{:S(2)}) collective-permute-start(bf16[256,512]{1,0:T(8,128)(2,1)S(1)} %get-tuple-element.53), channel_id=1, source_target_pairs={{0,8},{8,16},{16,24},{24,0},{1,9},{9,17},{17,25},{25,1},{2,10},{10... | collective-permute-start | bytes 786440 | tf_op jit(solution)/shard_map/ppermute | solution.py:450
  98.8 17.8 %collective-permute-start.13 = (bf16[1280,512]{1,0:T(8,128)(2,1)S(1)}, bf16[1280,512]{1,0:T(8,128)(2,1)S(1)}, u32[]{:S(2)}, u32[]{:S(2)}) collective-permute-start(bf16[1280,512]{1,0:T(8,128)(2,1)S(1)} %get-tuple-element.58), channel_id=1, source_target_pairs={{4,1},{6,3},{0,5},{2,7},{5,6},{1,2},{12,9},{14,11},{8,13},{10,15},... | collective-permute-start | bytes 3932168 | tf_op jit(solution)/shard_map/ppermute | solution.py:481
  101.6 27.0 %collective-permute-start.17 = (bf16[1024,512]{1,0:T(8,128)(2,1)S(1)}, bf16[1024,512]{1,0:T(8,128)(2,1)S(1)}, u32[]{:S(2)}, u32[]{:S(2)}) collective-permute-start(bf16[1024,512]{1,0:T(8,128)(2,1)S(1)} %get-tuple-element.62.own_ref), channel_id=1, source_target_pairs={{1,7},{2,0},{3,1},{5,3},{6,4},{7,5},{9,15},{10,8},{11,9},{13,11},{... | collective-permute-start | bytes 3145736 | tf_op jit(solution)/shard_map/ppermute | solution.py:480
  107.1 19.3 %collective-permute-start.15 = (bf16[256,512]{1,0:T(8,128)(2,1)S(1)}, bf16[256,512]{1,0:T(8,128)(2,1)S(1)}, u32[]{:S(2)}, u32[]{:S(2)}) collective-permute-start(bf16[256,512]{1,0:T(8,128)(2,1)S(1)} %get-tuple-element.60), channel_id=1, source_target_pairs={{0,16},{8,24},{16,0},{24,8},{1,17},{9,25},{17,1},{25,9},{2,18},{10... | collective-permute-start | bytes 786440 | tf_op jit(solution)/shard_map/ppermute | solution.py:450
  108.6 17.8 %collective-permute-start.16 = (bf16[256,512]{1,0:T(8,128)(2,1)S(1)}, bf16[256,512]{1,0:T(8,128)(2,1)S(1)}, u32[]{:S(2)}, u32[]{:S(2)}) collective-permute-start(bf16[256,512]{1,0:T(8,128)(2,1)S(1)} %get-tuple-element.61), channel_id=1, source_target_pairs={{0,24},{8,0},{16,8},{24,16},{1,25},{9,1},{17,9},{25,17},{2,26},{10... | collective-permute-start | bytes 786440 | tf_op jit(solution)/shard_map/ppermute | solution.py:450
  116.7 31.0 %collective-permute-start.18 = (bf16[1280,512]{1,0:T(8,128)(2,1)S(1)}, bf16[1280,512]{1,0:T(8,128)(2,1)S(1)}, u32[]{:S(2)}, u32[]{:S(2)}) collective-permute-start(bf16[1280,512]{1,0:T(8,128)(2,1)S(1)} %collective-permute-done.13.late_ref.refs_4_.refs_10_), channel_id=1, source_target_pairs={{5,6},{1,2},{13,14},{9,10},{21,22},{17,18},{29,30},{25,26}} | collective-permute-start | bytes 3932168 | tf_op jit(solution)/shard_map/ppermute | solution.py:488
  133.7 27.4 %collective-permute-start.23 = (bf16[2,1280,512]{2,1,0:T(8,128)(2,1)S(1)}, bf16[2,1280,512]{2,1,0:T(8,128)(2,1)S(1)}, u32[]{:S(2)}, u32[]{:S(2)}) collective-permute-start(bf16[2,1280,512]{2,1,0:T(8,128)(2,1)S(1)} %pick.5.refs_1_), channel_id=1, source_target_pairs={{0,1},{1,0},{2,3},{3,2},{4,5},{5,4},{6,7},{7,6},{8,9},{9,8},{10,11... | collective-permute-start | bytes 7864328 | tf_op jit(solution)/shard_map/ppermute | solution.py:495
  133.8 22.1 %collective-permute-start.19 = (bf16[768,512]{1,0:T(8,128)(2,1)S(1)}, bf16[768,512]{1,0:T(8,128)(2,1)S(1)}, u32[]{:S(2)}, u32[]{:S(2)}) collective-permute-start(bf16[768,512]{1,0:T(8,128)(2,1)S(1)} %join.7.own_ref), channel_id=1, source_target_pairs={{1,7},{2,0},{3,1},{5,3},{6,4},{7,5},{9,15},{10,8},{11,9},{13,11},{... | collective-permute-start | bytes 2359304 | tf_op jit(solution)/shard_map/ppermute | solution.py:480
  143.8 17.4 %collective-permute-start.22 = (bf16[2,1024,512]{2,1,0:T(8,128)(2,1)S(1)}, bf16[2,1024,512]{2,1,0:T(8,128)(2,1)S(1)}, u32[]{:S(2)}, u32[]{:S(2)}) collective-permute-start(bf16[2,1024,512]{2,1,0:T(8,128)(2,1)S(1)} %pick.4.refs_0_), channel_id=1, source_target_pairs={{0,1},{1,0},{2,3},{3,2},{4,5},{5,4},{6,7},{7,6},{8,9},{9,8},{10,11... | collective-permute-start | bytes 6291464 | tf_op jit(solution)/shard_map/ppermute | solution.py:495
  167.8 28.8 %collective-permute-start.35 = (bf16[256,512]{1,0:T(8,128)(2,1)S(1)}, bf16[256,512]{1,0:T(8,128)(2,1)S(1)}, u32[]{:S(2)}, u32[]{:S(2)}) collective-permute-start(bf16[256,512]{1,0:T(8,128)(2,1)S(1)} %get-tuple-element.76), channel_id=1, source_target_pairs={{0,24},{8,0},{16,8},{24,16},{1,25},{9,1},{17,9},{25,17},{2,26},{10... | collective-permute-start | bytes 786440 | tf_op jit(solution)/shard_map/ppermute | solution.py:450
  176.6 21.5 %collective-permute-start.36 = (bf16[256,512]{1,0:T(8,128)(2,1)S(1)}, bf16[256,512]{1,0:T(8,128)(2,1)S(1)}, u32[]{:S(2)}, u32[]{:S(2)}) collective-permute-start(bf16[256,512]{1,0:T(8,128)(2,1)S(1)} %get-tuple-element.77), channel_id=1, source_target_pairs={{0,16},{8,24},{16,0},{24,8},{1,17},{9,25},{17,1},{25,9},{2,18},{10... | collective-permute-start | bytes 786440 | tf_op jit(solution)/shard_map/ppermute | solution.py:450
  176.7 40.6 %collective-permute-start.37 = (bf16[256,512]{1,0:T(8,128)(2,1)S(1)}, bf16[256,512]{1,0:T(8,128)(2,1)S(1)}, u32[]{:S(2)}, u32[]{:S(2)}) collective-permute-start(bf16[256,512]{1,0:T(8,128)(2,1)S(1)} %get-tuple-element.78), channel_id=1, source_target_pairs={{0,8},{8,16},{16,24},{24,0},{1,9},{9,17},{17,25},{25,1},{2,10},{10... | collective-permute-start | bytes 786440 | tf_op jit(solution)/shard_map/ppermute | solution.py:450
  185.9 34.9 %collective-permute-start.32 = (bf16[256,512]{1,0:T(8,128)(2,1)S(1)}, bf16[256,512]{1,0:T(8,128)(2,1)S(1)}, u32[]{:S(2)}, u32[]{:S(2)}) collective-permute-start(bf16[256,512]{1,0:T(8,128)(2,1)S(1)} %get-tuple-element.72), channel_id=1, source_target_pairs={{0,24},{8,0},{16,8},{24,16},{1,25},{9,1},{17,9},{25,17},{2,26},{10... | collective-permute-start | bytes 786440 | tf_op jit(solution)/shard_map/ppermute | solution.py:450
  185.9 43.6 %collective-permute-start.33 = (bf16[256,512]{1,0:T(8,128)(2,1)S(1)}, bf16[256,512]{1,0:T(8,128)(2,1)S(1)}, u32[]{:S(2)}, u32[]{:S(2)}) collective-permute-start(bf16[256,512]{1,0:T(8,128)(2,1)S(1)} %get-tuple-element.73), channel_id=1, source_target_pairs={{0,16},{8,24},{16,0},{24,8},{1,17},{9,25},{17,1},{25,9},{2,18},{10... | collective-permute-start | bytes 786440 | tf_op jit(solution)/shard_map/ppermute | solution.py:450
  196.7 33.4 %collective-permute-start.34 = (bf16[256,512]{1,0:T(8,128)(2,1)S(1)}, bf16[256,512]{1,0:T(8,128)(2,1)S(1)}, u32[]{:S(2)}, u32[]{:S(2)}) collective-permute-start(bf16[256,512]{1,0:T(8,128)(2,1)S(1)} %get-tuple-element.74), channel_id=1, source_target_pairs={{0,8},{8,16},{16,24},{24,0},{1,9},{9,17},{17,25},{25,1},{2,10},{10... | collective-permute-start | bytes 786440 | tf_op jit(solution)/shard_map/ppermute | solution.py:450
  198.1 42.3 %collective-permute-start.29 = (bf16[256,512]{1,0:T(8,128)(2,1)S(1)}, bf16[256,512]{1,0:T(8,128)(2,1)S(1)}, u32[]{:S(2)}, u32[]{:S(2)}) collective-permute-start(bf16[256,512]{1,0:T(8,128)(2,1)S(1)} %get-tuple-element.68), channel_id=1, source_target_pairs={{0,24},{8,0},{16,8},{24,16},{1,25},{9,1},{17,9},{25,17},{2,26},{10... | collective-permute-start | bytes 786440 | tf_op jit(solution)/shard_map/ppermute | solution.py:450
  217.3 45.5 %collective-permute-start.30 = (bf16[256,512]{1,0:T(8,128)(2,1)}, bf16[256,512]{1,0:T(8,128)(2,1)S(1)}, u32[]{:S(2)}, u32[]{:S(2)}) collective-permute-start(bf16[256,512]{1,0:T(8,128)(2,1)} %get-tuple-element.69), channel_id=1, source_target_pairs={{0,16},{8,24},{16,0},{24,8},{1,17},{9,25},{17,1},{25,9},{2,18},{10... | collective-permute-start | bytes 786440 | tf_op jit(solution)/shard_map/ppermute | solution.py:450
  220.8 42.1 %collective-permute-start.31 = (bf16[256,512]{1,0:T(8,128)(2,1)}, bf16[256,512]{1,0:T(8,128)(2,1)S(1)}, u32[]{:S(2)}, u32[]{:S(2)}) collective-permute-start(bf16[256,512]{1,0:T(8,128)(2,1)} %get-tuple-element.70), channel_id=1, source_target_pairs={{0,8},{8,16},{16,24},{24,0},{1,9},{9,17},{17,25},{25,1},{2,10},{10... | collective-permute-start | bytes 786440 | tf_op jit(solution)/shard_map/ppermute | solution.py:450
  229.6 33.3 %collective-permute-start.26 = (bf16[256,512]{1,0:T(8,128)(2,1)}, bf16[256,512]{1,0:T(8,128)(2,1)}, u32[]{:S(2)}, u32[]{:S(2)}) collective-permute-start(bf16[256,512]{1,0:T(8,128)(2,1)} %get-tuple-element.64), channel_id=1, source_target_pairs={{0,24},{8,0},{16,8},{24,16},{1,25},{9,1},{17,9},{25,17},{2,26},{10... | collective-permute-start | bytes 786440 | tf_op jit(solution)/shard_map/ppermute | solution.py:450
  230.1 32.8 %collective-permute-start.27 = (bf16[256,512]{1,0:T(8,128)(2,1)}, bf16[256,512]{1,0:T(8,128)(2,1)}, u32[]{:S(2)}, u32[]{:S(2)}) collective-permute-start(bf16[256,512]{1,0:T(8,128)(2,1)} %get-tuple-element.65), channel_id=1, source_target_pairs={{0,16},{8,24},{16,0},{24,8},{1,17},{9,25},{17,1},{25,9},{2,18},{10... | collective-permute-start | bytes 786440 | tf_op jit(solution)/shard_map/ppermute | solution.py:450
  240.4 22.4 %collective-permute-start.28 = (bf16[256,512]{1,0:T(8,128)(2,1)}, bf16[256,512]{1,0:T(8,128)(2,1)}, u32[]{:S(2)}, u32[]{:S(2)}) collective-permute-start(bf16[256,512]{1,0:T(8,128)(2,1)} %get-tuple-element.66), channel_id=1, source_target_pairs={{0,8},{8,16},{16,24},{24,0},{1,9},{9,17},{17,25},{25,1},{2,10},{10... | collective-permute-start | bytes 786440 | tf_op jit(solution)/shard_map/ppermute | solution.py:450
  (13 other events, 186.1 us)
